TPU v7x, 256 devices: a whole 4x4x8 slice. The times are simulated.
256 devices in a mesh: frame: 16 (over x, z_hi), row: 8 (over y, core), head: 2 (over z_lo).
Axes of the slice: x: 4, y: 4, z: 8 (z_hi: 4, z_lo: 2; z = z_hi * 2 + z_lo), core: 2. Of those that a mesh axis runs over, the one named last changes fastest.
Arguments:
- queries: bfloat16 [32, 16, 32, 3072], P('frame', 'row', 'head'), may hold values from -6 to 6
- key_tokens: bfloat16 [32, 16, 32, 3072], P('frame', 'row', 'head'), may hold values from -6 to 6
- values: bfloat16 [32, 16, 32, 3072], P('frame', 'row', 'head'), may hold values from -6 to 6
- outputs: bfloat16 [32, 16, 32, 3072], P('frame', 'row', 'head'), may hold values from -6 to 6
- grad_out: bfloat16 [32, 16, 32, 3072], P('frame', 'row', 'head'), may hold values from -48 to 48
- log_sums: float32 [24, 32, 16, 32], P('head', 'frame', 'row'), may hold values from 5.5 to 7.5
Outputs:
- grad_queries: bfloat16 [32, 16, 32, 3072], P('frame', 'row', 'head')
- grad_keys: bfloat16 [32, 16, 32, 3072], P('frame', 'row', 'head')
- grad_values: bfloat16 [32, 16, 32, 3072], P('frame', 'row', 'head')
All inputs are finite; a program needn't handle non-finite values.
Results may differ from a plain program's by a relative error of at most 0.0055.
Values may be sent and summed in bfloat16 or wider, within the bound.
No kernel may reach another device: no remote copies, remote signals or barrier semaphores. Data moves between devices by JAX's collectives and lax.ppermute only.
A program may use at most 128 MiB of HBM per device.

v0:
```python
import math

import jax
import jax.numpy as jnp
from jax import lax
from jax.experimental import pallas as pl
from jax.experimental.pallas import tpu as pltpu
from jax.sharding import Mesh
from jax.sharding import PartitionSpec as P

HD = 128
HEADS = 24
F, R, CH, C = 2, 2, 16, 32
ZH, ZL = 4, 2
Z = ZH * ZL
HL = HEADS // Z
FX = F * ZH
FE = FX + 4
NX, NROW = 4, 8
RING = ("zh", "zl")
BIG = -float(2**30)
SCALE = 1.0 / math.sqrt(HD)
LOG2E = math.log2(math.e)
DOT0, LSE0, LSE1, FR0, RW0 = 0, 16, 80, 32, 48
VMEM = 56 * 1024 * 1024
BF, F32 = jnp.bfloat16, jnp.float32


def params(**kw):
    return pltpu.CompilerParams(vmem_limit_bytes=VMEM, **kw)


def call(kernel, outs, n_in, name, flops=0, nbytes=1 << 20, scratch=()):
    whole = pl.BlockSpec(memory_space=pltpu.VMEM)
    return pl.pallas_call(
        kernel,
        out_shape=outs,
        in_specs=[whole] * n_in,
        out_specs=jax.tree.map(lambda _: whole, outs),
        scratch_shapes=list(scratch),
        compiler_params=params(),
        cost_estimate=pl.CostEstimate(flops=flops, bytes_accessed=nbytes, transcendentals=0),
        name=name,
    )


def shape(*dims, dtype=BF):
    return jax.ShapeDtypeStruct(dims, dtype)


def lanes(*dims):
    return lax.broadcasted_iota(jnp.int32, dims, len(dims) - 1)


def three(x):
    hi = x.astype(BF).astype(F32)
    mid = (x - hi).astype(BF).astype(F32)
    lo = (x - hi - mid).astype(BF).astype(F32)
    return hi, mid, lo


def head_of(dest, h):
    return (HEADS // ZL) * (dest % ZL) + HL * (dest // ZL) + h


def pack_q(q_ref, do_ref, o_ref, lse_ref, out_ref):
    parts = three(lse_ref[...] * math.sqrt(HD))
    row = lax.broadcasted_iota(jnp.int32, (128, 16), 0)
    col = lax.broadcasted_iota(jnp.int32, (128, 16), 1)
    spread = jnp.zeros((128, 128), F32)
    for p, part in enumerate(parts):
        put = jnp.zeros((128, 16), F32)
        for h in range(HL):
            put = jnp.where((row % 16 == 3 * h + p) & (row < 64) & (col == (row // 16) * HL + h), 1.0, put)
        spread = spread + jnp.dot(put.astype(BF), part.astype(BF), preferred_element_type=F32)
    turned = spread.T.reshape(F * R, ZL, CH, 128)
    both = turned[:, 0] + pltpu.roll(turned[:, 1].reshape(F * R * CH, 128), 64, 1).reshape(F * R, CH, 128)
    both = both.reshape(F * R * CH, 128)
    lane = lanes(F * R * CH, 128)
    for dest in range(Z):
        side = jnp.zeros((F * R * CH, 128), F32)
        for h in range(HL):
            at = head_of(dest, h) * HD
            q = q_ref[:, :, :, at : at + HD]
            g = do_ref[:, :, :, at : at + HD]
            out_ref[dest, h] = q
            out_ref[dest, HL + h] = g
            o = o_ref[:, :, :, at : at + HD]
            dot = jnp.sum((g.astype(F32) * o.astype(F32)).reshape(F * R * CH, HD), axis=-1, keepdims=True)
            for p, part in enumerate(three(dot)):
                side = jnp.where(lane == DOT0 + 3 * h + p, part, side)
        zh = dest // ZL
        turn = (LSE0 - 16 * zh) % 128
        lse = both if turn == 0 else pltpu.roll(both, turn, 1)
        keep = ((lane >= LSE0) & (lane < LSE0 + 9)) | ((lane >= LSE1) & (lane < LSE1 + 9))
        side = jnp.where(keep, lse, side)
        out_ref[dest, 2 * HL] = side.astype(BF).reshape(F, R, CH, 128)


def pack_kv(k_ref, v_ref, out_ref):
    for dest in range(Z):
        for h in range(HL):
            at = head_of(dest, h) * HD
            out_ref[dest, h] = k_ref[:, :, :, at : at + HD]
            out_ref[dest, HL + h] = v_ref[:, :, :, at : at + HD]


def place(blocks, in_ref, ext_ref, lo_ref, hi_ref):
    for src in range(Z):
        zh, zl = src // ZL, src % ZL
        cols = slice(zl * CH, zl * CH + CH)
        for b in range(blocks):
            for f in range(F):
                piece = in_ref[src, b, f]
                ext_ref[2 + F * zh + f, b, :, cols] = piece
                if zh == 0:
                    lo_ref[f, b, :, cols] = piece
                if zh == ZH - 1:
                    hi_ref[f, b, :, cols] = piece


def gather_q(in_ref, ext_ref, lo_ref, hi_ref):
    place(2 * HL, in_ref, ext_ref, lo_ref, hi_ref)
    mine = lax.axis_index("zl")
    n = F * R * CH
    lane = lanes(n, 128)
    for src in range(Z):
        zh, zl = src // ZL, src % ZL
        cols = slice(zl * CH, zl * CH + CH)
        dot = in_ref[src, 2 * HL].astype(F32).reshape(n, 128)
        lse = in_ref[ZL * zh + mine, 2 * HL].astype(F32).reshape(n, 128)
        if zl == 1:
            lse = pltpu.roll(lse, 64, 1)
        side = jnp.where(lane < 16, dot, jnp.where(lane < 32, lse, 0.0))
        side = side.astype(BF).reshape(F, R, CH, 128)
        for f in range(F):
            ext_ref[2 + F * zh + f, 2 * HL, :, cols] = side[f]
            if zh == 0:
                lo_ref[f, 2 * HL, :, cols] = side[f]
            if zh == ZH - 1:
                hi_ref[f, 2 * HL, :, cols] = side[f]


def gather_kv(in_ref, ext_ref, lo_ref, hi_ref):
    place(2 * HL, in_ref, ext_ref, lo_ref, hi_ref)


def fill_x(ext_ref, before_ref, after_ref, out_ref, sem):
    del ext_ref
    one = pltpu.make_async_copy(before_ref, out_ref.at[pl.ds(0, 2)], sem.at[0])
    two = pltpu.make_async_copy(after_ref, out_ref.at[pl.ds(FE - 2, 2)], sem.at[1])
    one.start()
    two.start()
    one.wait()
    two.wait()


def own_marks(group):
    dims = (F * R * C, 128)
    token = lax.broadcasted_iota(jnp.int32, dims, 0)
    lane = lanes(*dims)
    frame = 2 + F * group + token // (R * C)
    row = 2 + (token // C) % R
    x, r = lax.axis_index("x"), lax.axis_index("row")
    e = lane - FR0
    real = x * FX + e - 2
    bad = (jnp.abs(e - frame) > 2) | (real < 0) | (real >= NX * FX)
    out = jnp.where((e >= 0) & (e < FE) & bad, BIG, 0.0)
    e = lane - RW0
    real = r * R + e - 2
    bad = (jnp.abs(e - row) > 2) | (real < 0) | (real >= NROW * R)
    return jnp.where((e >= 0) & (e < R + 4) & bad, BIG, out)


def far_marks(part):
    dims = (FE, R * C, 128)
    lane = lanes(*dims)
    frame = lax.broadcasted_iota(jnp.int32, dims, 0)
    row = R * part + lax.broadcasted_iota(jnp.int32, dims, 1) // C
    return jnp.where((lane == FR0 + frame) | (lane == RW0 + row), 1.0, 0.0)


def minus_at(start, n):
    lane = lanes(n, 128)
    return jnp.where((lane >= start) & (lane < start + 3), -1.0, 0.0)


def nt(a, b):
    return lax.dot_general(a, b, (((1,), (1,)), ((), ())), preferred_element_type=F32)


def key_grads(qm_ref, qo_ref, qp_ref, kv_ref, out_ref, side_ref):
    n = F * R * C
    refs = (qm_ref, qo_ref, qp_ref)
    lane = lanes(FE, R * C, 128)
    for part, ref in enumerate(refs):
        data = ref[:, 2 * HL].astype(F32).reshape(FE, R * C, 128)
        side_ref[part] = jnp.where(lane < 32, data, far_marks(part)).astype(BF)
    for group in range(ZH):
        marks = own_marks(group)
        frames = slice(F * group, F * group + F + 4)
        m = (F + 4) * R * C
        side = jnp.concatenate([side_ref[part, frames].reshape(m, 128) for part in range(3)], axis=0)
        for h in range(HL):
            own = slice(2 + F * group, 2 + F * group + F)
            k = kv_ref[own, h].reshape(n, HD)
            v = kv_ref[own, HL + h].reshape(n, HD)
            q = jnp.concatenate([ref[frames, h].reshape(m, HD) for ref in refs], axis=0)
            g = jnp.concatenate([ref[frames, HL + h].reshape(m, HD) for ref in refs], axis=0)
            k_side = (marks + minus_at(LSE0 + 3 * h, n)).astype(BF)
            v_side = minus_at(DOT0 + 3 * h, n).astype(BF)
            s = nt(jnp.concatenate([k, k_side], axis=1), jnp.concatenate([q, side], axis=1))
            d = nt(jnp.concatenate([v, v_side], axis=1), jnp.concatenate([g, side], axis=1))
            prob = jnp.exp2(s * (SCALE * LOG2E))
            score = (prob * d).astype(BF)
            dv = jnp.dot(prob.astype(BF), g, preferred_element_type=F32)
            dk = jnp.dot(score, q, preferred_element_type=F32) * SCALE
            dk = dk.astype(BF).reshape(F, R, C, HD)
            dv = dv.astype(BF).reshape(F, R, C, HD)
            for zl in range(ZL):
                cols = slice(zl * CH, zl * CH + CH)
                out_ref[ZL * group + zl, h] = dk[:, :, cols]
                out_ref[ZL * group + zl, HL + h] = dv[:, :, cols]


def query_grads(km_ref, ko_ref, kp_ref, q_ref, out_ref):
    n = F * R * C
    refs = (km_ref, ko_ref, kp_ref)
    lane = lanes(n, 128)
    for group in range(ZH):
        frames = slice(F * group, F * group + F + 4)
        own = slice(2 + F * group, 2 + F * group + F)
        m = (F + 4) * R * C
        data = q_ref[own, 2 * HL].astype(F32).reshape(n, 128)
        side = jnp.where(lane < 32, data, own_marks(group)).astype(BF)
        far = jnp.concatenate([far_marks(part)[frames].reshape(m, 128) for part in range(3)], axis=0)
        for h in range(HL):
            q = q_ref[own, h].reshape(n, HD)
            g = q_ref[own, HL + h].reshape(n, HD)
            k = jnp.concatenate([ref[frames, h].reshape(m, HD) for ref in refs], axis=0)
            v = jnp.concatenate([ref[frames, HL + h].reshape(m, HD) for ref in refs], axis=0)
            k_side = (far + minus_at(LSE0 + 3 * h, 3 * m)).astype(BF)
            v_side = minus_at(DOT0 + 3 * h, 3 * m).astype(BF)
            s = nt(jnp.concatenate([q, side], axis=1), jnp.concatenate([k, k_side], axis=1))
            d = nt(jnp.concatenate([g, side], axis=1), jnp.concatenate([v, v_side], axis=1))
            score = (jnp.exp2(s * (SCALE * LOG2E)) * d).astype(BF)
            dq = jnp.dot(score, k, preferred_element_type=F32) * SCALE
            dq = dq.astype(BF).reshape(F, R, C, HD)
            for zl in range(ZL):
                out_ref[ZL * group + zl, h] = dq[:, :, zl * CH : zl * CH + CH]


def unpack(in_ref, *out_refs):
    for i, out_ref in enumerate(out_refs):
        for src in range(Z):
            for h in range(HL):
                at = head_of(src, h) * HD
                out_ref[:, :, :, at : at + HD] = in_ref[src, HL * i + h]


def exchange(sends):
    return lax.all_to_all(sends, RING, split_axis=0, concat_axis=0, tiled=True)


def shift(block, axis, by):
    count = NX if axis == "x" else NROW
    return lax.ppermute(block, axis, [(i, (i + by) % count) for i in range(count)])


def with_x(ext, lo, hi):
    before = shift(hi, "x", 1)
    after = shift(lo, "x", -1)
    anywhere = pl.BlockSpec(memory_space=pl.ANY)
    return pl.pallas_call(
        fill_x,
        out_shape=shape(*ext.shape),
        in_specs=[anywhere] * 3,
        out_specs=anywhere,
        scratch_shapes=[pltpu.SemaphoreType.DMA((2,))],
        input_output_aliases={0: 0},
        compiler_params=params(),
        name="fill_x",
    )(ext, before, after)


def gathered(kernel, blocks, arrived, name):
    outs = (
        shape(FE, blocks, R, C, HD),
        shape(F, blocks, R, C, HD),
        shape(F, blocks, R, C, HD),
    )
    return call(kernel, outs, 1, name)(arrived)


def body(queries, key_tokens, values, outputs, grad_out, log_sums):
    lse = jnp.pad(log_sums.reshape(HEADS // ZL, F * R * C), ((0, 4), (0, 0)))
    sent_q = call(pack_q, shape(Z, 2 * HL + 1, F, R, CH, HD), 4, "pack_q")(queries, grad_out, outputs, lse)
    sent_kv = call(pack_kv, shape(Z, 2 * HL, F, R, CH, HD), 2, "pack_kv")(key_tokens, values)
    q_here = exchange(sent_q)
    kv_here = exchange(sent_kv)
    q_ext = with_x(*gathered(gather_q, 2 * HL + 1, q_here, "gather_q"))
    q_before, q_after = shift(q_ext, "row", 1), shift(q_ext, "row", -1)
    kv_own, kv_lo, kv_hi = gathered(gather_kv, 2 * HL, kv_here, "gather_kv")
    kv_ext = with_x(kv_own, kv_lo, kv_hi)
    kv_before, kv_after = shift(kv_ext, "row", 1), shift(kv_ext, "row", -1)
    pairs = ZH * HL * F * R * C * (F + 4) * 3 * R * C
    grads_kv = call(
        key_grads,
        shape(Z, 2 * HL, F, R, CH, HD),
        4,
        "key_grads",
        flops=pairs * 1536,
        scratch=[pltpu.VMEM((3, FE, R * C, 128), BF)],
    )(q_before, q_ext, q_after, kv_ext)
    kv_back = exchange(grads_kv)
    grads_q = call(query_grads, shape(Z, HL, F, R, CH, HD), 4, "query_grads", flops=pairs * 1280)(
        kv_before, kv_ext, kv_after, q_ext
    )
    q_back = exchange(grads_q)
    block = shape(F, R, CH, HEADS * HD)
    key_out, value_out = call(unpack, (block, block), 1, "unpack_kv")(kv_back)
    (query_out,) = call(unpack, (block,), 1, "unpack_q")(q_back)
    return query_out, key_out, value_out


def solution(mesh):
    fine = Mesh(mesh.devices.reshape(NX, ZH, NROW, ZL), ("x", "zh", "row", "zl"))
    block = P(("x", "zh"), "row", "zl", None)
    return jax.shard_map(
        body,
        mesh=fine,
        in_specs=(block,) * 5 + (P("zl", ("x", "zh"), "row", None),),
        out_specs=(block,) * 3,
        check_vma=False,
    )
```

profile of v0, /device:TPU:32, one launch (start us, length us, event | category | flops | bytes accessed | tf_op | source)
XLA Modules:
  0.0 154.1 jit_solution(16830797113749974598)
XLA Ops:
  0.6 0.0 copy-start.8
  0.6 2.1 %pack_kv.1 = bf16[8,6,2,2,16,128]{5,4,3,2,1,0:T(8,128)(2,1)} custom-call(bf16[2,2,16,3072]{3,2,1,0:T(8,128)(2,1)} %k_ref.1, bf16[2,2,16,3072]{3,2,1,0:T(8,128)(2,1)} %v_ref.1), custom_call_target="tpu_custom_call" | custom-call | bytes 1048576 | tf_op jit(solution)/shard_map/pack_kv/pallas_call | solution.py:298
  2.8 8.6 %all-to-all-start = ((bf16[8,6,2,2,16,128]{5,4,3,2,1,0:T(8,128)(2,1)}), bf16[8,6,2,2,16,128]{5,4,3,2,1,0:T(8,128)(2,1)S(1)}, u32[]{:S(2)}, u32[]{:S(2)}) async-start(bf16[8,6,2,2,16,128]{5,4,3,2,1,0:T(8,128)(2,1)} %pack_kv.1), calls=%async_computation | async-start | bytes 1572864 | tf_op jit(solution)/shard_map/all_to_all | solution.py:262
  11.4 0.0 copy-done.8
  11.4 0.1 reshape.9
  11.4 0.6 pad.4.lse_ref
  12.1 2.7 %pack_q.1 = bf16[8,7,2,2,16,128]{5,4,3,2,1,0:T(8,128)(2,1)} custom-call(bf16[2,2,16,3072]{3,2,1,0:T(8,128)(2,1)} %q_ref.1, bf16[2,2,16,3072]{3,2,1,0:T(8,128)(2,1)} %do_ref.1, bf16[2,2,16,3072]{3,2,1,0:T(8,128)(2,1)} %o_ref.1, f32[16,128]{1,0:T(8,128)} %pad.4.lse_ref), custom_call_target="tpu_custom_call" | custom-call | bytes 1048576 | tf_op jit(solution)/shard_map/pack_q/pallas_call | solution.py:297
  14.8 18.3 %all-to-all-done.in_ref = bf16[8,6,2,2,16,128]{5,4,3,2,1,0:T(8,128)(2,1)S(1)} async-done(((bf16[8,6,2,2,16,128]{5,4,3,2,1,0:T(8,128)(2,1)}), bf16[8,6,2,2,16,128]{5,4,3,2,1,0:T(8,128)(2,1)S(1)}, u32[]{:S(2)}, u32[]{:S(2)}) %all-to-all-start) | async-done | bytes 786464 | tf_op jit(solution)/shard_map/all_to_all | solution.py:262
  33.0 0.0 copy-start.1
  33.0 4.9 %all-to-all-start.1 = ((bf16[8,7,2,2,16,128]{5,4,3,2,1,0:T(8,128)(2,1)}), bf16[8,7,2,2,16,128]{5,4,3,2,1,0:T(8,128)(2,1)S(1)}, u32[]{:S(2)}, u32[]{:S(2)}) async-start(bf16[8,7,2,2,16,128]{5,4,3,2,1,0:T(8,128)(2,1)} %pack_q.1), calls=%async_computation.1 | async-start | bytes 1835008 | tf_op jit(solution)/shard_map/all_to_all | solution.py:262
  37.9 0.0 copy-done.1
  37.9 2.3 %gather_kv.1 = (bf16[12,6,2,32,128]{4,3,2,1,0:T(8,128)(2,1)}, bf16[2,6,2,32,128]{4,3,2,1,0:T(8,128)(2,1)}, bf16[2,6,2,32,128]{4,3,2,1,0:T(8,128)(2,1)}) custom-call(bf16[8,6,2,2,16,128]{5,4,3,2,1,0:T(8,128)(2,1)} %copy-done.1), custom_call_target="tpu_custom_call" | custom-call | bytes 1048576 | tf_op jit(solution)/shard_map/gather_kv/pallas_call | solution.py:292
  40.3 1.5 collective-permute-start
  41.8 1.7 %collective-permute-start.1 = (bf16[2,6,2,32,128]{4,3,2,1,0:T(8,128)(2,1)}, bf16[2,6,2,32,128]{4,3,2,1,0:T(8,128)(2,1)S(1)}, u32[]{:S(2)}, u32[]{:S(2)}) collective-permute-start(bf16[2,6,2,32,128]{4,3,2,1,0:T(8,128)(2,1)} %get-tuple-element.13), channel_id=1, source_target_pairs={{0,192},{64,0},{128,64},{192,128},{1,193},{65,1},{129,65},{193,129... | collective-permute-start | bytes 589832 | tf_op jit(solution)/shard_map/ppermute | solution.py:267
  43.5 4.7 %collective-permute-done.before_ref = bf16[2,6,2,32,128]{4,3,2,1,0:T(8,128)(2,1)S(1)} collective-permute-done((bf16[2,6,2,32,128]{4,3,2,1,0:T(8,128)(2,1)}, bf16[2,6,2,32,128]{4,3,2,1,0:T(8,128)(2,1)S(1)}, u32[]{:S(2)}, u32[]{:S(2)}) %collective-permute-start) | collective-permute-done | bytes 196640 | tf_op jit(solution)/shard_map/ppermute | solution.py:267
  48.2 0.0 copy-start.6
  48.2 0.0 collective-permute-done.1.after_ref
  48.2 0.0 copy-start.7
  48.2 0.7 copy-done.6
  48.9 0.1 copy-done.7
  49.0 13.0 %fill_x.2.ko_ref.kv_ref = bf16[12,6,2,32,128]{4,3,2,1,0:T(8,128)(2,1)} custom-call(bf16[12,6,2,32,128]{4,3,2,1,0:T(8,128)(2,1)} %get-tuple-element.11.ext_ref, bf16[2,6,2,32,128]{4,3,2,1,0:T(8,128)(2,1)} %copy-done.6, bf16[2,6,2,32,128]{4,3,2,1,0:T(8,128)(2,1)} %copy-done.7), custom_call_target="tpu_custom_call", output_to_operand_aliasing={{}: (0, {})} | custom-call | tf_op jit(solution)/shard_map/fill_x/pallas_call | solution.py:274
  62.0 1.5 collective-permute-start.3
  63.5 0.0 collective-permute-start.2
  63.5 0.0 all-to-all-done.1.in_ref
  63.5 0.0 copy-start
  63.5 1.0 copy-done
  64.5 2.5 %gather_q.1 = (bf16[12,7,2,32,128]{4,3,2,1,0:T(8,128)(2,1)}, bf16[2,7,2,32,128]{4,3,2,1,0:T(8,128)(2,1)}, bf16[2,7,2,32,128]{4,3,2,1,0:T(8,128)(2,1)}) custom-call(bf16[8,7,2,2,16,128]{5,4,3,2,1,0:T(8,128)(2,1)} %copy-done), custom_call_target="tpu_custom_call" | custom-call | bytes 1048576 | tf_op jit(solution)/shard_map/gather_q/pallas_call | solution.py:292
  67.0 1.1 collective-permute-start.4
  68.1 2.1 %collective-permute-start.5 = (bf16[2,7,2,32,128]{4,3,2,1,0:T(8,128)(2,1)}, bf16[2,7,2,32,128]{4,3,2,1,0:T(8,128)(2,1)S(1)}, u32[]{:S(2)}, u32[]{:S(2)}) collective-permute-start(bf16[2,7,2,32,128]{4,3,2,1,0:T(8,128)(2,1)} %get-tuple-element.16), channel_id=1, source_target_pairs={{0,192},{64,0},{128,64},{192,128},{1,193},{65,1},{129,65},{193,129... | collective-permute-start | bytes 688136 | tf_op jit(solution)/shard_map/ppermute | solution.py:267
  70.2 5.9 %collective-permute-done.4.before_ref = bf16[2,7,2,32,128]{4,3,2,1,0:T(8,128)(2,1)S(1)} collective-permute-done((bf16[2,7,2,32,128]{4,3,2,1,0:T(8,128)(2,1)}, bf16[2,7,2,32,128]{4,3,2,1,0:T(8,128)(2,1)S(1)}, u32[]{:S(2)}, u32[]{:S(2)}) %collective-permute-start.4) | collective-permute-done | bytes 229408 | tf_op jit(solution)/shard_map/ppermute | solution.py:267
  76.2 0.0 copy-start.4
  76.2 0.0 collective-permute-done.5.after_ref
  76.2 0.0 copy-start.5
  76.2 0.7 copy-done.4
  76.9 0.1 copy-done.5
  76.9 15.0 %fill_x.3.q_ref.qo_ref = bf16[12,7,2,32,128]{4,3,2,1,0:T(8,128)(2,1)} custom-call(bf16[12,7,2,32,128]{4,3,2,1,0:T(8,128)(2,1)} %get-tuple-element.14.ext_ref, bf16[2,7,2,32,128]{4,3,2,1,0:T(8,128)(2,1)} %copy-done.4, bf16[2,7,2,32,128]{4,3,2,1,0:T(8,128)(2,1)} %copy-done.5), custom_call_target="tpu_custom_call", output_to_operand_aliasing={{}: (0, {})} | custom-call | tf_op jit(solution)/shard_map/fill_x/pallas_call | solution.py:274
  92.0 2.8 %collective-permute-start.7 = (bf16[12,7,2,32,128]{4,3,2,1,0:T(8,128)(2,1)}, bf16[12,7,2,32,128]{4,3,2,1,0:T(8,128)(2,1)S(1)}, u32[]{:S(2)}, u32[]{:S(2)}) collective-permute-start(bf16[12,7,2,32,128]{4,3,2,1,0:T(8,128)(2,1)} %fill_x.3.q_ref.qo_ref), channel_id=1, source_target_pairs={{0,14},{2,0},{4,2},{6,4},{8,6},{10,8},{12,10},{14,12},{1,15},{3,1}... | collective-permute-start | bytes 4128776 | tf_op jit(solution)/shard_map/ppermute | solution.py:267
  94.8 0.0 collective-permute-start.6
  94.8 0.0 collective-permute-done.3.kp_ref
  94.8 0.0 collective-permute-done.2.km_ref
  94.8 9.0 %query_grads.1 = bf16[8,3,2,2,16,128]{5,4,3,2,1,0:T(8,128)(2,1)} custom-call(bf16[12,6,2,32,128]{4,3,2,1,0:T(8,128)(2,1)} %collective-permute-done.2.km_ref, bf16[12,6,2,32,128]{4,3,2,1,0:T(8,128)(2,1)} %fill_x.2.ko_ref.kv_ref, bf16[12,6,2,32,128]{4,3,2,1,0:T(8,128)(2,1)} %collective-permute-done.3.kp_ref, bf16[12,7,2,32,128]{4,3,2,1,0:T(8,128)(2,1)} %fill_x.3.q_ref.qo_ref), custom_call_target="tpu_custom_call" | custom-call | flops 2264924160 | bytes 1048576 | tf_op jit(solution)/shard_map/query_grads/pallas_call | solution.py:316
  103.8 6.7 %all-to-all-start.2 = ((bf16[8,3,2,2,16,128]{5,4,3,2,1,0:T(8,128)(2,1)}), bf16[8,3,2,2,16,128]{5,4,3,2,1,0:T(8,128)(2,1)S(1)}, u32[]{:S(2)}, u32[]{:S(2)}) async-start(bf16[8,3,2,2,16,128]{5,4,3,2,1,0:T(8,128)(2,1)} %query_grads.1), calls=%async_computation.2 | async-start | bytes 786432 | tf_op jit(solution)/shard_map/all_to_all | solution.py:262
  110.5 0.4 collective-permute-done.7.qp_ref
  110.9 0.0 copy-start.9
  110.9 3.0 %collective-permute-done.6.qm_ref = bf16[12,7,2,32,128]{4,3,2,1,0:T(8,128)(2,1)S(1)} collective-permute-done((bf16[12,7,2,32,128]{4,3,2,1,0:T(8,128)(2,1)}, bf16[12,7,2,32,128]{4,3,2,1,0:T(8,128)(2,1)S(1)}, u32[]{:S(2)}, u32[]{:S(2)}) %collective-permute-start.6) | collective-permute-done | bytes 1376288 | tf_op jit(solution)/shard_map/ppermute | solution.py:267
  113.9 0.0 copy-done.9
  113.9 0.0 copy-start.10
  113.9 1.1 copy-done.10
  115.0 9.7 %key_grads.1 = bf16[8,6,2,2,16,128]{5,4,3,2,1,0:T(8,128)(2,1)} custom-call(bf16[12,7,2,32,128]{4,3,2,1,0:T(8,128)(2,1)} %copy-done.10, bf16[12,7,2,32,128]{4,3,2,1,0:T(8,128)(2,1)} %fill_x.3.q_ref.qo_ref, bf16[12,7,2,32,128]{4,3,2,1,0:T(8,128)(2,1)} %copy-done.9, bf16[12,6,2,32,128]{4,3,2,1,0:T(8,128)(2,1)} %fill_x.2.ko_ref.kv_ref), custom_call_target="tpu_custom_call" | custom-call | flops 2717908992 | bytes 1048576 | tf_op jit(solution)/shard_map/key_grads/pallas_call | solution.py:307
  124.8 0.0 all-to-all-done.2.in_ref
  124.8 0.0 copy-start.3
  124.8 6.7 %all-to-all-start.3 = ((bf16[8,6,2,2,16,128]{5,4,3,2,1,0:T(8,128)(2,1)}), bf16[8,6,2,2,16,128]{5,4,3,2,1,0:T(8,128)(2,1)S(1)}, u32[]{:S(2)}, u32[]{:S(2)}) async-start(bf16[8,6,2,2,16,128]{5,4,3,2,1,0:T(8,128)(2,1)} %key_grads.1), calls=%async_computation.3 | async-start | bytes 1572864 | tf_op jit(solution)/shard_map/all_to_all | solution.py:262
  131.4 0.0 copy-done.3
  131.4 1.8 %unpack_q.1 = bf16[2,2,16,3072]{3,2,1,0:T(8,128)(2,1)} custom-call(bf16[8,3,2,2,16,128]{5,4,3,2,1,0:T(8,128)(2,1)} %copy-done.3), custom_call_target="tpu_custom_call" | custom-call | bytes 1048576 | tf_op jit(solution)/shard_map/unpack_q/pallas_call | solution.py:322
  133.2 17.8 %all-to-all-done.3.in_ref = bf16[8,6,2,2,16,128]{5,4,3,2,1,0:T(8,128)(2,1)S(1)} async-done(((bf16[8,6,2,2,16,128]{5,4,3,2,1,0:T(8,128)(2,1)}), bf16[8,6,2,2,16,128]{5,4,3,2,1,0:T(8,128)(2,1)S(1)}, u32[]{:S(2)}, u32[]{:S(2)}) %all-to-all-start.3) | async-done | bytes 786464 | tf_op jit(solution)/shard_map/all_to_all | solution.py:262
  151.0 0.0 copy-start.2
  151.0 0.9 copy-done.2
  151.9 2.2 %unpack_kv.1 = (bf16[2,2,16,3072]{3,2,1,0:T(8,128)(2,1)}, bf16[2,2,16,3072]{3,2,1,0:T(8,128)(2,1)}) custom-call(bf16[8,6,2,2,16,128]{5,4,3,2,1,0:T(8,128)(2,1)} %copy-done.2), custom_call_target="tpu_custom_call" | custom-call | bytes 1048576 | tf_op jit(solution)/shard_map/unpack_kv/pallas_call | solution.py:321
Async XLA Ops:
  0.6 10.7 %copy-start.8 = (f32[12,2,2,32]{3,2,1,0:T(2,128)S(1)}, f32[12,2,2,32]{3,2,1,0:T(2,128)}, u32[]{:S(2)}) copy-start(f32[12,2,2,32]{3,2,1,0:T(2,128)} %param.11) | copy-start | bytes 18436
  2.8 30.2 %all-to-all-start = ((bf16[8,6,2,2,16,128]{5,4,3,2,1,0:T(8,128)(2,1)}), bf16[8,6,2,2,16,128]{5,4,3,2,1,0:T(8,128)(2,1)S(1)}, u32[]{:S(2)}, u32[]{:S(2)}) async-start(bf16[8,6,2,2,16,128]{5,4,3,2,1,0:T(8,128)(2,1)} %pack_kv.1), calls=%async_computation | async-start | bytes 1572864 | tf_op jit(solution)/shard_map/all_to_all | solution.py:262
  33.0 4.9 %copy-start.1 = (bf16[8,6,2,2,16,128]{5,4,3,2,1,0:T(8,128)(2,1)}, bf16[8,6,2,2,16,128]{5,4,3,2,1,0:T(8,128)(2,1)S(1)}, u32[]{:S(2)}) copy-start(bf16[8,6,2,2,16,128]{5,4,3,2,1,0:T(8,128)(2,1)S(1)} %all-to-all-done.in_ref) | copy-start | bytes 2359300
  33.0 30.5 %all-to-all-start.1 = ((bf16[8,7,2,2,16,128]{5,4,3,2,1,0:T(8,128)(2,1)}), bf16[8,7,2,2,16,128]{5,4,3,2,1,0:T(8,128)(2,1)S(1)}, u32[]{:S(2)}, u32[]{:S(2)}) async-start(bf16[8,7,2,2,16,128]{5,4,3,2,1,0:T(8,128)(2,1)} %pack_q.1), calls=%async_computation.1 | async-start | bytes 1835008 | tf_op jit(solution)/shard_map/all_to_all | solution.py:262
  40.3 8.0 %collective-permute-start = (bf16[2,6,2,32,128]{4,3,2,1,0:T(8,128)(2,1)}, bf16[2,6,2,32,128]{4,3,2,1,0:T(8,128)(2,1)S(1)}, u32[]{:S(2)}, u32[]{:S(2)}) collective-permute-start(bf16[2,6,2,32,128]{4,3,2,1,0:T(8,128)(2,1)} %get-tuple-element.12), channel_id=1, source_target_pairs={{0,64},{64,128},{128,192},{192,0},{1,65},{65,129},{129,193},{193,1... | collective-permute-start | bytes 589832 | tf_op jit(solution)/shard_map/ppermute | solution.py:267
  41.8 6.5 %collective-permute-start.1 = (bf16[2,6,2,32,128]{4,3,2,1,0:T(8,128)(2,1)}, bf16[2,6,2,32,128]{4,3,2,1,0:T(8,128)(2,1)S(1)}, u32[]{:S(2)}, u32[]{:S(2)}) collective-permute-start(bf16[2,6,2,32,128]{4,3,2,1,0:T(8,128)(2,1)} %get-tuple-element.13), channel_id=1, source_target_pairs={{0,192},{64,0},{128,64},{192,128},{1,193},{65,1},{129,65},{193,129... | collective-permute-start | bytes 589832 | tf_op jit(solution)/shard_map/ppermute | solution.py:267
  48.2 0.7 copy-start.6
  48.2 0.7 copy-start.7
  62.0 32.8 %collective-permute-start.3 = (bf16[12,6,2,32,128]{4,3,2,1,0:T(8,128)(2,1)}, bf16[12,6,2,32,128]{4,3,2,1,0:T(8,128)(2,1)}, u32[]{:S(2)}, u32[]{:S(2)}) collective-permute-start(bf16[12,6,2,32,128]{4,3,2,1,0:T(8,128)(2,1)} %fill_x.2.ko_ref.kv_ref), channel_id=1, source_target_pairs={{0,14},{2,0},{4,2},{6,4},{8,6},{10,8},{12,10},{14,12},{1,15},{3,1}... | collective-permute-start | bytes 3538952 | tf_op jit(solution)/shard_map/ppermute | solution.py:267
  63.5 31.3 %collective-permute-start.2 = (bf16[12,6,2,32,128]{4,3,2,1,0:T(8,128)(2,1)}, bf16[12,6,2,32,128]{4,3,2,1,0:T(8,128)(2,1)}, u32[]{:S(2)}, u32[]{:S(2)}) collective-permute-start(bf16[12,6,2,32,128]{4,3,2,1,0:T(8,128)(2,1)} %fill_x.2.ko_ref.kv_ref), channel_id=1, source_target_pairs={{0,2},{2,4},{4,6},{6,8},{8,10},{10,12},{12,14},{14,0},{1,3},{3,5},... | collective-permute-start | bytes 3538952 | tf_op jit(solution)/shard_map/ppermute | solution.py:267
  63.5 1.0 copy-start
  67.0 9.2 %collective-permute-start.4 = (bf16[2,7,2,32,128]{4,3,2,1,0:T(8,128)(2,1)}, bf16[2,7,2,32,128]{4,3,2,1,0:T(8,128)(2,1)S(1)}, u32[]{:S(2)}, u32[]{:S(2)}) collective-permute-start(bf16[2,7,2,32,128]{4,3,2,1,0:T(8,128)(2,1)} %get-tuple-element.15), channel_id=1, source_target_pairs={{0,64},{64,128},{128,192},{192,0},{1,65},{65,129},{129,193},{193,1... | collective-permute-start | bytes 688136 | tf_op jit(solution)/shard_map/ppermute | solution.py:267
  68.1 8.1 %collective-permute-start.5 = (bf16[2,7,2,32,128]{4,3,2,1,0:T(8,128)(2,1)}, bf16[2,7,2,32,128]{4,3,2,1,0:T(8,128)(2,1)S(1)}, u32[]{:S(2)}, u32[]{:S(2)}) collective-permute-start(bf16[2,7,2,32,128]{4,3,2,1,0:T(8,128)(2,1)} %get-tuple-element.16), channel_id=1, source_target_pairs={{0,192},{64,0},{128,64},{192,128},{1,193},{65,1},{129,65},{193,129... | collective-permute-start | bytes 688136 | tf_op jit(solution)/shard_map/ppermute | solution.py:267
  76.2 0.7 copy-start.4
  76.2 0.8 copy-start.5
  92.0 18.9 %collective-permute-start.7 = (bf16[12,7,2,32,128]{4,3,2,1,0:T(8,128)(2,1)}, bf16[12,7,2,32,128]{4,3,2,1,0:T(8,128)(2,1)S(1)}, u32[]{:S(2)}, u32[]{:S(2)}) collective-permute-start(bf16[12,7,2,32,128]{4,3,2,1,0:T(8,128)(2,1)} %fill_x.3.q_ref.qo_ref), channel_id=1, source_target_pairs={{0,14},{2,0},{4,2},{6,4},{8,6},{10,8},{12,10},{14,12},{1,15},{3,1}... | collective-permute-start | bytes 4128776 | tf_op jit(solution)/shard_map/ppermute | solution.py:267
  94.8 19.2 %collective-permute-start.6 = (bf16[12,7,2,32,128]{4,3,2,1,0:T(8,128)(2,1)}, bf16[12,7,2,32,128]{4,3,2,1,0:T(8,128)(2,1)S(1)}, u32[]{:S(2)}, u32[]{:S(2)}) collective-permute-start(bf16[12,7,2,32,128]{4,3,2,1,0:T(8,128)(2,1)} %fill_x.3.q_ref.qo_ref), channel_id=1, source_target_pairs={{0,2},{2,4},{4,6},{6,8},{8,10},{10,12},{12,14},{14,0},{1,3},{3,5},... | collective-permute-start | bytes 4128776 | tf_op jit(solution)/shard_map/ppermute | solution.py:267
  103.8 21.0 %all-to-all-start.2 = ((bf16[8,3,2,2,16,128]{5,4,3,2,1,0:T(8,128)(2,1)}), bf16[8,3,2,2,16,128]{5,4,3,2,1,0:T(8,128)(2,1)S(1)}, u32[]{:S(2)}, u32[]{:S(2)}) async-start(bf16[8,3,2,2,16,128]{5,4,3,2,1,0:T(8,128)(2,1)} %query_grads.1), calls=%async_computation.2 | async-start | bytes 786432 | tf_op jit(solution)/shard_map/all_to_all | solution.py:262
  110.9 3.0 %copy-start.9 = (bf16[12,7,2,32,128]{4,3,2,1,0:T(8,128)(2,1)}, bf16[12,7,2,32,128]{4,3,2,1,0:T(8,128)(2,1)S(1)}, u32[]{:S(2)}) copy-start(bf16[12,7,2,32,128]{4,3,2,1,0:T(8,128)(2,1)S(1)} %collective-permute-done.7.qp_ref) | copy-start | bytes 4128772
  113.9 1.1 copy-start.10
  124.8 6.7 %copy-start.3 = (bf16[8,3,2,2,16,128]{5,4,3,2,1,0:T(8,128)(2,1)}, bf16[8,3,2,2,16,128]{5,4,3,2,1,0:T(8,128)(2,1)S(1)}, u32[]{:S(2)}) copy-start(bf16[8,3,2,2,16,128]{5,4,3,2,1,0:T(8,128)(2,1)S(1)} %all-to-all-done.2.in_ref) | copy-start | bytes 1179652
  124.8 26.3 %all-to-all-start.3 = ((bf16[8,6,2,2,16,128]{5,4,3,2,1,0:T(8,128)(2,1)}), bf16[8,6,2,2,16,128]{5,4,3,2,1,0:T(8,128)(2,1)S(1)}, u32[]{:S(2)}, u32[]{:S(2)}) async-start(bf16[8,6,2,2,16,128]{5,4,3,2,1,0:T(8,128)(2,1)} %key_grads.1), calls=%async_computation.3 | async-start | bytes 1572864 | tf_op jit(solution)/shard_map/all_to_all | solution.py:262
  151.0 0.9 copy-start.2
where the time goes:
time: 156 us; the launch traced here: 154 us
  Pallas kernels  60.5 us (39%)
  waiting for transfers between devices  50.2 us (32%)
  starting transfers between devices  37.6 us (24%)
  local copies, waits for them, and re-layouts  5.15 us (3%)
    all_to_all x4, waiting for transfers between devices, exchange(): return lax.all_to_all(sends, RING, split_axis=0, concat_axis=0, tiled=True)  36.1 us
    pallas_call x2, Pallas kernels, with_x(): pl.pallas_call(fill_x, out_shape=shape(*ext.shape), in_specs=[anywhere] *...  28 us
    all_to_all x4, starting transfers between devices, exchange(): return lax.all_to_all(sends, RING, split_axis=0, concat_axis=0, tiled=True)  26.8 us
    ppermute x8, waiting for transfers between devices, shift(): lax.ppermute(block, axis, [(i, (i + by) % count) for i in range(count)])  14.1 us
    ppermute x8, starting transfers between devices, shift(): lax.ppermute(block, axis, [(i, (i + by) % count) for i in range(count)])  10.8 us
    pallas_call x1, Pallas kernels, body(): call(key_grads, shape(Z, 2 * HL, F, R, CH, HD), 4, 'key_grads', flops=pai...  9.74 us
    pallas_call x1, Pallas kernels, body(): call(query_grads, shape(Z, HL, F, R, CH, HD), 4, 'query_grads', flops=pai...  9.03 us
    pallas_call x2, Pallas kernels, gathered(): return call(kernel, outs, 1, name)(arrived)  4.86 us
  transfers between devices with their start and end apart: 12, of which 6 were waited for; matrix products, arithmetic and copies ran while one was open for 0% of the time, Pallas kernels for 36%

commit v1 on v0

v1 whole, which is shorter than its diff:
```python
import math

import jax
import jax.numpy as jnp
from jax import lax
from jax.experimental import pallas as pl
from jax.experimental.pallas import tpu as pltpu
from jax.sharding import Mesh
from jax.sharding import PartitionSpec as P

HD = 128
HEADS = 24
F, R, CH = 2, 2, 16
ZH, ZL = 4, 2
Z = ZH * ZL
N = F * R * CH
HL = HEADS // Z
FX = F * ZH
FE = FX + 4
NX, NROW = 4, 8
RING = ("zh", "zl")
FAR = (4, 3, 5, 2, 6, 1, 7)
BIG = -float(2**30)
SCALE = 1.0 / math.sqrt(HD)
LOG2E = math.log2(math.e)
DOT0, LSE0, LSE1, FR0, RW0 = 0, 16, 80, 32, 48
VMEM = 28 * 1024 * 1024
SPAN = 2
BF, F32 = jnp.bfloat16, jnp.float32


def params(**kw):
    return pltpu.CompilerParams(vmem_limit_bytes=VMEM, **kw)


def call(kernel, outs, n_in, name, flops=0, nbytes=1 << 20, scratch=(), where=pltpu.VMEM, after=()):
    whole = pl.BlockSpec(memory_space=where)
    inner = lambda *refs: kernel(*refs[:n_in], *refs[n_in + len(after) :])
    made = pl.pallas_call(
        inner,
        out_shape=outs,
        in_specs=[whole] * n_in + [pl.BlockSpec(memory_space=pl.ANY)] * len(after),
        out_specs=jax.tree.map(lambda _: pl.BlockSpec(memory_space=pltpu.VMEM), outs),
        scratch_shapes=list(scratch),
        compiler_params=params(),
        cost_estimate=pl.CostEstimate(flops=flops, bytes_accessed=nbytes, transcendentals=0),
        name=name,
    )
    return lambda *args: made(*args, *after)


def shape(*dims, dtype=BF):
    return jax.ShapeDtypeStruct(dims, dtype)


def lanes(*dims):
    return lax.broadcasted_iota(jnp.int32, dims, len(dims) - 1)


def three(x):
    hi = x.astype(BF).astype(F32)
    mid = (x - hi).astype(BF).astype(F32)
    lo = (x - hi - mid).astype(BF).astype(F32)
    return hi, mid, lo


def head_of(dest, h):
    return (HEADS // ZL) * (dest % ZL) + HL * (dest // ZL) + h


def ring_place():
    return lax.axis_index("zh") * ZL + lax.axis_index("zl")


def head_lanes(dest, h):
    return pl.ds(pl.multiple_of(head_of(dest, h) * HD, HD), HD)


def pack(q_ref, do_ref, o_ref, k_ref, v_ref, lse_ref, *out_refs):
    parts = three(lse_ref[...] * math.sqrt(HD))
    row = lax.broadcasted_iota(jnp.int32, (128, 16), 0)
    col = lax.broadcasted_iota(jnp.int32, (128, 16), 1)
    spread = jnp.zeros((128, 128), F32)
    for p, part in enumerate(parts):
        put = jnp.zeros((128, 16), F32)
        for h in range(HL):
            put = jnp.where((row % 16 == 3 * h + p) & (row < 64) & (col == (row // 16) * HL + h), 1.0, put)
        spread = spread + jnp.dot(put.astype(BF), part.astype(BF), preferred_element_type=F32)
    turned = spread.T.reshape(F * R, ZL, CH, 128)
    second = pltpu.roll(turned[:, 1].reshape(N, 128), 64, 1)
    both = turned[:, 0].reshape(N, 128) + second
    lane = lanes(N, 128)
    keep = ((lane >= LSE0) & (lane < LSE0 + 9)) | ((lane >= LSE1) & (lane < LSE1 + 9))
    for k, out_ref in enumerate(out_refs):
        dest = lax.rem(ring_place() + k, Z)
        side = jnp.zeros((N, 128), F32)
        for h in range(HL):
            at = head_lanes(dest, h)
            g = do_ref[:, :, :, at]
            out_ref[2 * h] = q_ref[:, :, :, at]
            out_ref[2 * h + 1] = g
            out_ref[2 * HL + 1 + 2 * h] = k_ref[:, :, :, at]
            out_ref[2 * HL + 2 + 2 * h] = v_ref[:, :, :, at]
            dot = jnp.sum((g.astype(F32) * o_ref[:, :, :, at].astype(F32)).reshape(N, HD), axis=-1, keepdims=True)
            for p, part in enumerate(three(dot)):
                side = jnp.where(lane == DOT0 + 3 * h + p, part, side)
        lse = pltpu.roll(both, lax.rem(128 + LSE0 - 16 * (dest // ZL), 128), 1)
        out_ref[2 * HL] = jnp.where(keep, lse, side).astype(BF).reshape(F, R, CH, 128)


def gather_q(*refs):
    in_refs, (out_ref, lo_ref, hi_ref) = refs[:Z], refs[Z:]
    for k, in_ref in enumerate(in_refs):
        out_ref[lax.rem(ring_place() + Z - k, Z)] = in_ref[: 2 * HL + 1]
    mine = lax.axis_index("zl")
    lane = lanes(N, 128)
    for zh in range(ZH):
        lse = out_ref[ZL * zh + mine, 2 * HL].astype(F32).reshape(N, 128)
        for zl in range(ZL):
            dot = out_ref[ZL * zh + zl, 2 * HL].astype(F32).reshape(N, 128)
            here = lse if zl == 0 else pltpu.roll(lse, 64, 1)
            side = jnp.where(lane < 16, dot, jnp.where(lane < 32, here, 0.0))
            out_ref[ZL * zh + zl, 2 * HL] = side.astype(BF).reshape(F, R, CH, 128)
    lo_ref[...] = out_ref[:ZL]
    hi_ref[...] = out_ref[Z - ZL :]


def gather_kv(*refs):
    in_refs, (out_ref, lo_ref, hi_ref) = refs[:Z], refs[Z:]
    for k, in_ref in enumerate(in_refs):
        out_ref[lax.rem(ring_place() + Z - k, Z)] = in_ref[2 * HL + 1 :]
    lo_ref[...] = out_ref[:ZL]
    hi_ref[...] = out_ref[Z - ZL :]


def bad_frames(e, frame):
    real = lax.axis_index("x") * FX + e - 2
    return (jnp.abs(e - frame) > 2) | (real < 0) | (real >= NX * FX)


def bad_rows(e, row):
    real = lax.axis_index("row") * R + e - 2
    return (jnp.abs(e - row) > 2) | (real < 0) | (real >= NROW * R)


def far_place(part, group, dims, axis):
    token = lax.broadcasted_iota(jnp.int32, dims, axis)
    frame = F * (group + token // (ZL * N)) + (token // (R * CH)) % F
    return frame, R * part + (token // CH) % R


def seen(own, sides, group, block):
    first, last = group - 1, group + SPAN + 1
    pieces = [own[ZL * max(first, 0) : ZL * min(last, ZH), block]]
    if first < 0:
        pieces.insert(0, sides[:ZL, block])
    if last > ZH:
        pieces.append(sides[ZL:, block])
    pieces = [piece.reshape(-1, 128) for piece in pieces]
    return pieces[0] if len(pieces) == 1 else jnp.concatenate(pieces, axis=0)


def by_class(rows):
    m = rows.shape[1]
    spread = [jnp.broadcast_to(rows[i : i + 1], (CH, m)) for i in range(SPAN * F * R)]
    order = [z * F * R + i for z in range(SPAN) for _ in range(ZL) for i in range(F * R)]
    return jnp.concatenate([spread[i] for i in order], axis=0)


def nt(a, b):
    return lax.dot_general(a, b, (((1,), (1,)), ((), ())), preferred_element_type=F32)


def fetch(in_refs, bufs, sems):
    copies = {}
    for h in [HL] + list(range(HL)):
        for i, (ref, buf) in enumerate(zip(in_refs, bufs)):
            size = 2 if h < HL else 1
            if 2 * h < buf.shape[1]:
                at = pl.ds(2 * h, size)
                copies[h, i] = pltpu.make_async_copy(ref.at[:, at], buf.at[:, at], sems.at[h, i])
                copies[h, i].start()

    def ready(h):
        for (at, _), copy in copies.items():
            if at == h:
                copy.wait()

    return ready


def key_grads(*refs):
    in_refs, out_ref, bufs, sems = refs[:7], refs[7], refs[8:15], refs[15]
    ready = fetch(in_refs, bufs, sems)
    parts, kv = list(zip(bufs[:3], bufs[3:6])), bufs[6]
    n, m = SPAN * ZL * N, (SPAN + 2) * ZL * N
    lane = lanes(m, 128)
    ready(HL)
    shifts = {}
    for group in range(0, ZH, SPAN):
        dims = (32, 128)
        row = lax.broadcasted_iota(jnp.int32, dims, 0)
        pick = lanes(*dims)
        e = pick - FR0
        bad = bad_frames(e, 2 + F * group + (row % 8) // R) & (e >= 0) & (e < FE)
        marks = jnp.where(bad, BIG, 0.0)
        e = pick - RW0
        bad = bad_rows(e, 2 + row % R) & (e >= 0) & (e < R + 4)
        marks = jnp.where(bad, BIG, marks)
        at = pick - LSE0 - 3 * (row // 8)
        marks = jnp.where((at >= 0) & (at < 3), -1.0, marks)
        at = pick - DOT0 - 3 * (row - 24)
        marks = jnp.where(row < 24, marks, jnp.where((at >= 0) & (at < 3) & (row < 24 + HL), -1.0, 0.0)).astype(BF)
        for i, (own, sides) in enumerate(parts):
            frame, far_row = far_place(i, group, (m, 128), 0)
            ones = jnp.where((lane == FR0 + frame) | (lane == RW0 + far_row), 1.0, 0.0)
            side = jnp.where(lane < 32, seen(own, sides, group, 2 * HL).astype(F32), ones).astype(BF)
            shifts[group, i] = nt(marks, side)
    for h in range(HL):
        ready(h)
        for group in range(0, ZH, SPAN):
            here = slice(ZL * group, ZL * (group + SPAN))
            k = kv[here, 2 * h].reshape(n, HD)
            v = kv[here, 2 * h + 1].reshape(n, HD)
            dk = jnp.zeros((n, HD), F32)
            dv = jnp.zeros((n, HD), F32)
            for i, (own, sides) in enumerate(parts):
                q, g = seen(own, sides, group, 2 * h), seen(own, sides, group, 2 * h + 1)
                s = nt(k, q) + by_class(shifts[group, i][8 * h : 8 * h + 8])
                d = nt(v, g) + shifts[group, i][24 + h : 25 + h]
                prob = jnp.exp2(s * (SCALE * LOG2E))
                dv = dv + jnp.dot(prob.astype(BF), g, preferred_element_type=F32)
                dk = dk + jnp.dot((prob * d).astype(BF), q, preferred_element_type=F32)
            out_ref[here, 2 * h] = (dk * SCALE).astype(BF).reshape(SPAN * ZL, F, R, CH, HD)
            out_ref[here, 2 * h + 1] = dv.astype(BF).reshape(SPAN * ZL, F, R, CH, HD)


def query_grads(*refs):
    in_refs, out_refs, all_ref, bufs, sems = refs[:7], refs[7 : 7 + Z], refs[7 + Z], refs[8 + Z : 15 + Z], refs[15 + Z]
    ready = fetch(in_refs, bufs, sems)
    parts, qg = list(zip(bufs[:3], bufs[3:6])), bufs[6]
    n, m = SPAN * ZL * N, (SPAN + 2) * ZL * N
    lane = lanes(n, 128)
    masks = {}
    for group in range(0, ZH, SPAN):
        row = lax.broadcasted_iota(jnp.int32, (8, m), 0)
        for i in range(3):
            frame, far_row = far_place(i, group, (8, m), 1)
            bad = bad_frames(frame, 2 + F * group + row // R) | bad_rows(far_row, 2 + row % R)
            masks[group, i] = jnp.where(bad, BIG, 0.0)
    ready(HL)
    for h in range(HL):
        ready(h)
        for group in range(0, ZH, SPAN):
            here = slice(ZL * group, ZL * (group + SPAN))
            q = qg[here, 2 * h].reshape(n, HD)
            g = qg[here, 2 * h + 1].reshape(n, HD)
            data = qg[here, 2 * HL].astype(F32).reshape(n, 128)
            pick = lambda start: jnp.where((lane >= start) & (lane < start + 3), data, 0.0)
            lse = jnp.sum(pick(LSE0 + 3 * h), axis=-1, keepdims=True)
            dot = jnp.sum(pick(DOT0 + 3 * h), axis=-1, keepdims=True)
            dq = jnp.zeros((n, HD), F32)
            for i, (own, sides) in enumerate(parts):
                k, v = seen(own, sides, group, 2 * h), seen(own, sides, group, 2 * h + 1)
                s = nt(q, k) - lse + by_class(masks[group, i])
                d = nt(g, v) - dot
                score = (jnp.exp2(s * (SCALE * LOG2E)) * d).astype(BF)
                dq = dq + jnp.dot(score, k, preferred_element_type=F32)
            all_ref[here, h] = (dq * SCALE).astype(BF).reshape(SPAN * ZL, F, R, CH, HD)
    for k, out_ref in enumerate(out_refs):
        out_ref[...] = all_ref[lax.rem(ring_place() + k, Z)]


def unpack_kv(in_ref, *out_refs):
    for i, out_ref in enumerate(out_refs):
        for src in range(Z):
            for h in range(HL):
                at = head_of(src, h) * HD
                out_ref[:, :, :, at : at + HD] = in_ref[src, 2 * h + i]


def unpack_q(*refs):
    out_ref = refs[-1]
    for k, in_ref in enumerate(refs[:-1]):
        src = lax.rem(ring_place() + Z - k, Z)
        for h in range(HL):
            out_ref[:, :, :, head_lanes(src, h)] = in_ref[h]


def exchange(sends):
    return lax.all_to_all(sends, RING, split_axis=0, concat_axis=0, tiled=True)


def exchange_by_steps(sends):
    got = list(sends)
    for k in FAR:
        got[k] = lax.ppermute(sends[k], RING, [(i, (i + k) % Z) for i in range(Z)])
    return got


def shift(block, dx, dr):
    places = [(x, r) for x in range(NX) for r in range(NROW)]
    flat = lambda x, r: (x % NX) * NROW + r % NROW
    return lax.ppermute(block, ("x", "row"), [(flat(x + dx, r + dr), flat(x, r)) for x, r in places])


def halo(own, lo, hi):
    rows = [shift(own, 0, -1), own, shift(own, 0, 1)]
    sides = jnp.concatenate([shift(hi, -1, 0), shift(lo, 1, 0)], axis=0)
    return rows + [shift(sides, 0, -1), sides, shift(sides, 0, 1)]


def staged(blocks, last):
    whole = [pltpu.VMEM((n, blocks, F, R, CH, HD), BF) for n in (Z, Z, Z, 2 * ZL, 2 * ZL, 2 * ZL)]
    return whole + [pltpu.VMEM((Z, last, F, R, CH, HD), BF), pltpu.SemaphoreType.DMA((HL + 1, 7))]


def body(queries, key_tokens, values, outputs, grad_out, log_sums):
    lse = jnp.pad(log_sums.reshape(HEADS // ZL, F * R * CH * ZL), ((0, 4), (0, 0)))
    q_block, kv_block, dq_block = (shape(b, F, R, CH, HD) for b in (2 * HL + 1, 2 * HL, HL))
    wide = lambda block, n: shape(n, *block.shape)
    both = shape(4 * HL + 1, F, R, CH, HD)
    sent = call(pack, (both,) * Z, 6, "pack")(queries, grad_out, outputs, key_tokens, values, lse)
    got = exchange_by_steps(sent)
    q_here, q_lo, q_hi = call(
        gather_q, (wide(q_block, Z), wide(q_block, ZL), wide(q_block, ZL)), Z, "gather_q"
    )(*got)
    q_seen = halo(q_here, q_lo, q_hi)
    kv_here, kv_lo, kv_hi = call(
        gather_kv, (wide(kv_block, Z), wide(kv_block, ZL), wide(kv_block, ZL)), Z, "gather_kv", after=q_seen[4:5]
    )(*got)
    kv_seen = halo(kv_here, kv_lo, kv_hi)
    grads_kv = call(
        key_grads,
        wide(kv_block, Z),
        7,
        "key_grads",
        flops=10**10,
        scratch=staged(2 * HL + 1, 2 * HL),
        where=pl.ANY,
        after=kv_seen[4:5],
    )(*q_seen, kv_here)
    kv_back = exchange(grads_kv)
    grads_q = call(
        query_grads,
        (dq_block,) * Z,
        7,
        "query_grads",
        flops=10**11,
        scratch=[pltpu.VMEM((Z, HL, F, R, CH, HD), BF)] + staged(2 * HL, 2 * HL + 1),
        where=pl.ANY,
    )(*kv_seen, q_here)
    q_back = exchange_by_steps(grads_q)
    whole = shape(F, R, CH, HEADS * HD)
    key_out, value_out = call(unpack_kv, (whole, whole), 1, "unpack_kv")(kv_back)
    query_out = call(unpack_q, whole, Z, "unpack_q")(*q_back)
    return query_out, key_out, value_out


def solution(mesh):
    fine = Mesh(mesh.devices.reshape(NX, ZH, NROW, ZL), ("x", "zh", "row", "zl"))
    block = P(("x", "zh"), "row", "zl", None)
    return jax.shard_map(
        body,
        mesh=fine,
        in_specs=(block,) * 5 + (P("zl", ("x", "zh"), "row", None),),
        out_specs=(block,) * 3,
        check_vma=False,
    )
```

time: 156 us -> 129 us (0.83)
  Pallas kernels: 60.5 us -> 17.9 us
  starting transfers between devices: 37.6 us -> 52.3 us
    pallas_call x10 -> x7, Pallas kernels: 60.5 us -> 17.9 us  [call(): return lambda *args: made(*args, *after)]
    ppermute x8 -> x26, starting transfers between devices: 10.8 us -> 48.5 us  [the longest x14 32.4 us: exchange_by_steps(): got[k] = lax.ppermute(sends[k], RING, [(i, (i + k) % Z) for i in range(Z)])]
    all_to_all x4 -> x1, waiting for transfers between devices: 36.1 us -> 0.01 us  [exchange(): return lax.all_to_all(sends, RING, split_axis=0, concat_axis=0, tiled=True)]
    ppermute x8 -> x26, waiting for transfers between devices: 14.1 us -> 49.9 us  [the longest x14 37.6 us: exchange_by_steps(): got[k] = lax.ppermute(sends[k], RING, [(i, (i + k) % Z) for i in range(Z)])]
    all_to_all x4 -> x1, starting transfers between devices: 26.8 us -> 3.89 us  [exchange(): return lax.all_to_all(sends, RING, split_axis=0, concat_axis=0, tiled=True)]
    unnamed x22 -> x12, local copies, waits for them, and re-layouts: 4.46 us -> 5 us
  transfers between devices with their start and end apart: 12 -> 27, of which waited for: 6 -> 14; matrix products, arithmetic and copies ran while one was open for 0% -> 0% of each run, Pallas kernels for 36% -> 12%
where the time goes in v1:
time: 129 us; the launch traced here: 127 us
  starting transfers between devices  52.3 us (41%)
  waiting for transfers between devices  49.9 us (39%)
  Pallas kernels  17.9 us (14%)
  local copies, waits for them, and re-layouts  5.89 us (5%)
    ppermute x14, waiting for transfers between devices, exchange_by_steps(): got[k] = lax.ppermute(sends[k], RING, [(i, (i + k) % Z) for i in range(Z)])  37.6 us
    ppermute x14, starting transfers between devices, exchange_by_steps(): got[k] = lax.ppermute(sends[k], RING, [(i, (i + k) % Z) for i in range(Z)])  32.4 us
    pallas_call x7, Pallas kernels, call(): return lambda *args: made(*args, *after)  17.9 us
    ppermute x12, starting transfers between devices, shift(): lax.ppermute(block, ('x', 'row'), [(flat(x + dx, r + dr), flat(x, r)) for...  16 us
    ppermute x12, waiting for transfers between devices, shift(): lax.ppermute(block, ('x', 'row'), [(flat(x + dx, r + dr), flat(x, r)) for...  12.2 us
    unnamed x12, local copies, waits for them, and re-layouts  5 us
    all_to_all x1, starting transfers between devices, exchange(): return lax.all_to_all(sends, RING, split_axis=0, concat_axis=0, tiled=True)  3.89 us
  transfers between devices with their start and end apart: 27, of which 14 were waited for; matrix products, arithmetic and copies ran while one was open for 0% of the time, Pallas kernels for 12%

profile of v1, /device:TPU:32, one launch (start us, length us, event | category | flops | bytes accessed | tf_op | source)
XLA Modules:
  0.0 126.7 jit_solution(2983703765422161942)
XLA Ops:
  0.6 0.8 reshape.9
  1.5 0.0 copy-start
  1.5 1.0 copy-done
  2.5 1.0 copy-done.1
  3.5 1.0 copy-done.2
  4.5 1.0 copy-done.3
  5.5 1.0 copy-done.4
  6.4 0.9 pack.1
  7.3 2.0 %collective-permute-start = (bf16[13,2,2,16,128]{4,3,2,1,0:T(8,128)(2,1)S(1)}, bf16[13,2,2,16,128]{4,3,2,1,0:T(8,128)(2,1)S(1)}, u32[]{:S(2)}, u32[]{:S(2)}) collective-permute-start(bf16[13,2,2,16,128]{4,3,2,1,0:T(8,128)(2,1)S(1)} %get-tuple-element.28), channel_id=1, source_target_pairs={{0,1},{1,16},{16,17},{17,32},{32,33},{33,48},{48,49},{49,0},{2,3},... | collective-permute-start | bytes 638984 | tf_op jit(solution)/shard_map/ppermute | solution.py:297
  9.3 4.5 %collective-permute-start.1 = (bf16[13,2,2,16,128]{4,3,2,1,0:T(8,128)(2,1)S(1)}, bf16[13,2,2,16,128]{4,3,2,1,0:T(8,128)(2,1)S(1)}, u32[]{:S(2)}, u32[]{:S(2)}) collective-permute-start(bf16[13,2,2,16,128]{4,3,2,1,0:T(8,128)(2,1)S(1)} %get-tuple-element.29), channel_id=1, source_target_pairs={{0,16},{1,17},{16,32},{17,33},{32,48},{33,49},{48,0},{49,1},{2,18}... | collective-permute-start | bytes 638984 | tf_op jit(solution)/shard_map/ppermute | solution.py:297
  13.8 1.9 %collective-permute-start.2 = (bf16[13,2,2,16,128]{4,3,2,1,0:T(8,128)(2,1)S(1)}, bf16[13,2,2,16,128]{4,3,2,1,0:T(8,128)(2,1)S(1)}, u32[]{:S(2)}, u32[]{:S(2)}) collective-permute-start(bf16[13,2,2,16,128]{4,3,2,1,0:T(8,128)(2,1)S(1)} %get-tuple-element.30), channel_id=1, source_target_pairs={{0,17},{1,32},{16,33},{17,48},{32,49},{33,0},{48,1},{49,16},{2,19}... | collective-permute-start | bytes 638984 | tf_op jit(solution)/shard_map/ppermute | solution.py:297
  15.7 1.4 %collective-permute-start.3 = (bf16[13,2,2,16,128]{4,3,2,1,0:T(8,128)(2,1)S(1)}, bf16[13,2,2,16,128]{4,3,2,1,0:T(8,128)(2,1)S(1)}, u32[]{:S(2)}, u32[]{:S(2)}) collective-permute-start(bf16[13,2,2,16,128]{4,3,2,1,0:T(8,128)(2,1)S(1)} %get-tuple-element.31), channel_id=1, source_target_pairs={{0,32},{1,33},{16,48},{17,49},{32,0},{33,1},{48,16},{49,17},{2,34}... | collective-permute-start | bytes 638984 | tf_op jit(solution)/shard_map/ppermute | solution.py:297
  17.2 3.1 %collective-permute-start.4 = (bf16[13,2,2,16,128]{4,3,2,1,0:T(8,128)(2,1)S(1)}, bf16[13,2,2,16,128]{4,3,2,1,0:T(8,128)(2,1)S(1)}, u32[]{:S(2)}, u32[]{:S(2)}) collective-permute-start(bf16[13,2,2,16,128]{4,3,2,1,0:T(8,128)(2,1)S(1)} %get-tuple-element.32), channel_id=1, source_target_pairs={{0,33},{1,48},{16,49},{17,0},{32,1},{33,16},{48,17},{49,32},{2,35}... | collective-permute-start | bytes 638984 | tf_op jit(solution)/shard_map/ppermute | solution.py:297
  20.3 0.0 collective-permute-done.refs_1_
  20.3 2.4 %collective-permute-start.5 = (bf16[13,2,2,16,128]{4,3,2,1,0:T(8,128)(2,1)S(1)}, bf16[13,2,2,16,128]{4,3,2,1,0:T(8,128)(2,1)S(1)}, u32[]{:S(2)}, u32[]{:S(2)}) collective-permute-start(bf16[13,2,2,16,128]{4,3,2,1,0:T(8,128)(2,1)S(1)} %get-tuple-element.33), channel_id=1, source_target_pairs={{0,48},{1,49},{16,0},{17,1},{32,16},{33,17},{48,32},{49,33},{2,50}... | collective-permute-start | bytes 638984 | tf_op jit(solution)/shard_map/ppermute | solution.py:297
  22.7 6.9 %collective-permute-done.1.refs_2_ = bf16[13,2,2,16,128]{4,3,2,1,0:T(8,128)(2,1)S(1)} collective-permute-done((bf16[13,2,2,16,128]{4,3,2,1,0:T(8,128)(2,1)S(1)}, bf16[13,2,2,16,128]{4,3,2,1,0:T(8,128)(2,1)S(1)}, u32[]{:S(2)}, u32[]{:S(2)}) %collective-permute-start.1) | collective-permute-done | bytes 213024 | tf_op jit(solution)/shard_map/ppermute | solution.py:297
  29.6 2.1 %collective-permute-start.6 = (bf16[13,2,2,16,128]{4,3,2,1,0:T(8,128)(2,1)S(1)}, bf16[13,2,2,16,128]{4,3,2,1,0:T(8,128)(2,1)S(1)}, u32[]{:S(2)}, u32[]{:S(2)}) collective-permute-start(bf16[13,2,2,16,128]{4,3,2,1,0:T(8,128)(2,1)S(1)} %get-tuple-element.34), channel_id=1, source_target_pairs={{0,49},{1,0},{16,1},{17,16},{32,17},{33,32},{48,33},{49,48},{2,51}... | collective-permute-start | bytes 638984 | tf_op jit(solution)/shard_map/ppermute | solution.py:297
  31.7 16.1 %collective-permute-done.2.refs_3_ = bf16[13,2,2,16,128]{4,3,2,1,0:T(8,128)(2,1)S(1)} collective-permute-done((bf16[13,2,2,16,128]{4,3,2,1,0:T(8,128)(2,1)S(1)}, bf16[13,2,2,16,128]{4,3,2,1,0:T(8,128)(2,1)S(1)}, u32[]{:S(2)}, u32[]{:S(2)}) %collective-permute-start.2) | collective-permute-done | bytes 213024 | tf_op jit(solution)/shard_map/ppermute | solution.py:297
  47.8 0.0 collective-permute-done.3.refs_4_
  47.8 0.0 collective-permute-done.4.refs_5_
  47.8 6.5 %collective-permute-done.5.refs_6_ = bf16[13,2,2,16,128]{4,3,2,1,0:T(8,128)(2,1)S(1)} collective-permute-done((bf16[13,2,2,16,128]{4,3,2,1,0:T(8,128)(2,1)S(1)}, bf16[13,2,2,16,128]{4,3,2,1,0:T(8,128)(2,1)S(1)}, u32[]{:S(2)}, u32[]{:S(2)}) %collective-permute-start.5) | collective-permute-done | bytes 213024 | tf_op jit(solution)/shard_map/ppermute | solution.py:297
  54.2 2.7 %collective-permute-done.6.refs_7_ = bf16[13,2,2,16,128]{4,3,2,1,0:T(8,128)(2,1)S(1)} collective-permute-done((bf16[13,2,2,16,128]{4,3,2,1,0:T(8,128)(2,1)S(1)}, bf16[13,2,2,16,128]{4,3,2,1,0:T(8,128)(2,1)S(1)}, u32[]{:S(2)}, u32[]{:S(2)}) %collective-permute-start.6) | collective-permute-done | bytes 213024 | tf_op jit(solution)/shard_map/ppermute | solution.py:297
  56.9 0.4 gather_q.1
  57.3 1.6 %collective-permute-start.7 = (bf16[2,7,2,2,16,128]{5,4,3,2,1,0:T(8,128)(2,1)S(1)}, bf16[2,7,2,2,16,128]{5,4,3,2,1,0:T(8,128)(2,1)S(1)}, u32[]{:S(2)}, u32[]{:S(2)}) collective-permute-start(bf16[2,7,2,2,16,128]{5,4,3,2,1,0:T(8,128)(2,1)S(1)} %get-tuple-element.35), channel_id=1, source_target_pairs={{192,0},{194,2},{196,4},{198,6},{200,8},{202,10},{204,12},{206,14}... | collective-permute-start | bytes 688136 | tf_op jit(solution)/shard_map/ppermute | solution.py:304
  58.9 3.0 %collective-permute-start.23 = (bf16[8,7,2,2,16,128]{5,4,3,2,1,0:T(8,128)(2,1)S(1)}, bf16[8,7,2,2,16,128]{5,4,3,2,1,0:T(8,128)(2,1)S(1)}, u32[]{:S(2)}, u32[]{:S(2)}) collective-permute-start(bf16[8,7,2,2,16,128]{5,4,3,2,1,0:T(8,128)(2,1)S(1)} %get-tuple-element.40.refs_6_.refs_1_), channel_id=1, source_target_pairs={{2,0},{4,2},{6,4},{8,6},{10,8},{12,10},{14,12},{0,14},{66,64},{68,... | collective-permute-start | bytes 2752520 | tf_op jit(solution)/shard_map/ppermute | solution.py:304
  61.8 1.8 %collective-permute-start.8 = (bf16[2,7,2,2,16,128]{5,4,3,2,1,0:T(8,128)(2,1)S(1)}, bf16[2,7,2,2,16,128]{5,4,3,2,1,0:T(8,128)(2,1)S(1)}, u32[]{:S(2)}, u32[]{:S(2)}) collective-permute-start(bf16[2,7,2,2,16,128]{5,4,3,2,1,0:T(8,128)(2,1)S(1)} %get-tuple-element.36), channel_id=1, source_target_pairs={{64,0},{66,2},{68,4},{70,6},{72,8},{74,10},{76,12},{78,14},{128,64... | collective-permute-start | bytes 688136 | tf_op jit(solution)/shard_map/ppermute | solution.py:304
  63.6 2.5 %collective-permute-done.7 = bf16[2,7,2,2,16,128]{5,4,3,2,1,0:T(8,128)(2,1)S(1)} collective-permute-done((bf16[2,7,2,2,16,128]{5,4,3,2,1,0:T(8,128)(2,1)S(1)}, bf16[2,7,2,2,16,128]{5,4,3,2,1,0:T(8,128)(2,1)S(1)}, u32[]{:S(2)}, u32[]{:S(2)}) %collective-permute-start.7) | collective-permute-done | bytes 229408 | tf_op jit(solution)/shard_map/ppermute | solution.py:304
  66.1 1.9 %collective-permute-done.8 = bf16[2,7,2,2,16,128]{5,4,3,2,1,0:T(8,128)(2,1)S(1)} collective-permute-done((bf16[2,7,2,2,16,128]{5,4,3,2,1,0:T(8,128)(2,1)S(1)}, bf16[2,7,2,2,16,128]{5,4,3,2,1,0:T(8,128)(2,1)S(1)}, u32[]{:S(2)}, u32[]{:S(2)}) %collective-permute-start.8) | collective-permute-done | bytes 229408 | tf_op jit(solution)/shard_map/ppermute | solution.py:304
  68.1 0.1 gather_kv.1
  68.2 1.6 %collective-permute-start.11 = (bf16[2,6,2,2,16,128]{5,4,3,2,1,0:T(8,128)(2,1)S(1)}, bf16[2,6,2,2,16,128]{5,4,3,2,1,0:T(8,128)(2,1)S(1)}, u32[]{:S(2)}, u32[]{:S(2)}) collective-permute-start(bf16[2,6,2,2,16,128]{5,4,3,2,1,0:T(8,128)(2,1)S(1)} %get-tuple-element.38), channel_id=1, source_target_pairs={{192,0},{194,2},{196,4},{198,6},{200,8},{202,10},{204,12},{206,14}... | collective-permute-start | bytes 589832 | tf_op jit(solution)/shard_map/ppermute | solution.py:304
  69.8 0.0 collective-permute-start.24
  69.8 3.0 %collective-permute-start.25 = (bf16[4,7,2,2,16,128]{5,4,3,2,1,0:T(8,128)(2,1)S(1)}, bf16[4,7,2,2,16,128]{5,4,3,2,1,0:T(8,128)(2,1)S(1)}, u32[]{:S(2)}, u32[]{:S(2)}) collective-permute-start(bf16[4,7,2,2,16,128]{5,4,3,2,1,0:T(8,128)(2,1)S(1)} %constant_dynamic-update-slice_fusion.refs_8_.refs_4_), channel_id=1, source_target_pairs={{2,0},{4,2},{6,4},{8,6},{10,8},{12,10},{14,12},{0,14},{66,64},{68,... | collective-permute-start | bytes 1376264 | tf_op jit(solution)/shard_map/ppermute | solution.py:304
  72.7 2.4 %collective-permute-done.11 = bf16[2,6,2,2,16,128]{5,4,3,2,1,0:T(8,128)(2,1)S(1)} collective-permute-done((bf16[2,6,2,2,16,128]{5,4,3,2,1,0:T(8,128)(2,1)S(1)}, bf16[2,6,2,2,16,128]{5,4,3,2,1,0:T(8,128)(2,1)S(1)}, u32[]{:S(2)}, u32[]{:S(2)}) %collective-permute-start.11) | collective-permute-done | bytes 196640 | tf_op jit(solution)/shard_map/ppermute | solution.py:304
  75.2 1.7 %collective-permute-start.12 = (bf16[2,6,2,2,16,128]{5,4,3,2,1,0:T(8,128)(2,1)S(1)}, bf16[2,6,2,2,16,128]{5,4,3,2,1,0:T(8,128)(2,1)S(1)}, u32[]{:S(2)}, u32[]{:S(2)}) collective-permute-start(bf16[2,6,2,2,16,128]{5,4,3,2,1,0:T(8,128)(2,1)S(1)} %get-tuple-element.39), channel_id=1, source_target_pairs={{64,0},{66,2},{68,4},{70,6},{72,8},{74,10},{76,12},{78,14},{128,64... | collective-permute-start | bytes 589832 | tf_op jit(solution)/shard_map/ppermute | solution.py:304
  76.9 3.9 %collective-permute-done.12 = bf16[2,6,2,2,16,128]{5,4,3,2,1,0:T(8,128)(2,1)S(1)} collective-permute-done((bf16[2,6,2,2,16,128]{5,4,3,2,1,0:T(8,128)(2,1)S(1)}, bf16[2,6,2,2,16,128]{5,4,3,2,1,0:T(8,128)(2,1)S(1)}, u32[]{:S(2)}, u32[]{:S(2)}) %collective-permute-start.12) | collective-permute-done | bytes 196640 | tf_op jit(solution)/shard_map/ppermute | solution.py:304
  80.9 0.0 collective-permute-done.24.refs_3_
  80.9 0.5 collective-permute-start.9
  81.4 1.4 %collective-permute-start.13 = (bf16[4,6,2,2,16,128]{5,4,3,2,1,0:T(8,128)(2,1)S(1)}, bf16[4,6,2,2,16,128]{5,4,3,2,1,0:T(8,128)(2,1)S(1)}, u32[]{:S(2)}, u32[]{:S(2)}) collective-permute-start(bf16[4,6,2,2,16,128]{5,4,3,2,1,0:T(8,128)(2,1)S(1)} %constant_dynamic-update-slice_fusion.2.refs_4_.refs_7_), channel_id=1, source_target_pairs={{14,0},{0,2},{2,4},{4,6},{6,8},{8,10},{10,12},{12,14},{78,64},{64,... | collective-permute-start | bytes 1179656 | tf_op jit(solution)/shard_map/ppermute | solution.py:304
  82.8 0.0 collective-permute-done.22.refs_0_
  82.8 1.5 %collective-permute-start.14 = (bf16[4,6,2,2,16,128]{5,4,3,2,1,0:T(8,128)(2,1)S(1)}, bf16[4,6,2,2,16,128]{5,4,3,2,1,0:T(8,128)(2,1)}, u32[]{:S(2)}, u32[]{:S(2)}) collective-permute-start(bf16[4,6,2,2,16,128]{5,4,3,2,1,0:T(8,128)(2,1)S(1)} %constant_dynamic-update-slice_fusion.2.refs_4_.refs_7_), channel_id=1, source_target_pairs={{2,0},{4,2},{6,4},{8,6},{10,8},{12,10},{14,12},{0,14},{66,64},{68,... | collective-permute-start | bytes 1179656 | tf_op jit(solution)/shard_map/ppermute | solution.py:304
  84.4 0.0 collective-permute-done.23.refs_2_
  84.4 8.1 %key_grads.1 = bf16[8,6,2,2,16,128]{5,4,3,2,1,0:T(8,128)(2,1)} custom-call(bf16[8,7,2,2,16,128]{5,4,3,2,1,0:T(8,128)(2,1)S(1)} %collective-permute-done.22.refs_0_, bf16[8,7,2,2,16,128]{5,4,3,2,1,0:T(8,128)(2,1)S(1)} %get-tuple-element.40.refs_6_.refs_1_, bf16[8,7,2,2,16,128]{5,4,3,2,1,0:T(8,128)(2,1)S(1)} %collective-permute-done.23.refs_2_, ...), custom_call_target="tpu_custom_call" | custom-call | flops 10000000000 | bytes 1048576 | tf_op jit(solution)/shard_map/key_grads/pallas_call | solution.py:49
  92.5 3.9 %all-to-all-start = ((bf16[8,6,2,2,16,128]{5,4,3,2,1,0:T(8,128)(2,1)}), bf16[8,6,2,2,16,128]{5,4,3,2,1,0:T(8,128)(2,1)S(1)}, u32[]{:S(2)}, u32[]{:S(2)}) async-start(bf16[8,6,2,2,16,128]{5,4,3,2,1,0:T(8,128)(2,1)} %key_grads.1), calls=%async_computation | async-start | bytes 1572864 | tf_op jit(solution)/shard_map/all_to_all | solution.py:291
  96.4 1.4 %collective-permute-done.13.refs_3_ = bf16[4,6,2,2,16,128]{5,4,3,2,1,0:T(8,128)(2,1)S(1)} collective-permute-done((bf16[4,6,2,2,16,128]{5,4,3,2,1,0:T(8,128)(2,1)S(1)}, bf16[4,6,2,2,16,128]{5,4,3,2,1,0:T(8,128)(2,1)S(1)}, u32[]{:S(2)}, u32[]{:S(2)}) %collective-permute-start.13) | collective-permute-done | bytes 393248 | tf_op jit(solution)/shard_map/ppermute | solution.py:304
  97.7 0.0 collective-permute-done.14.refs_5_
  97.7 0.0 collective-permute-done.10.refs_2_
  97.8 0.0 collective-permute-done.9.refs_0_
  97.8 6.6 %query_grads.1 = (bf16[3,2,2,16,128]{4,3,2,1,0:T(8,128)(2,1)S(1)}, bf16[3,2,2,16,128]{4,3,2,1,0:T(8,128)(2,1)S(1)}, bf16[3,2,2,16,128]{4,3,2,1,0:T(8,128)(2,1)S(...) custom-call(bf16[8,6,2,2,16,128]{5,4,3,2,1,0:T(8,128)(2,1)} %collect, ...), custom_call_target="tpu_custom_call" | custom-call | flops 99999997952 | bytes 1048576 | tf_op jit(solution)/shard_map/query_grads/pallas_call | solution.py:49
  104.4 0.8 collective-permute-start.15
  105.2 3.1 %collective-permute-start.16 = (bf16[3,2,2,16,128]{4,3,2,1,0:T(8,128)(2,1)S(1)}, bf16[3,2,2,16,128]{4,3,2,1,0:T(8,128)(2,1)S(1)}, u32[]{:S(2)}, u32[]{:S(2)}) collective-permute-start(bf16[3,2,2,16,128]{4,3,2,1,0:T(8,128)(2,1)S(1)} %get-tuple-element.43), channel_id=1, source_target_pairs={{0,16},{1,17},{16,32},{17,33},{32,48},{33,49},{48,0},{49,1},{2,18}... | collective-permute-start | bytes 147464 | tf_op jit(solution)/shard_map/ppermute | solution.py:297
  108.3 0.6 collective-permute-start.17
  108.9 3.4 %collective-permute-start.18 = (bf16[3,2,2,16,128]{4,3,2,1,0:T(8,128)(2,1)S(1)}, bf16[3,2,2,16,128]{4,3,2,1,0:T(8,128)(2,1)S(1)}, u32[]{:S(2)}, u32[]{:S(2)}) collective-permute-start(bf16[3,2,2,16,128]{4,3,2,1,0:T(8,128)(2,1)S(1)} %get-tuple-element.45), channel_id=1, source_target_pairs={{0,32},{1,33},{16,48},{17,49},{32,0},{33,1},{48,16},{49,17},{2,34}... | collective-permute-start | bytes 147464 | tf_op jit(solution)/shard_map/ppermute | solution.py:297
  112.3 1.2 collective-permute-start.19
  113.4 2.7 %collective-permute-done.15.refs_1_ = bf16[3,2,2,16,128]{4,3,2,1,0:T(8,128)(2,1)S(1)} collective-permute-done((bf16[3,2,2,16,128]{4,3,2,1,0:T(8,128)(2,1)S(1)}, bf16[3,2,2,16,128]{4,3,2,1,0:T(8,128)(2,1)S(1)}, u32[]{:S(2)}, u32[]{:S(2)}) %collective-permute-start.15) | collective-permute-done | bytes 49184 | tf_op jit(solution)/shard_map/ppermute | solution.py:297
  116.1 4.7 %collective-permute-start.20 = (bf16[3,2,2,16,128]{4,3,2,1,0:T(8,128)(2,1)S(1)}, bf16[3,2,2,16,128]{4,3,2,1,0:T(8,128)(2,1)S(1)}, u32[]{:S(2)}, u32[]{:S(2)}) collective-permute-start(bf16[3,2,2,16,128]{4,3,2,1,0:T(8,128)(2,1)S(1)} %get-tuple-element.47), channel_id=1, source_target_pairs={{0,48},{1,49},{16,0},{17,1},{32,16},{33,17},{48,32},{49,33},{2,50}... | collective-permute-start | bytes 147464 | tf_op jit(solution)/shard_map/ppermute | solution.py:297
  120.8 1.3 collective-permute-start.21
  122.0 0.2 collective-permute-done.17.refs_3_
  122.2 0.0 collective-permute-done.18.refs_4_
  122.2 0.2 collective-permute-done.19.refs_5_
  122.5 0.7 collective-permute-done.20.refs_6_
  123.1 1.7 %collective-permute-done.21.refs_7_ = bf16[3,2,2,16,128]{4,3,2,1,0:T(8,128)(2,1)S(1)} collective-permute-done((bf16[3,2,2,16,128]{4,3,2,1,0:T(8,128)(2,1)S(1)}, bf16[3,2,2,16,128]{4,3,2,1,0:T(8,128)(2,1)S(1)}, u32[]{:S(2)}, u32[]{:S(2)}) %collective-permute-start.21) | collective-permute-done | bytes 49184 | tf_op jit(solution)/shard_map/ppermute | solution.py:297
  124.9 0.8 unpack_q.1
  125.7 0.0 all-to-all-done.refs_0_
  125.7 1.0 unpack_kv.1
  (13 shorter events, 0.1 us)
Async XLA Ops:
  1.5 1.0 copy-start
  2.5 1.0 copy-start.1
  3.5 1.0 copy-start.2
  4.5 1.0 copy-start.3
  5.5 1.0 copy-start.4
  7.3 13.0 %collective-permute-start = (bf16[13,2,2,16,128]{4,3,2,1,0:T(8,128)(2,1)S(1)}, bf16[13,2,2,16,128]{4,3,2,1,0:T(8,128)(2,1)S(1)}, u32[]{:S(2)}, u32[]{:S(2)}) collective-permute-start(bf16[13,2,2,16,128]{4,3,2,1,0:T(8,128)(2,1)S(1)} %get-tuple-element.28), channel_id=1, source_target_pairs={{0,1},{1,16},{16,17},{17,32},{32,33},{33,48},{48,49},{49,0},{2,3},... | collective-permute-start | bytes 638984 | tf_op jit(solution)/shard_map/ppermute | solution.py:297
  9.3 20.3 %collective-permute-start.1 = (bf16[13,2,2,16,128]{4,3,2,1,0:T(8,128)(2,1)S(1)}, bf16[13,2,2,16,128]{4,3,2,1,0:T(8,128)(2,1)S(1)}, u32[]{:S(2)}, u32[]{:S(2)}) collective-permute-start(bf16[13,2,2,16,128]{4,3,2,1,0:T(8,128)(2,1)S(1)} %get-tuple-element.29), channel_id=1, source_target_pairs={{0,16},{1,17},{16,32},{17,33},{32,48},{33,49},{48,0},{49,1},{2,18}... | collective-permute-start | bytes 638984 | tf_op jit(solution)/shard_map/ppermute | solution.py:297
  13.8 34.0 %collective-permute-start.2 = (bf16[13,2,2,16,128]{4,3,2,1,0:T(8,128)(2,1)S(1)}, bf16[13,2,2,16,128]{4,3,2,1,0:T(8,128)(2,1)S(1)}, u32[]{:S(2)}, u32[]{:S(2)}) collective-permute-start(bf16[13,2,2,16,128]{4,3,2,1,0:T(8,128)(2,1)S(1)} %get-tuple-element.30), channel_id=1, source_target_pairs={{0,17},{1,32},{16,33},{17,48},{32,49},{33,0},{48,1},{49,16},{2,19}... | collective-permute-start | bytes 638984 | tf_op jit(solution)/shard_map/ppermute | solution.py:297
  15.7 32.0 %collective-permute-start.3 = (bf16[13,2,2,16,128]{4,3,2,1,0:T(8,128)(2,1)S(1)}, bf16[13,2,2,16,128]{4,3,2,1,0:T(8,128)(2,1)S(1)}, u32[]{:S(2)}, u32[]{:S(2)}) collective-permute-start(bf16[13,2,2,16,128]{4,3,2,1,0:T(8,128)(2,1)S(1)} %get-tuple-element.31), channel_id=1, source_target_pairs={{0,32},{1,33},{16,48},{17,49},{32,0},{33,1},{48,16},{49,17},{2,34}... | collective-permute-start | bytes 638984 | tf_op jit(solution)/shard_map/ppermute | solution.py:297
  17.2 30.6 %collective-permute-start.4 = (bf16[13,2,2,16,128]{4,3,2,1,0:T(8,128)(2,1)S(1)}, bf16[13,2,2,16,128]{4,3,2,1,0:T(8,128)(2,1)S(1)}, u32[]{:S(2)}, u32[]{:S(2)}) collective-permute-start(bf16[13,2,2,16,128]{4,3,2,1,0:T(8,128)(2,1)S(1)} %get-tuple-element.32), channel_id=1, source_target_pairs={{0,33},{1,48},{16,49},{17,0},{32,1},{33,16},{48,17},{49,32},{2,35}... | collective-permute-start | bytes 638984 | tf_op jit(solution)/shard_map/ppermute | solution.py:297
  20.3 33.9 %collective-permute-start.5 = (bf16[13,2,2,16,128]{4,3,2,1,0:T(8,128)(2,1)S(1)}, bf16[13,2,2,16,128]{4,3,2,1,0:T(8,128)(2,1)S(1)}, u32[]{:S(2)}, u32[]{:S(2)}) collective-permute-start(bf16[13,2,2,16,128]{4,3,2,1,0:T(8,128)(2,1)S(1)} %get-tuple-element.33), channel_id=1, source_target_pairs={{0,48},{1,49},{16,0},{17,1},{32,16},{33,17},{48,32},{49,33},{2,50}... | collective-permute-start | bytes 638984 | tf_op jit(solution)/shard_map/ppermute | solution.py:297
  29.6 27.3 %collective-permute-start.6 = (bf16[13,2,2,16,128]{4,3,2,1,0:T(8,128)(2,1)S(1)}, bf16[13,2,2,16,128]{4,3,2,1,0:T(8,128)(2,1)S(1)}, u32[]{:S(2)}, u32[]{:S(2)}) collective-permute-start(bf16[13,2,2,16,128]{4,3,2,1,0:T(8,128)(2,1)S(1)} %get-tuple-element.34), channel_id=1, source_target_pairs={{0,49},{1,0},{16,1},{17,16},{32,17},{33,32},{48,33},{49,48},{2,51}... | collective-permute-start | bytes 638984 | tf_op jit(solution)/shard_map/ppermute | solution.py:297
  57.3 8.8 %collective-permute-start.7 = (bf16[2,7,2,2,16,128]{5,4,3,2,1,0:T(8,128)(2,1)S(1)}, bf16[2,7,2,2,16,128]{5,4,3,2,1,0:T(8,128)(2,1)S(1)}, u32[]{:S(2)}, u32[]{:S(2)}) collective-permute-start(bf16[2,7,2,2,16,128]{5,4,3,2,1,0:T(8,128)(2,1)S(1)} %get-tuple-element.35), channel_id=1, source_target_pairs={{192,0},{194,2},{196,4},{198,6},{200,8},{202,10},{204,12},{206,14}... | collective-permute-start | bytes 688136 | tf_op jit(solution)/shard_map/ppermute | solution.py:304
  58.9 24.0 %collective-permute-start.22 = (bf16[8,7,2,2,16,128]{5,4,3,2,1,0:T(8,128)(2,1)S(1)}, bf16[8,7,2,2,16,128]{5,4,3,2,1,0:T(8,128)(2,1)S(1)}, u32[]{:S(2)}, u32[]{:S(2)}) collective-permute-start(bf16[8,7,2,2,16,128]{5,4,3,2,1,0:T(8,128)(2,1)S(1)} %get-tuple-element.40.refs_6_.refs_1_), channel_id=1, source_target_pairs={{14,0},{0,2},{2,4},{4,6},{6,8},{8,10},{10,12},{12,14},{78,64},{64,... | collective-permute-start | bytes 2752520 | tf_op jit(solution)/shard_map/ppermute | solution.py:304
  58.9 25.5 %collective-permute-start.23 = (bf16[8,7,2,2,16,128]{5,4,3,2,1,0:T(8,128)(2,1)S(1)}, bf16[8,7,2,2,16,128]{5,4,3,2,1,0:T(8,128)(2,1)S(1)}, u32[]{:S(2)}, u32[]{:S(2)}) collective-permute-start(bf16[8,7,2,2,16,128]{5,4,3,2,1,0:T(8,128)(2,1)S(1)} %get-tuple-element.40.refs_6_.refs_1_), channel_id=1, source_target_pairs={{2,0},{4,2},{6,4},{8,6},{10,8},{12,10},{14,12},{0,14},{66,64},{68,... | collective-permute-start | bytes 2752520 | tf_op jit(solution)/shard_map/ppermute | solution.py:304
  61.8 6.2 %collective-permute-start.8 = (bf16[2,7,2,2,16,128]{5,4,3,2,1,0:T(8,128)(2,1)S(1)}, bf16[2,7,2,2,16,128]{5,4,3,2,1,0:T(8,128)(2,1)S(1)}, u32[]{:S(2)}, u32[]{:S(2)}) collective-permute-start(bf16[2,7,2,2,16,128]{5,4,3,2,1,0:T(8,128)(2,1)S(1)} %get-tuple-element.36), channel_id=1, source_target_pairs={{64,0},{66,2},{68,4},{70,6},{72,8},{74,10},{76,12},{78,14},{128,64... | collective-permute-start | bytes 688136 | tf_op jit(solution)/shard_map/ppermute | solution.py:304
  68.2 7.0 %collective-permute-start.11 = (bf16[2,6,2,2,16,128]{5,4,3,2,1,0:T(8,128)(2,1)S(1)}, bf16[2,6,2,2,16,128]{5,4,3,2,1,0:T(8,128)(2,1)S(1)}, u32[]{:S(2)}, u32[]{:S(2)}) collective-permute-start(bf16[2,6,2,2,16,128]{5,4,3,2,1,0:T(8,128)(2,1)S(1)} %get-tuple-element.38), channel_id=1, source_target_pairs={{192,0},{194,2},{196,4},{198,6},{200,8},{202,10},{204,12},{206,14}... | collective-permute-start | bytes 589832 | tf_op jit(solution)/shard_map/ppermute | solution.py:304
  69.8 11.1 %collective-permute-start.24 = (bf16[4,7,2,2,16,128]{5,4,3,2,1,0:T(8,128)(2,1)S(1)}, bf16[4,7,2,2,16,128]{5,4,3,2,1,0:T(8,128)(2,1)S(1)}, u32[]{:S(2)}, u32[]{:S(2)}) collective-permute-start(bf16[4,7,2,2,16,128]{5,4,3,2,1,0:T(8,128)(2,1)S(1)} %constant_dynamic-update-slice_fusion.refs_8_.refs_4_), channel_id=1, source_target_pairs={{14,0},{0,2},{2,4},{4,6},{6,8},{8,10},{10,12},{12,14},{78,64},{64,... | collective-permute-start | bytes 1376264 | tf_op jit(solution)/shard_map/ppermute | solution.py:304
  69.8 11.6 %collective-permute-start.25 = (bf16[4,7,2,2,16,128]{5,4,3,2,1,0:T(8,128)(2,1)S(1)}, bf16[4,7,2,2,16,128]{5,4,3,2,1,0:T(8,128)(2,1)S(1)}, u32[]{:S(2)}, u32[]{:S(2)}) collective-permute-start(bf16[4,7,2,2,16,128]{5,4,3,2,1,0:T(8,128)(2,1)S(1)} %constant_dynamic-update-slice_fusion.refs_8_.refs_4_), channel_id=1, source_target_pairs={{2,0},{4,2},{6,4},{8,6},{10,8},{12,10},{14,12},{0,14},{66,64},{68,... | collective-permute-start | bytes 1376264 | tf_op jit(solution)/shard_map/ppermute | solution.py:304
  75.2 5.7 %collective-permute-start.12 = (bf16[2,6,2,2,16,128]{5,4,3,2,1,0:T(8,128)(2,1)S(1)}, bf16[2,6,2,2,16,128]{5,4,3,2,1,0:T(8,128)(2,1)S(1)}, u32[]{:S(2)}, u32[]{:S(2)}) collective-permute-start(bf16[2,6,2,2,16,128]{5,4,3,2,1,0:T(8,128)(2,1)S(1)} %get-tuple-element.39), channel_id=1, source_target_pairs={{64,0},{66,2},{68,4},{70,6},{72,8},{74,10},{76,12},{78,14},{128,64... | collective-permute-start | bytes 589832 | tf_op jit(solution)/shard_map/ppermute | solution.py:304
  80.8 16.9 %collective-permute-start.10 = (bf16[8,6,2,2,16,128]{5,4,3,2,1,0:T(8,128)(2,1)S(1)}, bf16[8,6,2,2,16,128]{5,4,3,2,1,0:T(8,128)(2,1)}, u32[]{:S(2)}, u32[]{:S(2)}) collective-permute-start(bf16[8,6,2,2,16,128]{5,4,3,2,1,0:T(8,128)(2,1)S(1)} %get-tuple-element.37.refs_1_.refs_6_), channel_id=1, source_target_pairs={{2,0},{4,2},{6,4},{8,6},{10,8},{12,10},{14,12},{0,14},{66,64},{68,... | collective-permute-start | bytes 2359304 | tf_op jit(solution)/shard_map/ppermute | solution.py:304
  80.9 16.9 %collective-permute-start.9 = (bf16[8,6,2,2,16,128]{5,4,3,2,1,0:T(8,128)(2,1)S(1)}, bf16[8,6,2,2,16,128]{5,4,3,2,1,0:T(8,128)(2,1)}, u32[]{:S(2)}, u32[]{:S(2)}) collective-permute-start(bf16[8,6,2,2,16,128]{5,4,3,2,1,0:T(8,128)(2,1)S(1)} %get-tuple-element.37.refs_1_.refs_6_), channel_id=1, source_target_pairs={{14,0},{0,2},{2,4},{4,6},{6,8},{8,10},{10,12},{12,14},{78,64},{64,... | collective-permute-start | bytes 2359304 | tf_op jit(solution)/shard_map/ppermute | solution.py:304
  81.4 16.3 %collective-permute-start.13 = (bf16[4,6,2,2,16,128]{5,4,3,2,1,0:T(8,128)(2,1)S(1)}, bf16[4,6,2,2,16,128]{5,4,3,2,1,0:T(8,128)(2,1)S(1)}, u32[]{:S(2)}, u32[]{:S(2)}) collective-permute-start(bf16[4,6,2,2,16,128]{5,4,3,2,1,0:T(8,128)(2,1)S(1)} %constant_dynamic-update-slice_fusion.2.refs_4_.refs_7_), channel_id=1, source_target_pairs={{14,0},{0,2},{2,4},{4,6},{6,8},{8,10},{10,12},{12,14},{78,64},{64,... | collective-permute-start | bytes 1179656 | tf_op jit(solution)/shard_map/ppermute | solution.py:304
  82.8 14.9 %collective-permute-start.14 = (bf16[4,6,2,2,16,128]{5,4,3,2,1,0:T(8,128)(2,1)S(1)}, bf16[4,6,2,2,16,128]{5,4,3,2,1,0:T(8,128)(2,1)}, u32[]{:S(2)}, u32[]{:S(2)}) collective-permute-start(bf16[4,6,2,2,16,128]{5,4,3,2,1,0:T(8,128)(2,1)S(1)} %constant_dynamic-update-slice_fusion.2.refs_4_.refs_7_), channel_id=1, source_target_pairs={{2,0},{4,2},{6,4},{8,6},{10,8},{12,10},{14,12},{0,14},{66,64},{68,... | collective-permute-start | bytes 1179656 | tf_op jit(solution)/shard_map/ppermute | solution.py:304
  92.5 33.2 %all-to-all-start = ((bf16[8,6,2,2,16,128]{5,4,3,2,1,0:T(8,128)(2,1)}), bf16[8,6,2,2,16,128]{5,4,3,2,1,0:T(8,128)(2,1)S(1)}, u32[]{:S(2)}, u32[]{:S(2)}) async-start(bf16[8,6,2,2,16,128]{5,4,3,2,1,0:T(8,128)(2,1)} %key_grads.1), calls=%async_computation | async-start | bytes 1572864 | tf_op jit(solution)/shard_map/all_to_all | solution.py:291
  104.4 11.7 %collective-permute-start.15 = (bf16[3,2,2,16,128]{4,3,2,1,0:T(8,128)(2,1)S(1)}, bf16[3,2,2,16,128]{4,3,2,1,0:T(8,128)(2,1)S(1)}, u32[]{:S(2)}, u32[]{:S(2)}) collective-permute-start(bf16[3,2,2,16,128]{4,3,2,1,0:T(8,128)(2,1)S(1)} %get-tuple-element.42), channel_id=1, source_target_pairs={{0,1},{1,16},{16,17},{17,32},{32,33},{33,48},{48,49},{49,0},{2,3},... | collective-permute-start | bytes 147464 | tf_op jit(solution)/shard_map/ppermute | solution.py:297
  105.2 15.6 %collective-permute-start.16 = (bf16[3,2,2,16,128]{4,3,2,1,0:T(8,128)(2,1)S(1)}, bf16[3,2,2,16,128]{4,3,2,1,0:T(8,128)(2,1)S(1)}, u32[]{:S(2)}, u32[]{:S(2)}) collective-permute-start(bf16[3,2,2,16,128]{4,3,2,1,0:T(8,128)(2,1)S(1)} %get-tuple-element.43), channel_id=1, source_target_pairs={{0,16},{1,17},{16,32},{17,33},{32,48},{33,49},{48,0},{49,1},{2,18}... | collective-permute-start | bytes 147464 | tf_op jit(solution)/shard_map/ppermute | solution.py:297
  108.3 13.9 %collective-permute-start.17 = (bf16[3,2,2,16,128]{4,3,2,1,0:T(8,128)(2,1)S(1)}, bf16[3,2,2,16,128]{4,3,2,1,0:T(8,128)(2,1)S(1)}, u32[]{:S(2)}, u32[]{:S(2)}) collective-permute-start(bf16[3,2,2,16,128]{4,3,2,1,0:T(8,128)(2,1)S(1)} %get-tuple-element.44), channel_id=1, source_target_pairs={{0,17},{1,32},{16,33},{17,48},{32,49},{33,0},{48,1},{49,16},{2,19}... | collective-permute-start | bytes 147464 | tf_op jit(solution)/shard_map/ppermute | solution.py:297
  108.9 13.4 %collective-permute-start.18 = (bf16[3,2,2,16,128]{4,3,2,1,0:T(8,128)(2,1)S(1)}, bf16[3,2,2,16,128]{4,3,2,1,0:T(8,128)(2,1)S(1)}, u32[]{:S(2)}, u32[]{:S(2)}) collective-permute-start(bf16[3,2,2,16,128]{4,3,2,1,0:T(8,128)(2,1)S(1)} %get-tuple-element.45), channel_id=1, source_target_pairs={{0,32},{1,33},{16,48},{17,49},{32,0},{33,1},{48,16},{49,17},{2,34}... | collective-permute-start | bytes 147464 | tf_op jit(solution)/shard_map/ppermute | solution.py:297
  112.3 10.2 %collective-permute-start.19 = (bf16[3,2,2,16,128]{4,3,2,1,0:T(8,128)(2,1)S(1)}, bf16[3,2,2,16,128]{4,3,2,1,0:T(8,128)(2,1)S(1)}, u32[]{:S(2)}, u32[]{:S(2)}) collective-permute-start(bf16[3,2,2,16,128]{4,3,2,1,0:T(8,128)(2,1)S(1)} %get-tuple-element.46), channel_id=1, source_target_pairs={{0,33},{1,48},{16,49},{17,0},{32,1},{33,16},{48,17},{49,32},{2,35}... | collective-permute-start | bytes 147464 | tf_op jit(solution)/shard_map/ppermute | solution.py:297
  116.1 7.1 %collective-permute-start.20 = (bf16[3,2,2,16,128]{4,3,2,1,0:T(8,128)(2,1)S(1)}, bf16[3,2,2,16,128]{4,3,2,1,0:T(8,128)(2,1)S(1)}, u32[]{:S(2)}, u32[]{:S(2)}) collective-permute-start(bf16[3,2,2,16,128]{4,3,2,1,0:T(8,128)(2,1)S(1)} %get-tuple-element.47), channel_id=1, source_target_pairs={{0,48},{1,49},{16,0},{17,1},{32,16},{33,17},{48,32},{49,33},{2,50}... | collective-permute-start | bytes 147464 | tf_op jit(solution)/shard_map/ppermute | solution.py:297
  120.8 4.1 %collective-permute-start.21 = (bf16[3,2,2,16,128]{4,3,2,1,0:T(8,128)(2,1)S(1)}, bf16[3,2,2,16,128]{4,3,2,1,0:T(8,128)(2,1)S(1)}, u32[]{:S(2)}, u32[]{:S(2)}) collective-permute-start(bf16[3,2,2,16,128]{4,3,2,1,0:T(8,128)(2,1)S(1)} %get-tuple-element.48), channel_id=1, source_target_pairs={{0,49},{1,0},{16,1},{17,16},{32,17},{33,32},{48,33},{49,48},{2,51}... | collective-permute-start | bytes 147464 | tf_op jit(solution)/shard_map/ppermute | solution.py:297

commit v2 on v1

--- a/solution.py
+++ b/solution.py
@@ -24,7 +24,7 @@
 SCALE = 1.0 / math.sqrt(HD)
 LOG2E = math.log2(math.e)
 DOT0, LSE0, LSE1, FR0, RW0 = 0, 16, 80, 32, 48
-VMEM = 28 * 1024 * 1024
+VMEM = 20 * 1024 * 1024
 SPAN = 2
 BF, F32 = jnp.bfloat16, jnp.float32
 
@@ -76,8 +76,21 @@
     return pl.ds(pl.multiple_of(head_of(dest, h) * HD, HD), HD)
 
 
-def pack(q_ref, do_ref, o_ref, k_ref, v_ref, lse_ref, *out_refs):
-    parts = three(lse_ref[...] * math.sqrt(HD))
+def load(in_refs, bufs, sems):
+    copies = [pltpu.make_async_copy(ref, buf, sems.at[i]) for i, (ref, buf) in enumerate(zip(in_refs, bufs))]
+    for copy in copies:
+        copy.start()
+    for copy in copies:
+        copy.wait()
+
+
+def pack_q(*refs):
+    out_refs, bufs = refs[4 : 4 + Z], refs[4 + Z : 8 + Z]
+    load(refs[:4], bufs, refs[8 + Z])
+    q_ref, do_ref, o_ref, lse_ref = bufs
+    log_sums = jnp.concatenate([lse_ref[:, f, r] for f in range(F) for r in range(R)], axis=1)
+    log_sums = jnp.concatenate([log_sums, jnp.zeros((4, 128), F32)], axis=0)
+    parts = three(log_sums * math.sqrt(HD))
     row = lax.broadcasted_iota(jnp.int32, (128, 16), 0)
     col = lax.broadcasted_iota(jnp.int32, (128, 16), 1)
     spread = jnp.zeros((128, 128), F32)
@@ -99,8 +112,6 @@
             g = do_ref[:, :, :, at]
             out_ref[2 * h] = q_ref[:, :, :, at]
             out_ref[2 * h + 1] = g
-            out_ref[2 * HL + 1 + 2 * h] = k_ref[:, :, :, at]
-            out_ref[2 * HL + 2 + 2 * h] = v_ref[:, :, :, at]
             dot = jnp.sum((g.astype(F32) * o_ref[:, :, :, at].astype(F32)).reshape(N, HD), axis=-1, keepdims=True)
             for p, part in enumerate(three(dot)):
                 side = jnp.where(lane == DOT0 + 3 * h + p, part, side)
@@ -108,10 +119,20 @@
         out_ref[2 * HL] = jnp.where(keep, lse, side).astype(BF).reshape(F, R, CH, 128)
 
 
+def pack_kv(*refs):
+    out_ref, bufs = refs[2], refs[3:5]
+    load(refs[:2], bufs, refs[5])
+    for dest in range(Z):
+        for h in range(HL):
+            at = slice(head_of(dest, h) * HD, head_of(dest, h) * HD + HD)
+            out_ref[dest, 2 * h] = bufs[0][:, :, :, at]
+            out_ref[dest, 2 * h + 1] = bufs[1][:, :, :, at]
+
+
 def gather_q(*refs):
     in_refs, (out_ref, lo_ref, hi_ref) = refs[:Z], refs[Z:]
-    for k, in_ref in enumerate(in_refs):
-        out_ref[lax.rem(ring_place() + Z - k, Z)] = in_ref[: 2 * HL + 1]
+    for k, in_ref in zip((0,) + FAR, in_refs):
+        out_ref[lax.rem(ring_place() + Z - k, Z)] = in_ref[...]
     mine = lax.axis_index("zl")
     lane = lanes(N, 128)
     for zh in range(ZH):
@@ -125,12 +146,9 @@
     hi_ref[...] = out_ref[Z - ZL :]
 
 
-def gather_kv(*refs):
-    in_refs, (out_ref, lo_ref, hi_ref) = refs[:Z], refs[Z:]
-    for k, in_ref in enumerate(in_refs):
-        out_ref[lax.rem(ring_place() + Z - k, Z)] = in_ref[2 * HL + 1 :]
-    lo_ref[...] = out_ref[:ZL]
-    hi_ref[...] = out_ref[Z - ZL :]
+def ends(in_ref, lo_ref, hi_ref):
+    lo_ref[...] = in_ref[:ZL]
+    hi_ref[...] = in_ref[Z - ZL :]
 
 
 def bad_frames(e, frame):
@@ -171,31 +189,10 @@
     return lax.dot_general(a, b, (((1,), (1,)), ((), ())), preferred_element_type=F32)
 
 
-def fetch(in_refs, bufs, sems):
-    copies = {}
-    for h in [HL] + list(range(HL)):
-        for i, (ref, buf) in enumerate(zip(in_refs, bufs)):
-            size = 2 if h < HL else 1
-            if 2 * h < buf.shape[1]:
-                at = pl.ds(2 * h, size)
-                copies[h, i] = pltpu.make_async_copy(ref.at[:, at], buf.at[:, at], sems.at[h, i])
-                copies[h, i].start()
-
-    def ready(h):
-        for (at, _), copy in copies.items():
-            if at == h:
-                copy.wait()
-
-    return ready
-
-
 def key_grads(*refs):
-    in_refs, out_ref, bufs, sems = refs[:7], refs[7], refs[8:15], refs[15]
-    ready = fetch(in_refs, bufs, sems)
-    parts, kv = list(zip(bufs[:3], bufs[3:6])), bufs[6]
+    parts, kv, out_ref = list(zip(refs[:3], refs[3:6])), refs[6], refs[7]
     n, m = SPAN * ZL * N, (SPAN + 2) * ZL * N
     lane = lanes(m, 128)
-    ready(HL)
     shifts = {}
     for group in range(0, ZH, SPAN):
         dims = (32, 128)
@@ -217,7 +214,6 @@
             side = jnp.where(lane < 32, seen(own, sides, group, 2 * HL).astype(F32), ones).astype(BF)
             shifts[group, i] = nt(marks, side)
     for h in range(HL):
-        ready(h)
         for group in range(0, ZH, SPAN):
             here = slice(ZL * group, ZL * (group + SPAN))
             k = kv[here, 2 * h].reshape(n, HD)
@@ -236,9 +232,7 @@
 
 
 def query_grads(*refs):
-    in_refs, out_refs, all_ref, bufs, sems = refs[:7], refs[7 : 7 + Z], refs[7 + Z], refs[8 + Z : 15 + Z], refs[15 + Z]
-    ready = fetch(in_refs, bufs, sems)
-    parts, qg = list(zip(bufs[:3], bufs[3:6])), bufs[6]
+    parts, qg, out_refs, all_ref = list(zip(refs[:3], refs[3:6])), refs[6], refs[7 : 7 + Z], refs[7 + Z]
     n, m = SPAN * ZL * N, (SPAN + 2) * ZL * N
     lane = lanes(n, 128)
     masks = {}
@@ -248,9 +242,7 @@
             frame, far_row = far_place(i, group, (8, m), 1)
             bad = bad_frames(frame, 2 + F * group + row // R) | bad_rows(far_row, 2 + row % R)
             masks[group, i] = jnp.where(bad, BIG, 0.0)
-    ready(HL)
     for h in range(HL):
-        ready(h)
         for group in range(0, ZH, SPAN):
             here = slice(ZL * group, ZL * (group + SPAN))
             q = qg[here, 2 * h].reshape(n, HD)
@@ -281,7 +273,7 @@
 
 def unpack_q(*refs):
     out_ref = refs[-1]
-    for k, in_ref in enumerate(refs[:-1]):
+    for k, in_ref in zip((0,) + FAR, refs[:-1]):
         src = lax.rem(ring_place() + Z - k, Z)
         for h in range(HL):
             out_ref[:, :, :, head_lanes(src, h)] = in_ref[h]
@@ -292,10 +284,7 @@
 
 
 def exchange_by_steps(sends):
-    got = list(sends)
-    for k in FAR:
-        got[k] = lax.ppermute(sends[k], RING, [(i, (i + k) % Z) for i in range(Z)])
-    return got
+    return [sends[0]] + [lax.ppermute(sends[k], RING, [(i, (i + k) % Z) for i in range(Z)]) for k in FAR]
 
 
 def shift(block, dx, dr):
@@ -304,42 +293,41 @@
     return lax.ppermute(block, ("x", "row"), [(flat(x + dx, r + dr), flat(x, r)) for x, r in places])
 
 
-def halo(own, lo, hi):
+def join(a_ref, b_ref, out_ref):
+    out_ref[:ZL] = a_ref[...]
+    out_ref[ZL:] = b_ref[...]
+
+
+def halo(own, lo, hi, name, fill=None):
     rows = [shift(own, 0, -1), own, shift(own, 0, 1)]
-    sides = jnp.concatenate([shift(hi, -1, 0), shift(lo, 1, 0)], axis=0)
-    return rows + [shift(sides, 0, -1), sides, shift(sides, 0, 1)]
-
-
-def staged(blocks, last):
-    whole = [pltpu.VMEM((n, blocks, F, R, CH, HD), BF) for n in (Z, Z, Z, 2 * ZL, 2 * ZL, 2 * ZL)]
-    return whole + [pltpu.VMEM((Z, last, F, R, CH, HD), BF), pltpu.SemaphoreType.DMA((HL + 1, 7))]
+    before, after = shift(hi, -1, 0), shift(lo, 1, 0)
+    filler = (fill(),) if fill else ()
+    sides = call(join, shape(2 * ZL, *own.shape[1:]), 2, name, after=filler)(before, after)
+    return rows + [shift(sides, 0, -1), sides, shift(sides, 0, 1)], filler
 
 
 def body(queries, key_tokens, values, outputs, grad_out, log_sums):
-    lse = jnp.pad(log_sums.reshape(HEADS // ZL, F * R * CH * ZL), ((0, 4), (0, 0)))
     q_block, kv_block, dq_block = (shape(b, F, R, CH, HD) for b in (2 * HL + 1, 2 * HL, HL))
     wide = lambda block, n: shape(n, *block.shape)
-    both = shape(4 * HL + 1, F, R, CH, HD)
-    sent = call(pack, (both,) * Z, 6, "pack")(queries, grad_out, outputs, key_tokens, values, lse)
-    got = exchange_by_steps(sent)
+    whole = shape(F, R, CH, HEADS * HD)
+    room = lambda *shapes: [pltpu.VMEM(x.shape, x.dtype) for x in shapes] + [pltpu.SemaphoreType.DMA((len(shapes),))]
+    sent_q = call(pack_q, (q_block,) * Z, 4, "pack_q", scratch=room(whole, whole, whole, log_sums), where=pl.ANY)(
+        queries, grad_out, outputs, log_sums
+    )
+    q_got = exchange_by_steps(sent_q)
+    sent_kv = call(
+        pack_kv, wide(kv_block, Z), 2, "pack_kv", scratch=room(whole, whole), where=pl.ANY, after=q_got[1:]
+    )(key_tokens, values)
+    kv_here = exchange(sent_kv)
     q_here, q_lo, q_hi = call(
         gather_q, (wide(q_block, Z), wide(q_block, ZL), wide(q_block, ZL)), Z, "gather_q"
-    )(*got)
-    q_seen = halo(q_here, q_lo, q_hi)
-    kv_here, kv_lo, kv_hi = call(
-        gather_kv, (wide(kv_block, Z), wide(kv_block, ZL), wide(kv_block, ZL)), Z, "gather_kv", after=q_seen[4:5]
-    )(*got)
-    kv_seen = halo(kv_here, kv_lo, kv_hi)
-    grads_kv = call(
-        key_grads,
-        wide(kv_block, Z),
-        7,
-        "key_grads",
-        flops=10**10,
-        scratch=staged(2 * HL + 1, 2 * HL),
-        where=pl.ANY,
-        after=kv_seen[4:5],
-    )(*q_seen, kv_here)
+    )(*q_got)
+    q_seen, _ = halo(q_here, q_lo, q_hi, "join_q")
+    kv_lo, kv_hi = call(
+        ends, (wide(kv_block, ZL),) * 2, 1, "ends", after=(q_seen[0], q_seen[2], q_seen[3], q_seen[5])
+    )(kv_here)
+    keys = lambda: call(key_grads, wide(kv_block, Z), 7, "key_grads", flops=10**10)(*q_seen, kv_here)
+    kv_seen, (grads_kv,) = halo(kv_here, kv_lo, kv_hi, "join_kv", keys)
     kv_back = exchange(grads_kv)
     grads_q = call(
         query_grads,
@@ -347,11 +335,9 @@
         7,
         "query_grads",
         flops=10**11,
-        scratch=[pltpu.VMEM((Z, HL, F, R, CH, HD), BF)] + staged(2 * HL, 2 * HL + 1),
-        where=pl.ANY,
+        scratch=[pltpu.VMEM((Z, HL, F, R, CH, HD), BF)],
     )(*kv_seen, q_here)
     q_back = exchange_by_steps(grads_q)
-    whole = shape(F, R, CH, HEADS * HD)
     key_out, value_out = call(unpack_kv, (whole, whole), 1, "unpack_kv")(kv_back)
     query_out = call(unpack_q, whole, Z, "unpack_q")(*q_back)
     return query_out, key_out, value_out

time: 129 us -> 117 us (0.907); the launches traced: 127 us -> 116 us
  waiting for transfers between devices: 49.9 us -> 26.2 us
  starting transfers between devices: 52.3 us -> 66.9 us
  local copies, waits for them, and re-layouts: 5.89 us -> 4.55 us
    ppermute x14, waiting for transfers between devices: 37.6 us -> 13.8 us  [exchange_by_steps(): lax.ppermute(sends[k], RING, [(i, (i + k) % Z) for i in range(Z)])]
    all_to_all x1 -> x2, starting transfers between devices: 3.89 us -> 13 us  [exchange(): return lax.all_to_all(sends, RING, split_axis=0, concat_axis=0, tiled=True)]
    ppermute x14, starting transfers between devices: 32.4 us -> 36.8 us  [exchange_by_steps(): lax.ppermute(sends[k], RING, [(i, (i + k) % Z) for i in range(Z)])]
    unnamed x12 -> x22, local copies, waits for them, and re-layouts: 5 us -> 4.55 us
    pallas_call x7 -> x10, Pallas kernels: 17.9 us -> 18 us  [call(): return lambda *args: made(*args, *after)]
  transfers between devices with their start and end apart: 27 -> 28, of which waited for: 14 -> 10; matrix products, arithmetic and copies ran while one was open for 0% -> 0% of each run, Pallas kernels for 12% -> 12%
where the time goes in v2:
time: 117 us; the launch traced here: 116 us
  starting transfers between devices  66.9 us (57%)
  waiting for transfers between devices  26.2 us (22%)
  Pallas kernels  18 us (15%)
  local copies, waits for them, and re-layouts  4.55 us (4%)
    ppermute x14, starting transfers between devices, exchange_by_steps(): lax.ppermute(sends[k], RING, [(i, (i + k) % Z) for i in range(Z)])  36.8 us
    pallas_call x10, Pallas kernels, call(): return lambda *args: made(*args, *after)  18 us
    ppermute x12, starting transfers between devices, shift(): lax.ppermute(block, ('x', 'row'), [(flat(x + dx, r + dr), flat(x, r)) for...  17 us
    ppermute x14, waiting for transfers between devices, exchange_by_steps(): lax.ppermute(sends[k], RING, [(i, (i + k) % Z) for i in range(Z)])  13.8 us
    all_to_all x2, starting transfers between devices, exchange(): return lax.all_to_all(sends, RING, split_axis=0, concat_axis=0, tiled=True)  13 us
    ppermute x12, waiting for transfers between devices, shift(): lax.ppermute(block, ('x', 'row'), [(flat(x + dx, r + dr), flat(x, r)) for...  12 us
    unnamed x22, local copies, waits for them, and re-layouts  4.55 us
  transfers between devices with their start and end apart: 28, of which 10 were waited for; matrix products, arithmetic and copies ran while one was open for 0% of the time, Pallas kernels for 12%

profile of v2, /device:TPU:32, one launch (start us, length us, event | category | flops | bytes accessed | tf_op | source)
XLA Modules:
  0.0 116.3 jit_solution(6041286502533467106)
XLA Ops:
  0.7 1.0 copy-done.4
  1.7 1.0 copy-done.5
  2.7 1.0 copy-done.6
  3.7 0.7 copy-done.7
  4.4 1.3 %pack_q.1 = (bf16[7,2,2,16,128]{4,3,2,1,0:T(8,128)(2,1)S(1)}, bf16[7,2,2,16,128]{4,3,2,1,0:T(8,128)(2,1)S(1)}, bf16[7,2,2,16,128]{4,3,2,1,0:T(8,128)(2,1)S(1)}, ...) custom-call(bf16[2,2,16,3072]{3,2,1,0:T(8,128)(2,1)S(1)} %copy-done., ...), custom_call_target="tpu_custom_call" | custom-call | bytes 1048576 | tf_op jit(solution)/shard_map/pack_q/pallas_call | solution.py:49
  5.7 6.4 %collective-permute-start = (bf16[7,2,2,16,128]{4,3,2,1,0:T(8,128)(2,1)S(1)}, bf16[7,2,2,16,128]{4,3,2,1,0:T(8,128)(2,1)S(1)}, u32[]{:S(2)}, u32[]{:S(2)}) collective-permute-start(bf16[7,2,2,16,128]{4,3,2,1,0:T(8,128)(2,1)S(1)} %get-tuple-element.26), channel_id=1, source_target_pairs={{0,32},{1,33},{16,48},{17,49},{32,0},{33,1},{48,16},{49,17},{2,34}... | collective-permute-start | bytes 344072 | tf_op jit(solution)/shard_map/ppermute | solution.py:287
  12.1 0.0 collective-permute-start.1
  12.1 5.0 %collective-permute-start.2 = (bf16[7,2,2,16,128]{4,3,2,1,0:T(8,128)(2,1)S(1)}, bf16[7,2,2,16,128]{4,3,2,1,0:T(8,128)(2,1)S(1)}, u32[]{:S(2)}, u32[]{:S(2)}) collective-permute-start(bf16[7,2,2,16,128]{4,3,2,1,0:T(8,128)(2,1)S(1)} %get-tuple-element.28), channel_id=1, source_target_pairs={{0,33},{1,48},{16,49},{17,0},{32,1},{33,16},{48,17},{49,32},{2,35}... | collective-permute-start | bytes 344072 | tf_op jit(solution)/shard_map/ppermute | solution.py:287
  17.1 0.3 collective-permute-start.3
  17.4 3.9 %collective-permute-start.4 = (bf16[7,2,2,16,128]{4,3,2,1,0:T(8,128)(2,1)S(1)}, bf16[7,2,2,16,128]{4,3,2,1,0:T(8,128)(2,1)S(1)}, u32[]{:S(2)}, u32[]{:S(2)}) collective-permute-start(bf16[7,2,2,16,128]{4,3,2,1,0:T(8,128)(2,1)S(1)} %get-tuple-element.30), channel_id=1, source_target_pairs={{0,48},{1,49},{16,0},{17,1},{32,16},{33,17},{48,32},{49,33},{2,50}... | collective-permute-start | bytes 344072 | tf_op jit(solution)/shard_map/ppermute | solution.py:287
  21.3 0.0 collective-permute-done.refs_2_.refs_1_
  21.3 1.0 collective-permute-start.5
  22.3 1.3 %collective-permute-done.1.refs_3_.refs_2_ = bf16[7,2,2,16,128]{4,3,2,1,0:T(8,128)(2,1)S(1)} collective-permute-done((bf16[7,2,2,16,128]{4,3,2,1,0:T(8,128)(2,1)S(1)}, bf16[7,2,2,16,128]{4,3,2,1,0:T(8,128)(2,1)S(1)}, u32[]{:S(2)}, u32[]{:S(2)}) %collective-permute-start.1) | collective-permute-done | bytes 114720 | tf_op jit(solution)/shard_map/ppermute | solution.py:287
  23.6 4.5 %collective-permute-start.6 = (bf16[7,2,2,16,128]{4,3,2,1,0:T(8,128)(2,1)S(1)}, bf16[7,2,2,16,128]{4,3,2,1,0:T(8,128)(2,1)S(1)}, u32[]{:S(2)}, u32[]{:S(2)}) collective-permute-start(bf16[7,2,2,16,128]{4,3,2,1,0:T(8,128)(2,1)S(1)} %get-tuple-element.32), channel_id=1, source_target_pairs={{0,49},{1,0},{16,1},{17,16},{32,17},{33,32},{48,33},{49,48},{2,51}... | collective-permute-start | bytes 344072 | tf_op jit(solution)/shard_map/ppermute | solution.py:287
  28.2 0.0 collective-permute-done.2.refs_4_.refs_3_
  28.2 2.7 %collective-permute-done.3.refs_5_.refs_4_ = bf16[7,2,2,16,128]{4,3,2,1,0:T(8,128)(2,1)S(1)} collective-permute-done((bf16[7,2,2,16,128]{4,3,2,1,0:T(8,128)(2,1)S(1)}, bf16[7,2,2,16,128]{4,3,2,1,0:T(8,128)(2,1)S(1)}, u32[]{:S(2)}, u32[]{:S(2)}) %collective-permute-start.3) | collective-permute-done | bytes 114720 | tf_op jit(solution)/shard_map/ppermute | solution.py:287
  30.9 0.0 collective-permute-done.4.refs_6_.refs_5_
  30.9 1.6 %collective-permute-done.5.refs_7_.refs_6_ = bf16[7,2,2,16,128]{4,3,2,1,0:T(8,128)(2,1)S(1)} collective-permute-done((bf16[7,2,2,16,128]{4,3,2,1,0:T(8,128)(2,1)S(1)}, bf16[7,2,2,16,128]{4,3,2,1,0:T(8,128)(2,1)S(1)}, u32[]{:S(2)}, u32[]{:S(2)}) %collective-permute-start.5) | collective-permute-done | bytes 114720 | tf_op jit(solution)/shard_map/ppermute | solution.py:287
  32.5 0.5 collective-permute-done.6.refs_8_.refs_7_
  33.0 1.4 %pack_kv.1 = bf16[8,6,2,2,16,128]{5,4,3,2,1,0:T(8,128)(2,1)} custom-call(bf16[2,2,16,3072]{3,2,1,0:T(8,128)(2,1)S(1)} %copy-done.2, bf16[2,2,16,3072]{3,2,1,0:T(8,128)(2,1)S(1)} %copy-done.3, bf16[7,2,2,16,128]{4,3,2,1,0:T(8,128)(2,1)S(1)} %collective-permute-done.refs_2_.refs_1_, bf16[7,2,2,16,128]{4,3,2,1,0:T(8,128)(2,1)S(1)} %collective-permute-done.1.refs_3_.refs_2_, ...), custom_call_target="tpu_custom_call" | custom-call | bytes 1048576 | tf_op jit(solution)/shard_map/pack_kv/pallas_call | solution.py:49
  34.4 6.1 %all-to-all-start = ((bf16[8,6,2,2,16,128]{5,4,3,2,1,0:T(8,128)(2,1)}), bf16[8,6,2,2,16,128]{5,4,3,2,1,0:T(8,128)(2,1)S(1)}, u32[]{:S(2)}, u32[]{:S(2)}) async-start(bf16[8,6,2,2,16,128]{5,4,3,2,1,0:T(8,128)(2,1)} %pack_kv.1), calls=%async_computation | async-start | bytes 1572864 | tf_op jit(solution)/shard_map/all_to_all | solution.py:283
  40.5 0.4 gather_q.1
  40.9 1.6 %collective-permute-start.10 = (bf16[8,7,2,2,16,128]{5,4,3,2,1,0:T(8,128)(2,1)S(1)}, bf16[8,7,2,2,16,128]{5,4,3,2,1,0:T(8,128)(2,1)S(1)}, u32[]{:S(2)}, u32[]{:S(2)}) collective-permute-start(bf16[8,7,2,2,16,128]{5,4,3,2,1,0:T(8,128)(2,1)S(1)} %get-tuple-element.34.refs_1_.refs_6_), channel_id=1, source_target_pairs={{2,0},{4,2},{6,4},{8,6},{10,8},{12,10},{14,12},{0,14},{66,64},{68,... | collective-permute-start | bytes 2752520 | tf_op jit(solution)/shard_map/ppermute | solution.py:293
  42.5 0.0 collective-permute-start.9
  42.5 1.5 %collective-permute-start.11 = (bf16[2,7,2,2,16,128]{5,4,3,2,1,0:T(8,128)(2,1)S(1)}, bf16[2,7,2,2,16,128]{5,4,3,2,1,0:T(8,128)(2,1)S(1)}, u32[]{:S(2)}, u32[]{:S(2)}) collective-permute-start(bf16[2,7,2,2,16,128]{5,4,3,2,1,0:T(8,128)(2,1)S(1)} %get-tuple-element.35), channel_id=1, source_target_pairs={{192,0},{194,2},{196,4},{198,6},{200,8},{202,10},{204,12},{206,14}... | collective-permute-start | bytes 688136 | tf_op jit(solution)/shard_map/ppermute | solution.py:293
  44.0 1.7 %collective-permute-start.12 = (bf16[2,7,2,2,16,128]{5,4,3,2,1,0:T(8,128)(2,1)S(1)}, bf16[2,7,2,2,16,128]{5,4,3,2,1,0:T(8,128)(2,1)S(1)}, u32[]{:S(2)}, u32[]{:S(2)}) collective-permute-start(bf16[2,7,2,2,16,128]{5,4,3,2,1,0:T(8,128)(2,1)S(1)} %get-tuple-element.36), channel_id=1, source_target_pairs={{64,0},{66,2},{68,4},{70,6},{72,8},{74,10},{76,12},{78,14},{128,64... | collective-permute-start | bytes 688136 | tf_op jit(solution)/shard_map/ppermute | solution.py:293
  45.8 5.6 %collective-permute-done.11.refs_0_ = bf16[2,7,2,2,16,128]{5,4,3,2,1,0:T(8,128)(2,1)S(1)} collective-permute-done((bf16[2,7,2,2,16,128]{5,4,3,2,1,0:T(8,128)(2,1)S(1)}, bf16[2,7,2,2,16,128]{5,4,3,2,1,0:T(8,128)(2,1)S(1)}, u32[]{:S(2)}, u32[]{:S(2)}) %collective-permute-start.11) | collective-permute-done | bytes 229408 | tf_op jit(solution)/shard_map/ppermute | solution.py:293
  51.4 0.0 collective-permute-done.12.refs_1_
  51.4 0.0 collective-permute-start.13
  51.4 2.9 %collective-permute-start.14 = (bf16[4,7,2,2,16,128]{5,4,3,2,1,0:T(8,128)(2,1)S(1)}, bf16[4,7,2,2,16,128]{5,4,3,2,1,0:T(8,128)(2,1)S(1)}, u32[]{:S(2)}, u32[]{:S(2)}) collective-permute-start(bf16[4,7,2,2,16,128]{5,4,3,2,1,0:T(8,128)(2,1)S(1)} %join_q.1.refs_4_), channel_id=1, source_target_pairs={{2,0},{4,2},{6,4},{8,6},{10,8},{12,10},{14,12},{0,14},{66,64},{68,... | collective-permute-start | bytes 1376264 | tf_op jit(solution)/shard_map/ppermute | solution.py:293
  54.4 0.8 copy-done
  55.1 6.3 %collective-permute-done.13.refs_3_ = bf16[4,7,2,2,16,128]{5,4,3,2,1,0:T(8,128)(2,1)S(1)} collective-permute-done((bf16[4,7,2,2,16,128]{5,4,3,2,1,0:T(8,128)(2,1)S(1)}, bf16[4,7,2,2,16,128]{5,4,3,2,1,0:T(8,128)(2,1)S(1)}, u32[]{:S(2)}, u32[]{:S(2)}) %collective-permute-start.13) | collective-permute-done | bytes 458784 | tf_op jit(solution)/shard_map/ppermute | solution.py:293
  61.5 0.0 collective-permute-done.14.refs_4_.refs_5_
  61.5 0.0 collective-permute-done.10.refs_2_
  61.5 0.0 collective-permute-done.9.refs_1_.refs_0_
  61.5 0.4 all-to-all-done.refs_0_.refs_6_.refs_1_
  61.9 1.6 %collective-permute-start.15 = (bf16[2,6,2,2,16,128]{5,4,3,2,1,0:T(8,128)(2,1)S(1)}, bf16[2,6,2,2,16,128]{5,4,3,2,1,0:T(8,128)(2,1)S(1)}, u32[]{:S(2)}, u32[]{:S(2)}) collective-permute-start(bf16[2,6,2,2,16,128]{5,4,3,2,1,0:T(8,128)(2,1)S(1)} %get-tuple-element.37), channel_id=1, source_target_pairs={{192,0},{194,2},{196,4},{198,6},{200,8},{202,10},{204,12},{206,14}... | collective-permute-start | bytes 589832 | tf_op jit(solution)/shard_map/ppermute | solution.py:293
  63.5 1.7 %collective-permute-start.16 = (bf16[2,6,2,2,16,128]{5,4,3,2,1,0:T(8,128)(2,1)S(1)}, bf16[2,6,2,2,16,128]{5,4,3,2,1,0:T(8,128)(2,1)S(1)}, u32[]{:S(2)}, u32[]{:S(2)}) collective-permute-start(bf16[2,6,2,2,16,128]{5,4,3,2,1,0:T(8,128)(2,1)S(1)} %get-tuple-element.38), channel_id=1, source_target_pairs={{64,0},{66,2},{68,4},{70,6},{72,8},{74,10},{76,12},{78,14},{128,64... | collective-permute-start | bytes 589832 | tf_op jit(solution)/shard_map/ppermute | solution.py:293
  65.2 0.0 collective-permute-start.7
  65.2 3.0 %collective-permute-start.8 = (bf16[8,6,2,2,16,128]{5,4,3,2,1,0:T(8,128)(2,1)S(1)}, bf16[8,6,2,2,16,128]{5,4,3,2,1,0:T(8,128)(2,1)}, u32[]{:S(2)}, u32[]{:S(2)}) collective-permute-start(bf16[8,6,2,2,16,128]{5,4,3,2,1,0:T(8,128)(2,1)S(1)} %all-to-all-done.refs_0_.refs_6_.refs_1_), channel_id=1, source_target_pairs={{2,0},{4,2},{6,4},{8,6},{10,8},{12,10},{14,12},{0,14},{66,64},{68,... | collective-permute-start | bytes 2359304 | tf_op jit(solution)/shard_map/ppermute | solution.py:293
  68.2 6.6 %key_grads.1.refs_2_ = bf16[8,6,2,2,16,128]{5,4,3,2,1,0:T(8,128)(2,1)} custom-call(bf16[8,7,2,2,16,128]{5,4,3,2,1,0:T(8,128)(2,1)S(1)} %collective-permute-done.9.refs_1_.refs_0_, bf16[8,7,2,2,16,128]{5,4,3,2,1,0:T(8,128)(2,1)S(1)} %copy-done.9, bf16[8,7,2,2,16,128]{5,4,3,2,1,0:T(8,128)(2,1)S(1)} %collective-permute-done.10.refs_2_, ...), custom_call_target="tpu_custom_call" | custom-call | flops 10000000000 | bytes 1048576 | tf_op jit(solution)/shard_map/key_grads/pallas_call | solution.py:49
  74.7 0.0 collective-permute-done.15.refs_0_
  74.7 0.0 collective-permute-done.16.refs_1_
  74.8 0.0 collective-permute-start.17
  74.8 2.9 %collective-permute-start.18 = (bf16[4,6,2,2,16,128]{5,4,3,2,1,0:T(8,128)(2,1)S(1)}, bf16[4,6,2,2,16,128]{5,4,3,2,1,0:T(8,128)(2,1)}, u32[]{:S(2)}, u32[]{:S(2)}) collective-permute-start(bf16[4,6,2,2,16,128]{5,4,3,2,1,0:T(8,128)(2,1)S(1)} %join_kv.1.refs_4_), channel_id=1, source_target_pairs={{2,0},{4,2},{6,4},{8,6},{10,8},{12,10},{14,12},{0,14},{66,64},{68,... | collective-permute-start | bytes 1179656 | tf_op jit(solution)/shard_map/ppermute | solution.py:293
  77.8 6.9 %all-to-all-start.1 = ((bf16[8,6,2,2,16,128]{5,4,3,2,1,0:T(8,128)(2,1)}), bf16[8,6,2,2,16,128]{5,4,3,2,1,0:T(8,128)(2,1)S(1)}, u32[]{:S(2)}, u32[]{:S(2)}) async-start(bf16[8,6,2,2,16,128]{5,4,3,2,1,0:T(8,128)(2,1)} %key_grads.1.refs_2_), calls=%async_computation.1 | async-start | bytes 1572864 | tf_op jit(solution)/shard_map/all_to_all | solution.py:283
  84.6 0.0 collective-permute-done.17.refs_3_
  84.6 0.0 collective-permute-done.18.refs_5_
  84.6 0.0 collective-permute-done.7.refs_0_
  84.7 0.0 collective-permute-done.8.refs_2_
  84.7 6.3 %query_grads.1 = (bf16[3,2,2,16,128]{4,3,2,1,0:T(8,128)(2,1)S(1)}, bf16[3,2,2,16,128]{4,3,2,1,0:T(8,128)(2,1)S(1)}, bf16[3,2,2,16,128]{4,3,2,1,0:T(8,128)(2,1)S(...) custom-call(bf16[8,6,2,2,16,128]{5,4,3,2,1,0:T(8,128)(2,1)} %collect, ...), custom_call_target="tpu_custom_call" | custom-call | flops 99999997952 | bytes 1048576 | tf_op jit(solution)/shard_map/query_grads/pallas_call | solution.py:49
  91.0 4.6 %collective-permute-start.19 = (bf16[3,2,2,16,128]{4,3,2,1,0:T(8,128)(2,1)S(1)}, bf16[3,2,2,16,128]{4,3,2,1,0:T(8,128)(2,1)S(1)}, u32[]{:S(2)}, u32[]{:S(2)}) collective-permute-start(bf16[3,2,2,16,128]{4,3,2,1,0:T(8,128)(2,1)S(1)} %get-tuple-element.40), channel_id=1, source_target_pairs={{0,32},{1,33},{16,48},{17,49},{32,0},{33,1},{48,16},{49,17},{2,34}... | collective-permute-start | bytes 147464 | tf_op jit(solution)/shard_map/ppermute | solution.py:287
  95.6 0.1 collective-permute-start.20
  95.7 5.0 %collective-permute-start.21 = (bf16[3,2,2,16,128]{4,3,2,1,0:T(8,128)(2,1)S(1)}, bf16[3,2,2,16,128]{4,3,2,1,0:T(8,128)(2,1)S(1)}, u32[]{:S(2)}, u32[]{:S(2)}) collective-permute-start(bf16[3,2,2,16,128]{4,3,2,1,0:T(8,128)(2,1)S(1)} %get-tuple-element.42), channel_id=1, source_target_pairs={{0,33},{1,48},{16,49},{17,0},{32,1},{33,16},{48,17},{49,32},{2,35}... | collective-permute-start | bytes 147464 | tf_op jit(solution)/shard_map/ppermute | solution.py:287
  100.6 0.0 collective-permute-start.22
  100.6 4.1 %collective-permute-start.23 = (bf16[3,2,2,16,128]{4,3,2,1,0:T(8,128)(2,1)S(1)}, bf16[3,2,2,16,128]{4,3,2,1,0:T(8,128)(2,1)S(1)}, u32[]{:S(2)}, u32[]{:S(2)}) collective-permute-start(bf16[3,2,2,16,128]{4,3,2,1,0:T(8,128)(2,1)S(1)} %get-tuple-element.44), channel_id=1, source_target_pairs={{0,48},{1,49},{16,0},{17,1},{32,16},{33,17},{48,32},{49,33},{2,50}... | collective-permute-start | bytes 147464 | tf_op jit(solution)/shard_map/ppermute | solution.py:287
  104.7 4.5 %collective-permute-done.19.refs_1_ = bf16[3,2,2,16,128]{4,3,2,1,0:T(8,128)(2,1)S(1)} collective-permute-done((bf16[3,2,2,16,128]{4,3,2,1,0:T(8,128)(2,1)S(1)}, bf16[3,2,2,16,128]{4,3,2,1,0:T(8,128)(2,1)S(1)}, u32[]{:S(2)}, u32[]{:S(2)}) %collective-permute-start.19) | collective-permute-done | bytes 49184 | tf_op jit(solution)/shard_map/ppermute | solution.py:287
  109.2 1.2 %collective-permute-start.24 = (bf16[3,2,2,16,128]{4,3,2,1,0:T(8,128)(2,1)S(1)}, bf16[3,2,2,16,128]{4,3,2,1,0:T(8,128)(2,1)S(1)}, u32[]{:S(2)}, u32[]{:S(2)}) collective-permute-start(bf16[3,2,2,16,128]{4,3,2,1,0:T(8,128)(2,1)S(1)} %get-tuple-element.45), channel_id=1, source_target_pairs={{0,1},{1,16},{16,17},{17,32},{32,33},{33,48},{48,49},{49,0},{2,3},... | collective-permute-start | bytes 147464 | tf_op jit(solution)/shard_map/ppermute | solution.py:287
  110.4 0.0 collective-permute-done.20.refs_2_
  110.4 0.9 collective-permute-start.25
  111.2 2.0 %collective-permute-done.24.refs_6_ = bf16[3,2,2,16,128]{4,3,2,1,0:T(8,128)(2,1)S(1)} collective-permute-done((bf16[3,2,2,16,128]{4,3,2,1,0:T(8,128)(2,1)S(1)}, bf16[3,2,2,16,128]{4,3,2,1,0:T(8,128)(2,1)S(1)}, u32[]{:S(2)}, u32[]{:S(2)}) %collective-permute-start.24) | collective-permute-done | bytes 49184 | tf_op jit(solution)/shard_map/ppermute | solution.py:287
  113.3 1.2 %collective-permute-done.25.refs_7_ = bf16[3,2,2,16,128]{4,3,2,1,0:T(8,128)(2,1)S(1)} collective-permute-done((bf16[3,2,2,16,128]{4,3,2,1,0:T(8,128)(2,1)S(1)}, bf16[3,2,2,16,128]{4,3,2,1,0:T(8,128)(2,1)S(1)}, u32[]{:S(2)}, u32[]{:S(2)}) %collective-permute-start.25) | collective-permute-done | bytes 49184 | tf_op jit(solution)/shard_map/ppermute | solution.py:287
  114.5 0.8 unpack_q.1
  115.3 1.0 unpack_kv.1
  (24 shorter events, 0.1 us)
Async XLA Ops:
  0.6 32.3 %copy-start.2 = (bf16[2,2,16,3072]{3,2,1,0:T(8,128)(2,1)S(1)}, bf16[2,2,16,3072]{3,2,1,0:T(8,128)(2,1)}, u32[]{:S(2)}) copy-start(bf16[2,2,16,3072]{3,2,1,0:T(8,128)(2,1)} %refs_0_.3) | copy-start | bytes 1179652
  0.6 1.0 copy-start.4
  1.7 1.0 copy-start.5
  2.7 1.0 copy-start.6
  3.7 0.7 copy-start.7
  4.4 28.5 %copy-start.3 = (bf16[2,2,16,3072]{3,2,1,0:T(8,128)(2,1)S(1)}, bf16[2,2,16,3072]{3,2,1,0:T(8,128)(2,1)}, u32[]{:S(2)}) copy-start(bf16[2,2,16,3072]{3,2,1,0:T(8,128)(2,1)} %refs_1_.3) | copy-start | bytes 1179652
  5.7 15.6 %collective-permute-start = (bf16[7,2,2,16,128]{4,3,2,1,0:T(8,128)(2,1)S(1)}, bf16[7,2,2,16,128]{4,3,2,1,0:T(8,128)(2,1)S(1)}, u32[]{:S(2)}, u32[]{:S(2)}) collective-permute-start(bf16[7,2,2,16,128]{4,3,2,1,0:T(8,128)(2,1)S(1)} %get-tuple-element.26), channel_id=1, source_target_pairs={{0,32},{1,33},{16,48},{17,49},{32,0},{33,1},{48,16},{49,17},{2,34}... | collective-permute-start | bytes 344072 | tf_op jit(solution)/shard_map/ppermute | solution.py:287
  12.1 11.5 %collective-permute-start.1 = (bf16[7,2,2,16,128]{4,3,2,1,0:T(8,128)(2,1)S(1)}, bf16[7,2,2,16,128]{4,3,2,1,0:T(8,128)(2,1)S(1)}, u32[]{:S(2)}, u32[]{:S(2)}) collective-permute-start(bf16[7,2,2,16,128]{4,3,2,1,0:T(8,128)(2,1)S(1)} %get-tuple-element.27), channel_id=1, source_target_pairs={{0,17},{1,32},{16,33},{17,48},{32,49},{33,0},{48,1},{49,16},{2,19}... | collective-permute-start | bytes 344072 | tf_op jit(solution)/shard_map/ppermute | solution.py:287
  12.1 16.0 %collective-permute-start.2 = (bf16[7,2,2,16,128]{4,3,2,1,0:T(8,128)(2,1)S(1)}, bf16[7,2,2,16,128]{4,3,2,1,0:T(8,128)(2,1)S(1)}, u32[]{:S(2)}, u32[]{:S(2)}) collective-permute-start(bf16[7,2,2,16,128]{4,3,2,1,0:T(8,128)(2,1)S(1)} %get-tuple-element.28), channel_id=1, source_target_pairs={{0,33},{1,48},{16,49},{17,0},{32,1},{33,16},{48,17},{49,32},{2,35}... | collective-permute-start | bytes 344072 | tf_op jit(solution)/shard_map/ppermute | solution.py:287
  17.1 13.7 %collective-permute-start.3 = (bf16[7,2,2,16,128]{4,3,2,1,0:T(8,128)(2,1)S(1)}, bf16[7,2,2,16,128]{4,3,2,1,0:T(8,128)(2,1)S(1)}, u32[]{:S(2)}, u32[]{:S(2)}) collective-permute-start(bf16[7,2,2,16,128]{4,3,2,1,0:T(8,128)(2,1)S(1)} %get-tuple-element.29), channel_id=1, source_target_pairs={{0,16},{1,17},{16,32},{17,33},{32,48},{33,49},{48,0},{49,1},{2,18}... | collective-permute-start | bytes 344072 | tf_op jit(solution)/shard_map/ppermute | solution.py:287
  17.4 13.5 %collective-permute-start.4 = (bf16[7,2,2,16,128]{4,3,2,1,0:T(8,128)(2,1)S(1)}, bf16[7,2,2,16,128]{4,3,2,1,0:T(8,128)(2,1)S(1)}, u32[]{:S(2)}, u32[]{:S(2)}) collective-permute-start(bf16[7,2,2,16,128]{4,3,2,1,0:T(8,128)(2,1)S(1)} %get-tuple-element.30), channel_id=1, source_target_pairs={{0,48},{1,49},{16,0},{17,1},{32,16},{33,17},{48,32},{49,33},{2,50}... | collective-permute-start | bytes 344072 | tf_op jit(solution)/shard_map/ppermute | solution.py:287
  21.3 11.2 %collective-permute-start.5 = (bf16[7,2,2,16,128]{4,3,2,1,0:T(8,128)(2,1)S(1)}, bf16[7,2,2,16,128]{4,3,2,1,0:T(8,128)(2,1)S(1)}, u32[]{:S(2)}, u32[]{:S(2)}) collective-permute-start(bf16[7,2,2,16,128]{4,3,2,1,0:T(8,128)(2,1)S(1)} %get-tuple-element.31), channel_id=1, source_target_pairs={{0,1},{1,16},{16,17},{17,32},{32,33},{33,48},{48,49},{49,0},{2,3},... | collective-permute-start | bytes 344072 | tf_op jit(solution)/shard_map/ppermute | solution.py:287
  23.6 9.3 %collective-permute-start.6 = (bf16[7,2,2,16,128]{4,3,2,1,0:T(8,128)(2,1)S(1)}, bf16[7,2,2,16,128]{4,3,2,1,0:T(8,128)(2,1)S(1)}, u32[]{:S(2)}, u32[]{:S(2)}) collective-permute-start(bf16[7,2,2,16,128]{4,3,2,1,0:T(8,128)(2,1)S(1)} %get-tuple-element.32), channel_id=1, source_target_pairs={{0,49},{1,0},{16,1},{17,16},{32,17},{33,32},{48,33},{49,48},{2,51}... | collective-permute-start | bytes 344072 | tf_op jit(solution)/shard_map/ppermute | solution.py:287
  34.4 27.5 %all-to-all-start = ((bf16[8,6,2,2,16,128]{5,4,3,2,1,0:T(8,128)(2,1)}), bf16[8,6,2,2,16,128]{5,4,3,2,1,0:T(8,128)(2,1)S(1)}, u32[]{:S(2)}, u32[]{:S(2)}) async-start(bf16[8,6,2,2,16,128]{5,4,3,2,1,0:T(8,128)(2,1)} %pack_kv.1), calls=%async_computation | async-start | bytes 1572864 | tf_op jit(solution)/shard_map/all_to_all | solution.py:283
  40.9 20.6 %copy-start.8 = (bf16[8,7,2,2,16,128]{5,4,3,2,1,0:T(8,128)(2,1)}, bf16[8,7,2,2,16,128]{5,4,3,2,1,0:T(8,128)(2,1)S(1)}, u32[]{:S(2)}) copy-start(bf16[8,7,2,2,16,128]{5,4,3,2,1,0:T(8,128)(2,1)S(1)} %get-tuple-element.34.refs_1_.refs_6_) | copy-start | bytes 2752516
  40.9 20.6 %collective-permute-start.10 = (bf16[8,7,2,2,16,128]{5,4,3,2,1,0:T(8,128)(2,1)S(1)}, bf16[8,7,2,2,16,128]{5,4,3,2,1,0:T(8,128)(2,1)S(1)}, u32[]{:S(2)}, u32[]{:S(2)}) collective-permute-start(bf16[8,7,2,2,16,128]{5,4,3,2,1,0:T(8,128)(2,1)S(1)} %get-tuple-element.34.refs_1_.refs_6_), channel_id=1, source_target_pairs={{2,0},{4,2},{6,4},{8,6},{10,8},{12,10},{14,12},{0,14},{66,64},{68,... | collective-permute-start | bytes 2752520 | tf_op jit(solution)/shard_map/ppermute | solution.py:293
  42.5 19.0 %collective-permute-start.9 = (bf16[8,7,2,2,16,128]{5,4,3,2,1,0:T(8,128)(2,1)S(1)}, bf16[8,7,2,2,16,128]{5,4,3,2,1,0:T(8,128)(2,1)S(1)}, u32[]{:S(2)}, u32[]{:S(2)}) collective-permute-start(bf16[8,7,2,2,16,128]{5,4,3,2,1,0:T(8,128)(2,1)S(1)} %get-tuple-element.34.refs_1_.refs_6_), channel_id=1, source_target_pairs={{14,0},{0,2},{2,4},{4,6},{6,8},{8,10},{10,12},{12,14},{78,64},{64,... | collective-permute-start | bytes 2752520 | tf_op jit(solution)/shard_map/ppermute | solution.py:293
  42.5 8.8 %collective-permute-start.11 = (bf16[2,7,2,2,16,128]{5,4,3,2,1,0:T(8,128)(2,1)S(1)}, bf16[2,7,2,2,16,128]{5,4,3,2,1,0:T(8,128)(2,1)S(1)}, u32[]{:S(2)}, u32[]{:S(2)}) collective-permute-start(bf16[2,7,2,2,16,128]{5,4,3,2,1,0:T(8,128)(2,1)S(1)} %get-tuple-element.35), channel_id=1, source_target_pairs={{192,0},{194,2},{196,4},{198,6},{200,8},{202,10},{204,12},{206,14}... | collective-permute-start | bytes 688136 | tf_op jit(solution)/shard_map/ppermute | solution.py:293
  44.0 7.3 %collective-permute-start.12 = (bf16[2,7,2,2,16,128]{5,4,3,2,1,0:T(8,128)(2,1)S(1)}, bf16[2,7,2,2,16,128]{5,4,3,2,1,0:T(8,128)(2,1)S(1)}, u32[]{:S(2)}, u32[]{:S(2)}) collective-permute-start(bf16[2,7,2,2,16,128]{5,4,3,2,1,0:T(8,128)(2,1)S(1)} %get-tuple-element.36), channel_id=1, source_target_pairs={{64,0},{66,2},{68,4},{70,6},{72,8},{74,10},{76,12},{78,14},{128,64... | collective-permute-start | bytes 688136 | tf_op jit(solution)/shard_map/ppermute | solution.py:293
  51.4 10.1 %collective-permute-start.13 = (bf16[4,7,2,2,16,128]{5,4,3,2,1,0:T(8,128)(2,1)S(1)}, bf16[4,7,2,2,16,128]{5,4,3,2,1,0:T(8,128)(2,1)S(1)}, u32[]{:S(2)}, u32[]{:S(2)}) collective-permute-start(bf16[4,7,2,2,16,128]{5,4,3,2,1,0:T(8,128)(2,1)S(1)} %join_q.1.refs_4_), channel_id=1, source_target_pairs={{14,0},{0,2},{2,4},{4,6},{6,8},{8,10},{10,12},{12,14},{78,64},{64,... | collective-permute-start | bytes 1376264 | tf_op jit(solution)/shard_map/ppermute | solution.py:293
  51.4 10.0 %collective-permute-start.14 = (bf16[4,7,2,2,16,128]{5,4,3,2,1,0:T(8,128)(2,1)S(1)}, bf16[4,7,2,2,16,128]{5,4,3,2,1,0:T(8,128)(2,1)S(1)}, u32[]{:S(2)}, u32[]{:S(2)}) collective-permute-start(bf16[4,7,2,2,16,128]{5,4,3,2,1,0:T(8,128)(2,1)S(1)} %join_q.1.refs_4_), channel_id=1, source_target_pairs={{2,0},{4,2},{6,4},{8,6},{10,8},{12,10},{14,12},{0,14},{66,64},{68,... | collective-permute-start | bytes 1376264 | tf_op jit(solution)/shard_map/ppermute | solution.py:293
  54.4 0.8 copy-start
  61.9 6.3 %copy-start.1 = (bf16[4,7,2,2,16,128]{5,4,3,2,1,0:T(8,128)(2,1)S(1)}, bf16[4,7,2,2,16,128]{5,4,3,2,1,0:T(8,128)(2,1)}, u32[]{:S(2)}) copy-start(bf16[4,7,2,2,16,128]{5,4,3,2,1,0:T(8,128)(2,1)} %copy-done) | copy-start | bytes 1376260
  61.9 6.3 %copy-start.9 = (bf16[8,7,2,2,16,128]{5,4,3,2,1,0:T(8,128)(2,1)S(1)}, bf16[8,7,2,2,16,128]{5,4,3,2,1,0:T(8,128)(2,1)}, u32[]{:S(2)}) copy-start(bf16[8,7,2,2,16,128]{5,4,3,2,1,0:T(8,128)(2,1)} %copy-done.8) | copy-start | bytes 2752516
  61.9 12.8 %collective-permute-start.15 = (bf16[2,6,2,2,16,128]{5,4,3,2,1,0:T(8,128)(2,1)S(1)}, bf16[2,6,2,2,16,128]{5,4,3,2,1,0:T(8,128)(2,1)S(1)}, u32[]{:S(2)}, u32[]{:S(2)}) collective-permute-start(bf16[2,6,2,2,16,128]{5,4,3,2,1,0:T(8,128)(2,1)S(1)} %get-tuple-element.37), channel_id=1, source_target_pairs={{192,0},{194,2},{196,4},{198,6},{200,8},{202,10},{204,12},{206,14}... | collective-permute-start | bytes 589832 | tf_op jit(solution)/shard_map/ppermute | solution.py:293
  63.5 11.3 %collective-permute-start.16 = (bf16[2,6,2,2,16,128]{5,4,3,2,1,0:T(8,128)(2,1)S(1)}, bf16[2,6,2,2,16,128]{5,4,3,2,1,0:T(8,128)(2,1)S(1)}, u32[]{:S(2)}, u32[]{:S(2)}) collective-permute-start(bf16[2,6,2,2,16,128]{5,4,3,2,1,0:T(8,128)(2,1)S(1)} %get-tuple-element.38), channel_id=1, source_target_pairs={{64,0},{66,2},{68,4},{70,6},{72,8},{74,10},{76,12},{78,14},{128,64... | collective-permute-start | bytes 589832 | tf_op jit(solution)/shard_map/ppermute | solution.py:293
  65.2 19.4 %collective-permute-start.7 = (bf16[8,6,2,2,16,128]{5,4,3,2,1,0:T(8,128)(2,1)S(1)}, bf16[8,6,2,2,16,128]{5,4,3,2,1,0:T(8,128)(2,1)}, u32[]{:S(2)}, u32[]{:S(2)}) collective-permute-start(bf16[8,6,2,2,16,128]{5,4,3,2,1,0:T(8,128)(2,1)S(1)} %all-to-all-done.refs_0_.refs_6_.refs_1_), channel_id=1, source_target_pairs={{14,0},{0,2},{2,4},{4,6},{6,8},{8,10},{10,12},{12,14},{78,64},{64,... | collective-permute-start | bytes 2359304 | tf_op jit(solution)/shard_map/ppermute | solution.py:293
  65.2 19.4 %collective-permute-start.8 = (bf16[8,6,2,2,16,128]{5,4,3,2,1,0:T(8,128)(2,1)S(1)}, bf16[8,6,2,2,16,128]{5,4,3,2,1,0:T(8,128)(2,1)}, u32[]{:S(2)}, u32[]{:S(2)}) collective-permute-start(bf16[8,6,2,2,16,128]{5,4,3,2,1,0:T(8,128)(2,1)S(1)} %all-to-all-done.refs_0_.refs_6_.refs_1_), channel_id=1, source_target_pairs={{2,0},{4,2},{6,4},{8,6},{10,8},{12,10},{14,12},{0,14},{66,64},{68,... | collective-permute-start | bytes 2359304 | tf_op jit(solution)/shard_map/ppermute | solution.py:293
  74.8 9.9 %copy-start.10 = (bf16[8,7,2,2,16,128]{5,4,3,2,1,0:T(8,128)(2,1)S(1)}, bf16[8,7,2,2,16,128]{5,4,3,2,1,0:T(8,128)(2,1)}, u32[]{:S(2)}) copy-start(bf16[8,7,2,2,16,128]{5,4,3,2,1,0:T(8,128)(2,1)} %copy-done.8) | copy-start | bytes 2752516
  74.8 9.8 %collective-permute-start.17 = (bf16[4,6,2,2,16,128]{5,4,3,2,1,0:T(8,128)(2,1)S(1)}, bf16[4,6,2,2,16,128]{5,4,3,2,1,0:T(8,128)(2,1)S(1)}, u32[]{:S(2)}, u32[]{:S(2)}) collective-permute-start(bf16[4,6,2,2,16,128]{5,4,3,2,1,0:T(8,128)(2,1)S(1)} %join_kv.1.refs_4_), channel_id=1, source_target_pairs={{14,0},{0,2},{2,4},{4,6},{6,8},{8,10},{10,12},{12,14},{78,64},{64,... | collective-permute-start | bytes 1179656 | tf_op jit(solution)/shard_map/ppermute | solution.py:293
  74.8 9.8 %collective-permute-start.18 = (bf16[4,6,2,2,16,128]{5,4,3,2,1,0:T(8,128)(2,1)S(1)}, bf16[4,6,2,2,16,128]{5,4,3,2,1,0:T(8,128)(2,1)}, u32[]{:S(2)}, u32[]{:S(2)}) collective-permute-start(bf16[4,6,2,2,16,128]{5,4,3,2,1,0:T(8,128)(2,1)S(1)} %join_kv.1.refs_4_), channel_id=1, source_target_pairs={{2,0},{4,2},{6,4},{8,6},{10,8},{12,10},{14,12},{0,14},{66,64},{68,... | collective-permute-start | bytes 1179656 | tf_op jit(solution)/shard_map/ppermute | solution.py:293
  77.8 37.5 %all-to-all-start.1 = ((bf16[8,6,2,2,16,128]{5,4,3,2,1,0:T(8,128)(2,1)}), bf16[8,6,2,2,16,128]{5,4,3,2,1,0:T(8,128)(2,1)S(1)}, u32[]{:S(2)}, u32[]{:S(2)}) async-start(bf16[8,6,2,2,16,128]{5,4,3,2,1,0:T(8,128)(2,1)} %key_grads.1.refs_2_), calls=%async_computation.1 | async-start | bytes 1572864 | tf_op jit(solution)/shard_map/all_to_all | solution.py:283
  91.0 18.2 %collective-permute-start.19 = (bf16[3,2,2,16,128]{4,3,2,1,0:T(8,128)(2,1)S(1)}, bf16[3,2,2,16,128]{4,3,2,1,0:T(8,128)(2,1)S(1)}, u32[]{:S(2)}, u32[]{:S(2)}) collective-permute-start(bf16[3,2,2,16,128]{4,3,2,1,0:T(8,128)(2,1)S(1)} %get-tuple-element.40), channel_id=1, source_target_pairs={{0,32},{1,33},{16,48},{17,49},{32,0},{33,1},{48,16},{49,17},{2,34}... | collective-permute-start | bytes 147464 | tf_op jit(solution)/shard_map/ppermute | solution.py:287
  95.6 14.8 %collective-permute-start.20 = (bf16[3,2,2,16,128]{4,3,2,1,0:T(8,128)(2,1)S(1)}, bf16[3,2,2,16,128]{4,3,2,1,0:T(8,128)(2,1)S(1)}, u32[]{:S(2)}, u32[]{:S(2)}) collective-permute-start(bf16[3,2,2,16,128]{4,3,2,1,0:T(8,128)(2,1)S(1)} %get-tuple-element.41), channel_id=1, source_target_pairs={{0,17},{1,32},{16,33},{17,48},{32,49},{33,0},{48,1},{49,16},{2,19}... | collective-permute-start | bytes 147464 | tf_op jit(solution)/shard_map/ppermute | solution.py:287
  95.7 15.6 %collective-permute-start.21 = (bf16[3,2,2,16,128]{4,3,2,1,0:T(8,128)(2,1)S(1)}, bf16[3,2,2,16,128]{4,3,2,1,0:T(8,128)(2,1)S(1)}, u32[]{:S(2)}, u32[]{:S(2)}) collective-permute-start(bf16[3,2,2,16,128]{4,3,2,1,0:T(8,128)(2,1)S(1)} %get-tuple-element.42), channel_id=1, source_target_pairs={{0,33},{1,48},{16,49},{17,0},{32,1},{33,16},{48,17},{49,32},{2,35}... | collective-permute-start | bytes 147464 | tf_op jit(solution)/shard_map/ppermute | solution.py:287
  100.6 10.6 %collective-permute-start.22 = (bf16[3,2,2,16,128]{4,3,2,1,0:T(8,128)(2,1)S(1)}, bf16[3,2,2,16,128]{4,3,2,1,0:T(8,128)(2,1)S(1)}, u32[]{:S(2)}, u32[]{:S(2)}) collective-permute-start(bf16[3,2,2,16,128]{4,3,2,1,0:T(8,128)(2,1)S(1)} %get-tuple-element.43), channel_id=1, source_target_pairs={{0,16},{1,17},{16,32},{17,33},{32,48},{33,49},{48,0},{49,1},{2,18}... | collective-permute-start | bytes 147464 | tf_op jit(solution)/shard_map/ppermute | solution.py:287
  100.6 10.6 %collective-permute-start.23 = (bf16[3,2,2,16,128]{4,3,2,1,0:T(8,128)(2,1)S(1)}, bf16[3,2,2,16,128]{4,3,2,1,0:T(8,128)(2,1)S(1)}, u32[]{:S(2)}, u32[]{:S(2)}) collective-permute-start(bf16[3,2,2,16,128]{4,3,2,1,0:T(8,128)(2,1)S(1)} %get-tuple-element.44), channel_id=1, source_target_pairs={{0,48},{1,49},{16,0},{17,1},{32,16},{33,17},{48,32},{49,33},{2,50}... | collective-permute-start | bytes 147464 | tf_op jit(solution)/shard_map/ppermute | solution.py:287
  109.2 4.1 %collective-permute-start.24 = (bf16[3,2,2,16,128]{4,3,2,1,0:T(8,128)(2,1)S(1)}, bf16[3,2,2,16,128]{4,3,2,1,0:T(8,128)(2,1)S(1)}, u32[]{:S(2)}, u32[]{:S(2)}) collective-permute-start(bf16[3,2,2,16,128]{4,3,2,1,0:T(8,128)(2,1)S(1)} %get-tuple-element.45), channel_id=1, source_target_pairs={{0,1},{1,16},{16,17},{17,32},{32,33},{33,48},{48,49},{49,0},{2,3},... | collective-permute-start | bytes 147464 | tf_op jit(solution)/shard_map/ppermute | solution.py:287
  110.4 4.1 %collective-permute-start.25 = (bf16[3,2,2,16,128]{4,3,2,1,0:T(8,128)(2,1)S(1)}, bf16[3,2,2,16,128]{4,3,2,1,0:T(8,128)(2,1)S(1)}, u32[]{:S(2)}, u32[]{:S(2)}) collective-permute-start(bf16[3,2,2,16,128]{4,3,2,1,0:T(8,128)(2,1)S(1)} %get-tuple-element.46), channel_id=1, source_target_pairs={{0,49},{1,0},{16,1},{17,16},{32,17},{33,32},{48,33},{49,48},{2,51}... | collective-permute-start | bytes 147464 | tf_op jit(solution)/shard_map/ppermute | solution.py:287

commit v3 on v2

--- a/solution.py
+++ b/solution.py
@@ -20,6 +20,7 @@
 NX, NROW = 4, 8
 RING = ("zh", "zl")
 FAR = (4, 3, 5, 2, 6, 1, 7)
+NEAR = (1, 2, 3, 4, 5, 6, 7)
 BIG = -float(2**30)
 SCALE = 1.0 / math.sqrt(HD)
 LOG2E = math.log2(math.e)
@@ -29,11 +30,7 @@
 BF, F32 = jnp.bfloat16, jnp.float32
 
 
-def params(**kw):
-    return pltpu.CompilerParams(vmem_limit_bytes=VMEM, **kw)
-
-
-def call(kernel, outs, n_in, name, flops=0, nbytes=1 << 20, scratch=(), where=pltpu.VMEM, after=()):
+def call(kernel, outs, n_in, name, flops=0, nbytes=1 << 20, scratch=(), where=pltpu.VMEM, after=(), limit=VMEM, **more):
     whole = pl.BlockSpec(memory_space=where)
     inner = lambda *refs: kernel(*refs[:n_in], *refs[n_in + len(after) :])
     made = pl.pallas_call(
@@ -42,9 +39,10 @@
         in_specs=[whole] * n_in + [pl.BlockSpec(memory_space=pl.ANY)] * len(after),
         out_specs=jax.tree.map(lambda _: pl.BlockSpec(memory_space=pltpu.VMEM), outs),
         scratch_shapes=list(scratch),
-        compiler_params=params(),
+        compiler_params=pltpu.CompilerParams(vmem_limit_bytes=limit),
         cost_estimate=pl.CostEstimate(flops=flops, bytes_accessed=nbytes, transcendentals=0),
         name=name,
+        **more,
     )
     return lambda *args: made(*args, *after)
 
@@ -273,7 +271,7 @@
 
 def unpack_q(*refs):
     out_ref = refs[-1]
-    for k, in_ref in zip((0,) + FAR, refs[:-1]):
+    for k, in_ref in zip((0,) + NEAR, refs[:-1]):
         src = lax.rem(ring_place() + Z - k, Z)
         for h in range(HL):
             out_ref[:, :, :, head_lanes(src, h)] = in_ref[h]
@@ -283,8 +281,8 @@
     return lax.all_to_all(sends, RING, split_axis=0, concat_axis=0, tiled=True)
 
 
-def exchange_by_steps(sends):
-    return [sends[0]] + [lax.ppermute(sends[k], RING, [(i, (i + k) % Z) for i in range(Z)]) for k in FAR]
+def exchange_by_steps(sends, order):
+    return [sends[0]] + [lax.ppermute(sends[k], RING, [(i, (i + k) % Z) for i in range(Z)]) for k in order]
 
 
 def shift(block, dx, dr):
@@ -311,10 +309,10 @@
     wide = lambda block, n: shape(n, *block.shape)
     whole = shape(F, R, CH, HEADS * HD)
     room = lambda *shapes: [pltpu.VMEM(x.shape, x.dtype) for x in shapes] + [pltpu.SemaphoreType.DMA((len(shapes),))]
-    sent_q = call(pack_q, (q_block,) * Z, 4, "pack_q", scratch=room(whole, whole, whole, log_sums), where=pl.ANY)(
+    sent_q = call(pack_q, (q_block,) * Z, 4, "pack_q", scratch=room(whole, whole, whole, log_sums), where=pl.ANY, limit=60 * 1024 * 1024)(
         queries, grad_out, outputs, log_sums
     )
-    q_got = exchange_by_steps(sent_q)
+    q_got = exchange_by_steps(sent_q, FAR)
     sent_kv = call(
         pack_kv, wide(kv_block, Z), 2, "pack_kv", scratch=room(whole, whole), where=pl.ANY, after=q_got[1:]
     )(key_tokens, values)
@@ -337,9 +335,9 @@
         flops=10**11,
         scratch=[pltpu.VMEM((Z, HL, F, R, CH, HD), BF)],
     )(*kv_seen, q_here)
-    q_back = exchange_by_steps(grads_q)
+    q_back = exchange_by_steps(grads_q, NEAR)
     key_out, value_out = call(unpack_kv, (whole, whole), 1, "unpack_kv")(kv_back)
-    query_out = call(unpack_q, whole, Z, "unpack_q")(*q_back)
+    query_out = call(unpack_q, whole, Z, "unpack_q", after=(key_out,))(*q_back)
     return query_out, key_out, value_out
 
 

time: 117 us -> 113 us (0.966)
  waiting for transfers between devices: 26.2 us -> 21.6 us
  local copies, waits for them, and re-layouts: 4.55 us -> 1.79 us
  Pallas kernels: 18 us -> 20.1 us
  starting transfers between devices: 66.9 us -> 68.6 us
    ppermute x14, waiting for transfers between devices: 13.8 us -> 9.26 us  [exchange_by_steps(): lax.ppermute(sends[k], RING, [(i, (i + k) % Z) for i in range(Z)])]
    unnamed x22 -> x18, local copies, waits for them, and re-layouts: 4.55 us -> 1.79 us
    pallas_call x10, Pallas kernels: 18 us -> 20.1 us  [call(): return lambda *args: made(*args, *after)]
    ppermute x14, starting transfers between devices: 36.8 us -> 38.4 us  [exchange_by_steps(): lax.ppermute(sends[k], RING, [(i, (i + k) % Z) for i in range(Z)])]
  transfers between devices with their start and end apart: 28 -> 28, of which waited for: 10 -> 10; matrix products, arithmetic and copies ran while one was open for 0% -> 0% of each run, Pallas kernels for 12% -> 13%
where the time goes in v3:
time: 113 us
  starting transfers between devices  68.6 us (61%)
  waiting for transfers between devices  21.6 us (19%)
  Pallas kernels  20.1 us (18%)
  local copies, waits for them, and re-layouts  1.79 us (2%)
    ppermute x14, starting transfers between devices, exchange_by_steps(): lax.ppermute(sends[k], RING, [(i, (i + k) % Z) for i in range(Z)])  38.4 us
    pallas_call x10, Pallas kernels, call(): return lambda *args: made(*args, *after)  20.1 us
    ppermute x12, starting transfers between devices, shift(): lax.ppermute(block, ('x', 'row'), [(flat(x + dx, r + dr), flat(x, r)) for...  17 us
    all_to_all x2, starting transfers between devices, exchange(): return lax.all_to_all(sends, RING, split_axis=0, concat_axis=0, tiled=True)  13.1 us
    ppermute x12, waiting for transfers between devices, shift(): lax.ppermute(block, ('x', 'row'), [(flat(x + dx, r + dr), flat(x, r)) for...  12 us
    ppermute x14, waiting for transfers between devices, exchange_by_steps(): lax.ppermute(sends[k], RING, [(i, (i + k) % Z) for i in range(Z)])  9.26 us
  transfers between devices with their start and end apart: 28, of which 10 were waited for; matrix products, arithmetic and copies ran while one was open for 0% of the time, Pallas kernels for 13%

profile of v3, /device:TPU:32, one launch (start us, length us, event | category | flops | bytes accessed | tf_op | source)
XLA Modules:
  0.0 112.9 jit_solution(3743817899922525006)
XLA Ops:
  0.7 2.8 %pack_q.1 = (bf16[7,2,2,16,128]{4,3,2,1,0:T(8,128)(2,1)}, bf16[7,2,2,16,128]{4,3,2,1,0:T(8,128)(2,1)}, bf16[7,2,2,16,128]{4,3,2,1,0:T(8,128)(2,1)}, bf16[7,2,2,1...) custom-call(bf16[2,2,16,3072]{3,2,1,0:T(8,128)(2,1)} %refs_0_.2, ...), custom_call_target="tpu_custom_call" | custom-call | bytes 1048576 | tf_op jit(solution)/shard_map/pack_q/pallas_call | solution.py:47
  3.5 6.4 %collective-permute-start = (bf16[7,2,2,16,128]{4,3,2,1,0:T(8,128)(2,1)}, bf16[7,2,2,16,128]{4,3,2,1,0:T(8,128)(2,1)S(1)}, u32[]{:S(2)}, u32[]{:S(2)}) collective-permute-start(bf16[7,2,2,16,128]{4,3,2,1,0:T(8,128)(2,1)} %get-tuple-element.26), channel_id=1, source_target_pairs={{0,32},{1,33},{16,48},{17,49},{32,0},{33,1},{48,16},{49,17},{2,34}... | collective-permute-start | bytes 344072 | tf_op jit(solution)/shard_map/ppermute | solution.py:285
  9.8 0.0 collective-permute-start.1
  9.9 5.0 %collective-permute-start.2 = (bf16[7,2,2,16,128]{4,3,2,1,0:T(8,128)(2,1)}, bf16[7,2,2,16,128]{4,3,2,1,0:T(8,128)(2,1)S(1)}, u32[]{:S(2)}, u32[]{:S(2)}) collective-permute-start(bf16[7,2,2,16,128]{4,3,2,1,0:T(8,128)(2,1)} %get-tuple-element.28), channel_id=1, source_target_pairs={{0,33},{1,48},{16,49},{17,0},{32,1},{33,16},{48,17},{49,32},{2,35}... | collective-permute-start | bytes 344072 | tf_op jit(solution)/shard_map/ppermute | solution.py:285
  14.9 0.3 collective-permute-start.3
  15.1 3.9 %collective-permute-start.4 = (bf16[7,2,2,16,128]{4,3,2,1,0:T(8,128)(2,1)}, bf16[7,2,2,16,128]{4,3,2,1,0:T(8,128)(2,1)S(1)}, u32[]{:S(2)}, u32[]{:S(2)}) collective-permute-start(bf16[7,2,2,16,128]{4,3,2,1,0:T(8,128)(2,1)} %get-tuple-element.30), channel_id=1, source_target_pairs={{0,48},{1,49},{16,0},{17,1},{32,16},{33,17},{48,32},{49,33},{2,50}... | collective-permute-start | bytes 344072 | tf_op jit(solution)/shard_map/ppermute | solution.py:285
  19.0 0.0 collective-permute-done.refs_2_.refs_1_
  19.0 1.2 %collective-permute-start.5 = (bf16[7,2,2,16,128]{4,3,2,1,0:T(8,128)(2,1)}, bf16[7,2,2,16,128]{4,3,2,1,0:T(8,128)(2,1)S(1)}, u32[]{:S(2)}, u32[]{:S(2)}) collective-permute-start(bf16[7,2,2,16,128]{4,3,2,1,0:T(8,128)(2,1)} %get-tuple-element.31), channel_id=1, source_target_pairs={{0,1},{1,16},{16,17},{17,32},{32,33},{33,48},{48,49},{49,0},{2,3},... | collective-permute-start | bytes 344072 | tf_op jit(solution)/shard_map/ppermute | solution.py:285
  20.2 1.3 %collective-permute-done.1.refs_3_.refs_2_ = bf16[7,2,2,16,128]{4,3,2,1,0:T(8,128)(2,1)S(1)} collective-permute-done((bf16[7,2,2,16,128]{4,3,2,1,0:T(8,128)(2,1)}, bf16[7,2,2,16,128]{4,3,2,1,0:T(8,128)(2,1)S(1)}, u32[]{:S(2)}, u32[]{:S(2)}) %collective-permute-start.1) | collective-permute-done | bytes 114720 | tf_op jit(solution)/shard_map/ppermute | solution.py:285
  21.6 4.5 %collective-permute-start.6 = (bf16[7,2,2,16,128]{4,3,2,1,0:T(8,128)(2,1)}, bf16[7,2,2,16,128]{4,3,2,1,0:T(8,128)(2,1)S(1)}, u32[]{:S(2)}, u32[]{:S(2)}) collective-permute-start(bf16[7,2,2,16,128]{4,3,2,1,0:T(8,128)(2,1)} %get-tuple-element.32), channel_id=1, source_target_pairs={{0,49},{1,0},{16,1},{17,16},{32,17},{33,32},{48,33},{49,48},{2,51}... | collective-permute-start | bytes 344072 | tf_op jit(solution)/shard_map/ppermute | solution.py:285
  26.1 0.0 collective-permute-done.2.refs_4_.refs_3_
  26.1 2.7 %collective-permute-done.3.refs_5_.refs_4_ = bf16[7,2,2,16,128]{4,3,2,1,0:T(8,128)(2,1)S(1)} collective-permute-done((bf16[7,2,2,16,128]{4,3,2,1,0:T(8,128)(2,1)}, bf16[7,2,2,16,128]{4,3,2,1,0:T(8,128)(2,1)S(1)}, u32[]{:S(2)}, u32[]{:S(2)}) %collective-permute-start.3) | collective-permute-done | bytes 114720 | tf_op jit(solution)/shard_map/ppermute | solution.py:285
  28.8 0.0 collective-permute-done.4.refs_6_.refs_5_
  28.8 1.6 %collective-permute-done.5.refs_7_.refs_6_ = bf16[7,2,2,16,128]{4,3,2,1,0:T(8,128)(2,1)S(1)} collective-permute-done((bf16[7,2,2,16,128]{4,3,2,1,0:T(8,128)(2,1)}, bf16[7,2,2,16,128]{4,3,2,1,0:T(8,128)(2,1)S(1)}, u32[]{:S(2)}, u32[]{:S(2)}) %collective-permute-start.5) | collective-permute-done | bytes 114720 | tf_op jit(solution)/shard_map/ppermute | solution.py:285
  30.4 0.5 collective-permute-done.6.refs_8_.refs_7_
  30.9 1.4 %pack_kv.1 = bf16[8,6,2,2,16,128]{5,4,3,2,1,0:T(8,128)(2,1)} custom-call(bf16[2,2,16,3072]{3,2,1,0:T(8,128)(2,1)S(1)} %copy-done.2, bf16[2,2,16,3072]{3,2,1,0:T(8,128)(2,1)S(1)} %copy-done.3, bf16[7,2,2,16,128]{4,3,2,1,0:T(8,128)(2,1)S(1)} %collective-permute-done.refs_2_.refs_1_, bf16[7,2,2,16,128]{4,3,2,1,0:T(8,128)(2,1)S(1)} %collective-permute-done.1.refs_3_.refs_2_, ...), custom_call_target="tpu_custom_call" | custom-call | bytes 1048576 | tf_op jit(solution)/shard_map/pack_kv/pallas_call | solution.py:47
  32.3 0.0 copy-start.5
  32.4 6.3 %all-to-all-start = ((bf16[8,6,2,2,16,128]{5,4,3,2,1,0:T(8,128)(2,1)}), bf16[8,6,2,2,16,128]{5,4,3,2,1,0:T(8,128)(2,1)S(1)}, u32[]{:S(2)}, u32[]{:S(2)}) async-start(bf16[8,6,2,2,16,128]{5,4,3,2,1,0:T(8,128)(2,1)} %pack_kv.1), calls=%async_computation | async-start | bytes 1572864 | tf_op jit(solution)/shard_map/all_to_all | solution.py:281
  38.6 0.4 gather_q.1
  39.0 1.6 %collective-permute-start.10 = (bf16[8,7,2,2,16,128]{5,4,3,2,1,0:T(8,128)(2,1)S(1)}, bf16[8,7,2,2,16,128]{5,4,3,2,1,0:T(8,128)(2,1)S(1)}, u32[]{:S(2)}, u32[]{:S(2)}) collective-permute-start(bf16[8,7,2,2,16,128]{5,4,3,2,1,0:T(8,128)(2,1)S(1)} %get-tuple-element.34.refs_1_.refs_6_), channel_id=1, source_target_pairs={{2,0},{4,2},{6,4},{8,6},{10,8},{12,10},{14,12},{0,14},{66,64},{68,... | collective-permute-start | bytes 2752520 | tf_op jit(solution)/shard_map/ppermute | solution.py:291
  40.6 0.0 collective-permute-start.9
  40.7 1.5 %collective-permute-start.11 = (bf16[2,7,2,2,16,128]{5,4,3,2,1,0:T(8,128)(2,1)S(1)}, bf16[2,7,2,2,16,128]{5,4,3,2,1,0:T(8,128)(2,1)S(1)}, u32[]{:S(2)}, u32[]{:S(2)}) collective-permute-start(bf16[2,7,2,2,16,128]{5,4,3,2,1,0:T(8,128)(2,1)S(1)} %get-tuple-element.35), channel_id=1, source_target_pairs={{192,0},{194,2},{196,4},{198,6},{200,8},{202,10},{204,12},{206,14}... | collective-permute-start | bytes 688136 | tf_op jit(solution)/shard_map/ppermute | solution.py:291
  42.1 1.7 %collective-permute-start.12 = (bf16[2,7,2,2,16,128]{5,4,3,2,1,0:T(8,128)(2,1)S(1)}, bf16[2,7,2,2,16,128]{5,4,3,2,1,0:T(8,128)(2,1)S(1)}, u32[]{:S(2)}, u32[]{:S(2)}) collective-permute-start(bf16[2,7,2,2,16,128]{5,4,3,2,1,0:T(8,128)(2,1)S(1)} %get-tuple-element.36), channel_id=1, source_target_pairs={{64,0},{66,2},{68,4},{70,6},{72,8},{74,10},{76,12},{78,14},{128,64... | collective-permute-start | bytes 688136 | tf_op jit(solution)/shard_map/ppermute | solution.py:291
  43.9 5.6 %collective-permute-done.11.refs_0_ = bf16[2,7,2,2,16,128]{5,4,3,2,1,0:T(8,128)(2,1)S(1)} collective-permute-done((bf16[2,7,2,2,16,128]{5,4,3,2,1,0:T(8,128)(2,1)S(1)}, bf16[2,7,2,2,16,128]{5,4,3,2,1,0:T(8,128)(2,1)S(1)}, u32[]{:S(2)}, u32[]{:S(2)}) %collective-permute-start.11) | collective-permute-done | bytes 229408 | tf_op jit(solution)/shard_map/ppermute | solution.py:291
  49.5 0.0 collective-permute-done.12.refs_1_
  49.5 0.0 collective-permute-start.13
  49.5 2.9 %collective-permute-start.14 = (bf16[4,7,2,2,16,128]{5,4,3,2,1,0:T(8,128)(2,1)S(1)}, bf16[4,7,2,2,16,128]{5,4,3,2,1,0:T(8,128)(2,1)S(1)}, u32[]{:S(2)}, u32[]{:S(2)}) collective-permute-start(bf16[4,7,2,2,16,128]{5,4,3,2,1,0:T(8,128)(2,1)S(1)} %join_q.1.refs_4_), channel_id=1, source_target_pairs={{2,0},{4,2},{6,4},{8,6},{10,8},{12,10},{14,12},{0,14},{66,64},{68,... | collective-permute-start | bytes 1376264 | tf_op jit(solution)/shard_map/ppermute | solution.py:291
  52.5 0.8 copy-done
  53.3 6.3 %collective-permute-done.13.refs_3_ = bf16[4,7,2,2,16,128]{5,4,3,2,1,0:T(8,128)(2,1)S(1)} collective-permute-done((bf16[4,7,2,2,16,128]{5,4,3,2,1,0:T(8,128)(2,1)S(1)}, bf16[4,7,2,2,16,128]{5,4,3,2,1,0:T(8,128)(2,1)S(1)}, u32[]{:S(2)}, u32[]{:S(2)}) %collective-permute-start.13) | collective-permute-done | bytes 458784 | tf_op jit(solution)/shard_map/ppermute | solution.py:291
  59.6 0.0 collective-permute-done.14.refs_4_.refs_5_
  59.6 0.0 collective-permute-done.10.refs_2_
  59.6 0.0 collective-permute-done.9.refs_1_.refs_0_
  59.6 0.4 all-to-all-done.refs_0_.refs_6_.refs_1_
  60.0 1.6 %collective-permute-start.15 = (bf16[2,6,2,2,16,128]{5,4,3,2,1,0:T(8,128)(2,1)S(1)}, bf16[2,6,2,2,16,128]{5,4,3,2,1,0:T(8,128)(2,1)S(1)}, u32[]{:S(2)}, u32[]{:S(2)}) collective-permute-start(bf16[2,6,2,2,16,128]{5,4,3,2,1,0:T(8,128)(2,1)S(1)} %get-tuple-element.37), channel_id=1, source_target_pairs={{192,0},{194,2},{196,4},{198,6},{200,8},{202,10},{204,12},{206,14}... | collective-permute-start | bytes 589832 | tf_op jit(solution)/shard_map/ppermute | solution.py:291
  61.6 1.7 %collective-permute-start.16 = (bf16[2,6,2,2,16,128]{5,4,3,2,1,0:T(8,128)(2,1)S(1)}, bf16[2,6,2,2,16,128]{5,4,3,2,1,0:T(8,128)(2,1)S(1)}, u32[]{:S(2)}, u32[]{:S(2)}) collective-permute-start(bf16[2,6,2,2,16,128]{5,4,3,2,1,0:T(8,128)(2,1)S(1)} %get-tuple-element.38), channel_id=1, source_target_pairs={{64,0},{66,2},{68,4},{70,6},{72,8},{74,10},{76,12},{78,14},{128,64... | collective-permute-start | bytes 589832 | tf_op jit(solution)/shard_map/ppermute | solution.py:291
  63.3 0.0 collective-permute-start.7
  63.3 3.0 %collective-permute-start.8 = (bf16[8,6,2,2,16,128]{5,4,3,2,1,0:T(8,128)(2,1)S(1)}, bf16[8,6,2,2,16,128]{5,4,3,2,1,0:T(8,128)(2,1)}, u32[]{:S(2)}, u32[]{:S(2)}) collective-permute-start(bf16[8,6,2,2,16,128]{5,4,3,2,1,0:T(8,128)(2,1)S(1)} %all-to-all-done.refs_0_.refs_6_.refs_1_), channel_id=1, source_target_pairs={{2,0},{4,2},{6,4},{8,6},{10,8},{12,10},{14,12},{0,14},{66,64},{68,... | collective-permute-start | bytes 2359304 | tf_op jit(solution)/shard_map/ppermute | solution.py:291
  66.3 6.6 %key_grads.1.refs_2_ = bf16[8,6,2,2,16,128]{5,4,3,2,1,0:T(8,128)(2,1)} custom-call(bf16[8,7,2,2,16,128]{5,4,3,2,1,0:T(8,128)(2,1)S(1)} %collective-permute-done.9.refs_1_.refs_0_, bf16[8,7,2,2,16,128]{5,4,3,2,1,0:T(8,128)(2,1)S(1)} %copy-done.7, bf16[8,7,2,2,16,128]{5,4,3,2,1,0:T(8,128)(2,1)S(1)} %collective-permute-done.10.refs_2_, ...), custom_call_target="tpu_custom_call" | custom-call | flops 10000000000 | bytes 1048576 | tf_op jit(solution)/shard_map/key_grads/pallas_call | solution.py:47
  72.9 0.0 collective-permute-done.15.refs_0_
  72.9 0.0 collective-permute-done.16.refs_1_
  72.9 0.0 collective-permute-start.17
  72.9 2.9 %collective-permute-start.18 = (bf16[4,6,2,2,16,128]{5,4,3,2,1,0:T(8,128)(2,1)S(1)}, bf16[4,6,2,2,16,128]{5,4,3,2,1,0:T(8,128)(2,1)}, u32[]{:S(2)}, u32[]{:S(2)}) collective-permute-start(bf16[4,6,2,2,16,128]{5,4,3,2,1,0:T(8,128)(2,1)S(1)} %join_kv.1.refs_4_), channel_id=1, source_target_pairs={{2,0},{4,2},{6,4},{8,6},{10,8},{12,10},{14,12},{0,14},{66,64},{68,... | collective-permute-start | bytes 1179656 | tf_op jit(solution)/shard_map/ppermute | solution.py:291
  75.9 6.9 %all-to-all-start.1 = ((bf16[8,6,2,2,16,128]{5,4,3,2,1,0:T(8,128)(2,1)}), bf16[8,6,2,2,16,128]{5,4,3,2,1,0:T(8,128)(2,1)S(1)}, u32[]{:S(2)}, u32[]{:S(2)}) async-start(bf16[8,6,2,2,16,128]{5,4,3,2,1,0:T(8,128)(2,1)} %key_grads.1.refs_2_), calls=%async_computation.1 | async-start | bytes 1572864 | tf_op jit(solution)/shard_map/all_to_all | solution.py:281
  82.8 0.0 collective-permute-done.17.refs_3_
  82.8 0.0 collective-permute-done.18.refs_5_
  82.8 0.0 collective-permute-done.7.refs_0_
  82.8 0.0 collective-permute-done.8.refs_2_
  82.8 7.0 %query_grads.1 = (bf16[3,2,2,16,128]{4,3,2,1,0:T(8,128)(2,1)S(1)}, bf16[3,2,2,16,128]{4,3,2,1,0:T(8,128)(2,1)S(1)}, bf16[3,2,2,16,128]{4,3,2,1,0:T(8,128)(2,1)S(...) custom-call(bf16[8,6,2,2,16,128]{5,4,3,2,1,0:T(8,128)(2,1)} %collect, ...), custom_call_target="tpu_custom_call" | custom-call | flops 99999997952 | bytes 1048576 | tf_op jit(solution)/shard_map/query_grads/pallas_call | solution.py:47
  89.8 1.5 %collective-permute-start.19 = (bf16[3,2,2,16,128]{4,3,2,1,0:T(8,128)(2,1)S(1)}, bf16[3,2,2,16,128]{4,3,2,1,0:T(8,128)(2,1)S(1)}, u32[]{:S(2)}, u32[]{:S(2)}) collective-permute-start(bf16[3,2,2,16,128]{4,3,2,1,0:T(8,128)(2,1)S(1)} %get-tuple-element.40), channel_id=1, source_target_pairs={{0,1},{1,16},{16,17},{17,32},{32,33},{33,48},{48,49},{49,0},{2,3},... | collective-permute-start | bytes 147464 | tf_op jit(solution)/shard_map/ppermute | solution.py:285
  91.2 3.6 %collective-permute-start.20 = (bf16[3,2,2,16,128]{4,3,2,1,0:T(8,128)(2,1)S(1)}, bf16[3,2,2,16,128]{4,3,2,1,0:T(8,128)(2,1)S(1)}, u32[]{:S(2)}, u32[]{:S(2)}) collective-permute-start(bf16[3,2,2,16,128]{4,3,2,1,0:T(8,128)(2,1)S(1)} %get-tuple-element.41), channel_id=1, source_target_pairs={{0,16},{1,17},{16,32},{17,33},{32,48},{33,49},{48,0},{49,1},{2,18}... | collective-permute-start | bytes 147464 | tf_op jit(solution)/shard_map/ppermute | solution.py:285
  94.8 0.6 collective-permute-start.21
  95.4 3.2 %collective-permute-start.22 = (bf16[3,2,2,16,128]{4,3,2,1,0:T(8,128)(2,1)S(1)}, bf16[3,2,2,16,128]{4,3,2,1,0:T(8,128)(2,1)S(1)}, u32[]{:S(2)}, u32[]{:S(2)}) collective-permute-start(bf16[3,2,2,16,128]{4,3,2,1,0:T(8,128)(2,1)S(1)} %get-tuple-element.43), channel_id=1, source_target_pairs={{0,32},{1,33},{16,48},{17,49},{32,0},{33,1},{48,16},{49,17},{2,34}... | collective-permute-start | bytes 147464 | tf_op jit(solution)/shard_map/ppermute | solution.py:285
  98.6 1.2 %collective-permute-start.23 = (bf16[3,2,2,16,128]{4,3,2,1,0:T(8,128)(2,1)S(1)}, bf16[3,2,2,16,128]{4,3,2,1,0:T(8,128)(2,1)S(1)}, u32[]{:S(2)}, u32[]{:S(2)}) collective-permute-start(bf16[3,2,2,16,128]{4,3,2,1,0:T(8,128)(2,1)S(1)} %get-tuple-element.44), channel_id=1, source_target_pairs={{0,33},{1,48},{16,49},{17,0},{32,1},{33,16},{48,17},{49,32},{2,35}... | collective-permute-start | bytes 147464 | tf_op jit(solution)/shard_map/ppermute | solution.py:285
  99.9 0.7 collective-permute-done.19.refs_1_
  100.6 6.3 %collective-permute-start.24 = (bf16[3,2,2,16,128]{4,3,2,1,0:T(8,128)(2,1)S(1)}, bf16[3,2,2,16,128]{4,3,2,1,0:T(8,128)(2,1)S(1)}, u32[]{:S(2)}, u32[]{:S(2)}) collective-permute-start(bf16[3,2,2,16,128]{4,3,2,1,0:T(8,128)(2,1)S(1)} %get-tuple-element.45), channel_id=1, source_target_pairs={{0,48},{1,49},{16,0},{17,1},{32,16},{33,17},{48,32},{49,33},{2,50}... | collective-permute-start | bytes 147464 | tf_op jit(solution)/shard_map/ppermute | solution.py:285
  106.9 0.0 collective-permute-done.20.refs_2_
  106.9 0.7 collective-permute-start.25
  107.6 0.0 all-to-all-done.1.refs_0_
  107.6 1.0 unpack_kv.1
  108.7 0.0 collective-permute-done.21.refs_3_
  108.7 0.5 collective-permute-done.24.refs_6_
  109.1 1.9 %collective-permute-done.25.refs_7_ = bf16[3,2,2,16,128]{4,3,2,1,0:T(8,128)(2,1)S(1)} collective-permute-done((bf16[3,2,2,16,128]{4,3,2,1,0:T(8,128)(2,1)S(1)}, bf16[3,2,2,16,128]{4,3,2,1,0:T(8,128)(2,1)S(1)}, u32[]{:S(2)}, u32[]{:S(2)}) %collective-permute-start.25) | collective-permute-done | bytes 49184 | tf_op jit(solution)/shard_map/ppermute | solution.py:285
  111.0 1.0 copy-done.4
  112.0 0.8 unpack_q.1
  (20 shorter events, 0.1 us)
Async XLA Ops:
  0.6 30.3 %copy-start.2 = (bf16[2,2,16,3072]{3,2,1,0:T(8,128)(2,1)S(1)}, bf16[2,2,16,3072]{3,2,1,0:T(8,128)(2,1)}, u32[]{:S(2)}) copy-start(bf16[2,2,16,3072]{3,2,1,0:T(8,128)(2,1)} %refs_0_.3) | copy-start | bytes 1179652
  0.6 30.3 %copy-start.3 = (bf16[2,2,16,3072]{3,2,1,0:T(8,128)(2,1)S(1)}, bf16[2,2,16,3072]{3,2,1,0:T(8,128)(2,1)}, u32[]{:S(2)}) copy-start(bf16[2,2,16,3072]{3,2,1,0:T(8,128)(2,1)} %refs_1_.3) | copy-start | bytes 1179652
  3.5 15.6 %collective-permute-start = (bf16[7,2,2,16,128]{4,3,2,1,0:T(8,128)(2,1)}, bf16[7,2,2,16,128]{4,3,2,1,0:T(8,128)(2,1)S(1)}, u32[]{:S(2)}, u32[]{:S(2)}) collective-permute-start(bf16[7,2,2,16,128]{4,3,2,1,0:T(8,128)(2,1)} %get-tuple-element.26), channel_id=1, source_target_pairs={{0,32},{1,33},{16,48},{17,49},{32,0},{33,1},{48,16},{49,17},{2,34}... | collective-permute-start | bytes 344072 | tf_op jit(solution)/shard_map/ppermute | solution.py:285
  9.8 11.7 %collective-permute-start.1 = (bf16[7,2,2,16,128]{4,3,2,1,0:T(8,128)(2,1)}, bf16[7,2,2,16,128]{4,3,2,1,0:T(8,128)(2,1)S(1)}, u32[]{:S(2)}, u32[]{:S(2)}) collective-permute-start(bf16[7,2,2,16,128]{4,3,2,1,0:T(8,128)(2,1)} %get-tuple-element.27), channel_id=1, source_target_pairs={{0,17},{1,32},{16,33},{17,48},{32,49},{33,0},{48,1},{49,16},{2,19}... | collective-permute-start | bytes 344072 | tf_op jit(solution)/shard_map/ppermute | solution.py:285
  9.9 16.2 %collective-permute-start.2 = (bf16[7,2,2,16,128]{4,3,2,1,0:T(8,128)(2,1)}, bf16[7,2,2,16,128]{4,3,2,1,0:T(8,128)(2,1)S(1)}, u32[]{:S(2)}, u32[]{:S(2)}) collective-permute-start(bf16[7,2,2,16,128]{4,3,2,1,0:T(8,128)(2,1)} %get-tuple-element.28), channel_id=1, source_target_pairs={{0,33},{1,48},{16,49},{17,0},{32,1},{33,16},{48,17},{49,32},{2,35}... | collective-permute-start | bytes 344072 | tf_op jit(solution)/shard_map/ppermute | solution.py:285
  14.9 13.9 %collective-permute-start.3 = (bf16[7,2,2,16,128]{4,3,2,1,0:T(8,128)(2,1)}, bf16[7,2,2,16,128]{4,3,2,1,0:T(8,128)(2,1)S(1)}, u32[]{:S(2)}, u32[]{:S(2)}) collective-permute-start(bf16[7,2,2,16,128]{4,3,2,1,0:T(8,128)(2,1)} %get-tuple-element.29), channel_id=1, source_target_pairs={{0,16},{1,17},{16,32},{17,33},{32,48},{33,49},{48,0},{49,1},{2,18}... | collective-permute-start | bytes 344072 | tf_op jit(solution)/shard_map/ppermute | solution.py:285
  15.1 13.7 %collective-permute-start.4 = (bf16[7,2,2,16,128]{4,3,2,1,0:T(8,128)(2,1)}, bf16[7,2,2,16,128]{4,3,2,1,0:T(8,128)(2,1)S(1)}, u32[]{:S(2)}, u32[]{:S(2)}) collective-permute-start(bf16[7,2,2,16,128]{4,3,2,1,0:T(8,128)(2,1)} %get-tuple-element.30), channel_id=1, source_target_pairs={{0,48},{1,49},{16,0},{17,1},{32,16},{33,17},{48,32},{49,33},{2,50}... | collective-permute-start | bytes 344072 | tf_op jit(solution)/shard_map/ppermute | solution.py:285
  19.0 11.4 %collective-permute-start.5 = (bf16[7,2,2,16,128]{4,3,2,1,0:T(8,128)(2,1)}, bf16[7,2,2,16,128]{4,3,2,1,0:T(8,128)(2,1)S(1)}, u32[]{:S(2)}, u32[]{:S(2)}) collective-permute-start(bf16[7,2,2,16,128]{4,3,2,1,0:T(8,128)(2,1)} %get-tuple-element.31), channel_id=1, source_target_pairs={{0,1},{1,16},{16,17},{17,32},{32,33},{33,48},{48,49},{49,0},{2,3},... | collective-permute-start | bytes 344072 | tf_op jit(solution)/shard_map/ppermute | solution.py:285
  21.6 9.3 %collective-permute-start.6 = (bf16[7,2,2,16,128]{4,3,2,1,0:T(8,128)(2,1)}, bf16[7,2,2,16,128]{4,3,2,1,0:T(8,128)(2,1)S(1)}, u32[]{:S(2)}, u32[]{:S(2)}) collective-permute-start(bf16[7,2,2,16,128]{4,3,2,1,0:T(8,128)(2,1)} %get-tuple-element.32), channel_id=1, source_target_pairs={{0,49},{1,0},{16,1},{17,16},{32,17},{33,32},{48,33},{49,48},{2,51}... | collective-permute-start | bytes 344072 | tf_op jit(solution)/shard_map/ppermute | solution.py:285
  32.3 6.3 %copy-start.5 = (bf16[7,2,2,16,128]{4,3,2,1,0:T(8,128)(2,1)S(1)}, bf16[7,2,2,16,128]{4,3,2,1,0:T(8,128)(2,1)}, u32[]{:S(2)}) copy-start(bf16[7,2,2,16,128]{4,3,2,1,0:T(8,128)(2,1)} %get-tuple-element.33.refs_0_) | copy-start | bytes 344068
  32.4 27.6 %all-to-all-start = ((bf16[8,6,2,2,16,128]{5,4,3,2,1,0:T(8,128)(2,1)}), bf16[8,6,2,2,16,128]{5,4,3,2,1,0:T(8,128)(2,1)S(1)}, u32[]{:S(2)}, u32[]{:S(2)}) async-start(bf16[8,6,2,2,16,128]{5,4,3,2,1,0:T(8,128)(2,1)} %pack_kv.1), calls=%async_computation | async-start | bytes 1572864 | tf_op jit(solution)/shard_map/all_to_all | solution.py:281
  39.0 20.6 %copy-start.6 = (bf16[8,7,2,2,16,128]{5,4,3,2,1,0:T(8,128)(2,1)}, bf16[8,7,2,2,16,128]{5,4,3,2,1,0:T(8,128)(2,1)S(1)}, u32[]{:S(2)}) copy-start(bf16[8,7,2,2,16,128]{5,4,3,2,1,0:T(8,128)(2,1)S(1)} %get-tuple-element.34.refs_1_.refs_6_) | copy-start | bytes 2752516
  39.0 20.6 %collective-permute-start.10 = (bf16[8,7,2,2,16,128]{5,4,3,2,1,0:T(8,128)(2,1)S(1)}, bf16[8,7,2,2,16,128]{5,4,3,2,1,0:T(8,128)(2,1)S(1)}, u32[]{:S(2)}, u32[]{:S(2)}) collective-permute-start(bf16[8,7,2,2,16,128]{5,4,3,2,1,0:T(8,128)(2,1)S(1)} %get-tuple-element.34.refs_1_.refs_6_), channel_id=1, source_target_pairs={{2,0},{4,2},{6,4},{8,6},{10,8},{12,10},{14,12},{0,14},{66,64},{68,... | collective-permute-start | bytes 2752520 | tf_op jit(solution)/shard_map/ppermute | solution.py:291
  40.6 19.0 %collective-permute-start.9 = (bf16[8,7,2,2,16,128]{5,4,3,2,1,0:T(8,128)(2,1)S(1)}, bf16[8,7,2,2,16,128]{5,4,3,2,1,0:T(8,128)(2,1)S(1)}, u32[]{:S(2)}, u32[]{:S(2)}) collective-permute-start(bf16[8,7,2,2,16,128]{5,4,3,2,1,0:T(8,128)(2,1)S(1)} %get-tuple-element.34.refs_1_.refs_6_), channel_id=1, source_target_pairs={{14,0},{0,2},{2,4},{4,6},{6,8},{8,10},{10,12},{12,14},{78,64},{64,... | collective-permute-start | bytes 2752520 | tf_op jit(solution)/shard_map/ppermute | solution.py:291
  40.7 8.8 %collective-permute-start.11 = (bf16[2,7,2,2,16,128]{5,4,3,2,1,0:T(8,128)(2,1)S(1)}, bf16[2,7,2,2,16,128]{5,4,3,2,1,0:T(8,128)(2,1)S(1)}, u32[]{:S(2)}, u32[]{:S(2)}) collective-permute-start(bf16[2,7,2,2,16,128]{5,4,3,2,1,0:T(8,128)(2,1)S(1)} %get-tuple-element.35), channel_id=1, source_target_pairs={{192,0},{194,2},{196,4},{198,6},{200,8},{202,10},{204,12},{206,14}... | collective-permute-start | bytes 688136 | tf_op jit(solution)/shard_map/ppermute | solution.py:291
  42.1 7.3 %collective-permute-start.12 = (bf16[2,7,2,2,16,128]{5,4,3,2,1,0:T(8,128)(2,1)S(1)}, bf16[2,7,2,2,16,128]{5,4,3,2,1,0:T(8,128)(2,1)S(1)}, u32[]{:S(2)}, u32[]{:S(2)}) collective-permute-start(bf16[2,7,2,2,16,128]{5,4,3,2,1,0:T(8,128)(2,1)S(1)} %get-tuple-element.36), channel_id=1, source_target_pairs={{64,0},{66,2},{68,4},{70,6},{72,8},{74,10},{76,12},{78,14},{128,64... | collective-permute-start | bytes 688136 | tf_op jit(solution)/shard_map/ppermute | solution.py:291
  49.5 10.1 %collective-permute-start.13 = (bf16[4,7,2,2,16,128]{5,4,3,2,1,0:T(8,128)(2,1)S(1)}, bf16[4,7,2,2,16,128]{5,4,3,2,1,0:T(8,128)(2,1)S(1)}, u32[]{:S(2)}, u32[]{:S(2)}) collective-permute-start(bf16[4,7,2,2,16,128]{5,4,3,2,1,0:T(8,128)(2,1)S(1)} %join_q.1.refs_4_), channel_id=1, source_target_pairs={{14,0},{0,2},{2,4},{4,6},{6,8},{8,10},{10,12},{12,14},{78,64},{64,... | collective-permute-start | bytes 1376264 | tf_op jit(solution)/shard_map/ppermute | solution.py:291
  49.5 10.1 %collective-permute-start.14 = (bf16[4,7,2,2,16,128]{5,4,3,2,1,0:T(8,128)(2,1)S(1)}, bf16[4,7,2,2,16,128]{5,4,3,2,1,0:T(8,128)(2,1)S(1)}, u32[]{:S(2)}, u32[]{:S(2)}) collective-permute-start(bf16[4,7,2,2,16,128]{5,4,3,2,1,0:T(8,128)(2,1)S(1)} %join_q.1.refs_4_), channel_id=1, source_target_pairs={{2,0},{4,2},{6,4},{8,6},{10,8},{12,10},{14,12},{0,14},{66,64},{68,... | collective-permute-start | bytes 1376264 | tf_op jit(solution)/shard_map/ppermute | solution.py:291
  52.5 0.8 copy-start
  60.0 6.3 %copy-start.1 = (bf16[4,7,2,2,16,128]{5,4,3,2,1,0:T(8,128)(2,1)S(1)}, bf16[4,7,2,2,16,128]{5,4,3,2,1,0:T(8,128)(2,1)}, u32[]{:S(2)}) copy-start(bf16[4,7,2,2,16,128]{5,4,3,2,1,0:T(8,128)(2,1)} %copy-done) | copy-start | bytes 1376260
  60.0 6.3 %copy-start.7 = (bf16[8,7,2,2,16,128]{5,4,3,2,1,0:T(8,128)(2,1)S(1)}, bf16[8,7,2,2,16,128]{5,4,3,2,1,0:T(8,128)(2,1)}, u32[]{:S(2)}) copy-start(bf16[8,7,2,2,16,128]{5,4,3,2,1,0:T(8,128)(2,1)} %copy-done.6) | copy-start | bytes 2752516
  60.0 12.9 %collective-permute-start.15 = (bf16[2,6,2,2,16,128]{5,4,3,2,1,0:T(8,128)(2,1)S(1)}, bf16[2,6,2,2,16,128]{5,4,3,2,1,0:T(8,128)(2,1)S(1)}, u32[]{:S(2)}, u32[]{:S(2)}) collective-permute-start(bf16[2,6,2,2,16,128]{5,4,3,2,1,0:T(8,128)(2,1)S(1)} %get-tuple-element.37), channel_id=1, source_target_pairs={{192,0},{194,2},{196,4},{198,6},{200,8},{202,10},{204,12},{206,14}... | collective-permute-start | bytes 589832 | tf_op jit(solution)/shard_map/ppermute | solution.py:291
  61.6 11.3 %collective-permute-start.16 = (bf16[2,6,2,2,16,128]{5,4,3,2,1,0:T(8,128)(2,1)S(1)}, bf16[2,6,2,2,16,128]{5,4,3,2,1,0:T(8,128)(2,1)S(1)}, u32[]{:S(2)}, u32[]{:S(2)}) collective-permute-start(bf16[2,6,2,2,16,128]{5,4,3,2,1,0:T(8,128)(2,1)S(1)} %get-tuple-element.38), channel_id=1, source_target_pairs={{64,0},{66,2},{68,4},{70,6},{72,8},{74,10},{76,12},{78,14},{128,64... | collective-permute-start | bytes 589832 | tf_op jit(solution)/shard_map/ppermute | solution.py:291
  63.3 19.4 %collective-permute-start.7 = (bf16[8,6,2,2,16,128]{5,4,3,2,1,0:T(8,128)(2,1)S(1)}, bf16[8,6,2,2,16,128]{5,4,3,2,1,0:T(8,128)(2,1)}, u32[]{:S(2)}, u32[]{:S(2)}) collective-permute-start(bf16[8,6,2,2,16,128]{5,4,3,2,1,0:T(8,128)(2,1)S(1)} %all-to-all-done.refs_0_.refs_6_.refs_1_), channel_id=1, source_target_pairs={{14,0},{0,2},{2,4},{4,6},{6,8},{8,10},{10,12},{12,14},{78,64},{64,... | collective-permute-start | bytes 2359304 | tf_op jit(solution)/shard_map/ppermute | solution.py:291
  63.3 19.4 %collective-permute-start.8 = (bf16[8,6,2,2,16,128]{5,4,3,2,1,0:T(8,128)(2,1)S(1)}, bf16[8,6,2,2,16,128]{5,4,3,2,1,0:T(8,128)(2,1)}, u32[]{:S(2)}, u32[]{:S(2)}) collective-permute-start(bf16[8,6,2,2,16,128]{5,4,3,2,1,0:T(8,128)(2,1)S(1)} %all-to-all-done.refs_0_.refs_6_.refs_1_), channel_id=1, source_target_pairs={{2,0},{4,2},{6,4},{8,6},{10,8},{12,10},{14,12},{0,14},{66,64},{68,... | collective-permute-start | bytes 2359304 | tf_op jit(solution)/shard_map/ppermute | solution.py:291
  72.9 9.9 %copy-start.8 = (bf16[8,7,2,2,16,128]{5,4,3,2,1,0:T(8,128)(2,1)S(1)}, bf16[8,7,2,2,16,128]{5,4,3,2,1,0:T(8,128)(2,1)}, u32[]{:S(2)}) copy-start(bf16[8,7,2,2,16,128]{5,4,3,2,1,0:T(8,128)(2,1)} %copy-done.6) | copy-start | bytes 2752516
  72.9 9.8 %collective-permute-start.17 = (bf16[4,6,2,2,16,128]{5,4,3,2,1,0:T(8,128)(2,1)S(1)}, bf16[4,6,2,2,16,128]{5,4,3,2,1,0:T(8,128)(2,1)S(1)}, u32[]{:S(2)}, u32[]{:S(2)}) collective-permute-start(bf16[4,6,2,2,16,128]{5,4,3,2,1,0:T(8,128)(2,1)S(1)} %join_kv.1.refs_4_), channel_id=1, source_target_pairs={{14,0},{0,2},{2,4},{4,6},{6,8},{8,10},{10,12},{12,14},{78,64},{64,... | collective-permute-start | bytes 1179656 | tf_op jit(solution)/shard_map/ppermute | solution.py:291
  72.9 9.8 %collective-permute-start.18 = (bf16[4,6,2,2,16,128]{5,4,3,2,1,0:T(8,128)(2,1)S(1)}, bf16[4,6,2,2,16,128]{5,4,3,2,1,0:T(8,128)(2,1)}, u32[]{:S(2)}, u32[]{:S(2)}) collective-permute-start(bf16[4,6,2,2,16,128]{5,4,3,2,1,0:T(8,128)(2,1)S(1)} %join_kv.1.refs_4_), channel_id=1, source_target_pairs={{2,0},{4,2},{6,4},{8,6},{10,8},{12,10},{14,12},{0,14},{66,64},{68,... | collective-permute-start | bytes 1179656 | tf_op jit(solution)/shard_map/ppermute | solution.py:291
  75.9 31.8 %all-to-all-start.1 = ((bf16[8,6,2,2,16,128]{5,4,3,2,1,0:T(8,128)(2,1)}), bf16[8,6,2,2,16,128]{5,4,3,2,1,0:T(8,128)(2,1)S(1)}, u32[]{:S(2)}, u32[]{:S(2)}) async-start(bf16[8,6,2,2,16,128]{5,4,3,2,1,0:T(8,128)(2,1)} %key_grads.1.refs_2_), calls=%async_computation.1 | async-start | bytes 1572864 | tf_op jit(solution)/shard_map/all_to_all | solution.py:281
  89.8 10.8 %collective-permute-start.19 = (bf16[3,2,2,16,128]{4,3,2,1,0:T(8,128)(2,1)S(1)}, bf16[3,2,2,16,128]{4,3,2,1,0:T(8,128)(2,1)S(1)}, u32[]{:S(2)}, u32[]{:S(2)}) collective-permute-start(bf16[3,2,2,16,128]{4,3,2,1,0:T(8,128)(2,1)S(1)} %get-tuple-element.40), channel_id=1, source_target_pairs={{0,1},{1,16},{16,17},{17,32},{32,33},{33,48},{48,49},{49,0},{2,3},... | collective-permute-start | bytes 147464 | tf_op jit(solution)/shard_map/ppermute | solution.py:285
  91.2 15.7 %collective-permute-start.20 = (bf16[3,2,2,16,128]{4,3,2,1,0:T(8,128)(2,1)S(1)}, bf16[3,2,2,16,128]{4,3,2,1,0:T(8,128)(2,1)S(1)}, u32[]{:S(2)}, u32[]{:S(2)}) collective-permute-start(bf16[3,2,2,16,128]{4,3,2,1,0:T(8,128)(2,1)S(1)} %get-tuple-element.41), channel_id=1, source_target_pairs={{0,16},{1,17},{16,32},{17,33},{32,48},{33,49},{48,0},{49,1},{2,18}... | collective-permute-start | bytes 147464 | tf_op jit(solution)/shard_map/ppermute | solution.py:285
  94.8 13.9 %collective-permute-start.21 = (bf16[3,2,2,16,128]{4,3,2,1,0:T(8,128)(2,1)}, bf16[3,2,2,16,128]{4,3,2,1,0:T(8,128)(2,1)S(1)}, u32[]{:S(2)}, u32[]{:S(2)}) collective-permute-start(bf16[3,2,2,16,128]{4,3,2,1,0:T(8,128)(2,1)} %get-tuple-element.42), channel_id=1, source_target_pairs={{0,17},{1,32},{16,33},{17,48},{32,49},{33,0},{48,1},{49,16},{2,19}... | collective-permute-start | bytes 147464 | tf_op jit(solution)/shard_map/ppermute | solution.py:285
  95.4 13.3 %collective-permute-start.22 = (bf16[3,2,2,16,128]{4,3,2,1,0:T(8,128)(2,1)S(1)}, bf16[3,2,2,16,128]{4,3,2,1,0:T(8,128)(2,1)S(1)}, u32[]{:S(2)}, u32[]{:S(2)}) collective-permute-start(bf16[3,2,2,16,128]{4,3,2,1,0:T(8,128)(2,1)S(1)} %get-tuple-element.43), channel_id=1, source_target_pairs={{0,32},{1,33},{16,48},{17,49},{32,0},{33,1},{48,16},{49,17},{2,34}... | collective-permute-start | bytes 147464 | tf_op jit(solution)/shard_map/ppermute | solution.py:285
  98.6 10.1 %collective-permute-start.23 = (bf16[3,2,2,16,128]{4,3,2,1,0:T(8,128)(2,1)S(1)}, bf16[3,2,2,16,128]{4,3,2,1,0:T(8,128)(2,1)S(1)}, u32[]{:S(2)}, u32[]{:S(2)}) collective-permute-start(bf16[3,2,2,16,128]{4,3,2,1,0:T(8,128)(2,1)S(1)} %get-tuple-element.44), channel_id=1, source_target_pairs={{0,33},{1,48},{16,49},{17,0},{32,1},{33,16},{48,17},{49,32},{2,35}... | collective-permute-start | bytes 147464 | tf_op jit(solution)/shard_map/ppermute | solution.py:285
  100.6 8.5 %collective-permute-start.24 = (bf16[3,2,2,16,128]{4,3,2,1,0:T(8,128)(2,1)S(1)}, bf16[3,2,2,16,128]{4,3,2,1,0:T(8,128)(2,1)S(1)}, u32[]{:S(2)}, u32[]{:S(2)}) collective-permute-start(bf16[3,2,2,16,128]{4,3,2,1,0:T(8,128)(2,1)S(1)} %get-tuple-element.45), channel_id=1, source_target_pairs={{0,48},{1,49},{16,0},{17,1},{32,16},{33,17},{48,32},{49,33},{2,50}... | collective-permute-start | bytes 147464 | tf_op jit(solution)/shard_map/ppermute | solution.py:285
  106.9 4.1 %collective-permute-start.25 = (bf16[3,2,2,16,128]{4,3,2,1,0:T(8,128)(2,1)S(1)}, bf16[3,2,2,16,128]{4,3,2,1,0:T(8,128)(2,1)S(1)}, u32[]{:S(2)}, u32[]{:S(2)}) collective-permute-start(bf16[3,2,2,16,128]{4,3,2,1,0:T(8,128)(2,1)S(1)} %get-tuple-element.46), channel_id=1, source_target_pairs={{0,49},{1,0},{16,1},{17,16},{32,17},{33,32},{48,33},{49,48},{2,51}... | collective-permute-start | bytes 147464 | tf_op jit(solution)/shard_map/ppermute | solution.py:285
  111.0 1.0 copy-start.4

commit v4 on v3

--- a/solution.py
+++ b/solution.py
@@ -24,7 +24,7 @@
 BIG = -float(2**30)
 SCALE = 1.0 / math.sqrt(HD)
 LOG2E = math.log2(math.e)
-DOT0, LSE0, LSE1, FR0, RW0 = 0, 16, 80, 32, 48
+DOT0, LSE0, FR0, RW0 = 0, 16, 32, 48
 VMEM = 20 * 1024 * 1024
 SPAN = 2
 BF, F32 = jnp.bfloat16, jnp.float32
@@ -101,20 +101,24 @@
     second = pltpu.roll(turned[:, 1].reshape(N, 128), 64, 1)
     both = turned[:, 0].reshape(N, 128) + second
     lane = lanes(N, 128)
-    keep = ((lane >= LSE0) & (lane < LSE0 + 9)) | ((lane >= LSE1) & (lane < LSE1 + 9))
     for k, out_ref in enumerate(out_refs):
         dest = lax.rem(ring_place() + k, Z)
         side = jnp.zeros((N, 128), F32)
         for h in range(HL):
             at = head_lanes(dest, h)
             g = do_ref[:, :, :, at]
-            out_ref[2 * h] = q_ref[:, :, :, at]
-            out_ref[2 * h + 1] = g
+            out_ref[8 * h : 8 * h + 4] = q_ref[:, :, :, at].reshape(4, CH, HD)
+            out_ref[8 * h + 4 : 8 * h + 8] = g.reshape(4, CH, HD)
             dot = jnp.sum((g.astype(F32) * o_ref[:, :, :, at].astype(F32)).reshape(N, HD), axis=-1, keepdims=True)
             for p, part in enumerate(three(dot)):
                 side = jnp.where(lane == DOT0 + 3 * h + p, part, side)
-        lse = pltpu.roll(both, lax.rem(128 + LSE0 - 16 * (dest // ZL), 128), 1)
-        out_ref[2 * HL] = jnp.where(keep, lse, side).astype(BF).reshape(F, R, CH, 128)
+        lse = pltpu.roll(both, lax.rem(128 + 9 - 16 * (dest // ZL), 128), 1)
+        side = jnp.where((lane >= 9) & (lane < 18), lse, side)
+        side = jnp.where((lane >= 18) & (lane < 27), pltpu.roll(lse, 128 - 55, 1), side).reshape(F * R, CH, 128)
+        packed = side[0]
+        for j in range(1, F * R):
+            packed = packed + pltpu.roll(side[j], 32 * j, 1)
+        out_ref[8 * HL] = packed.astype(BF)
 
 
 def pack_kv(*refs):
@@ -130,15 +134,20 @@
 def gather_q(*refs):
     in_refs, (out_ref, lo_ref, hi_ref) = refs[:Z], refs[Z:]
     for k, in_ref in zip((0,) + FAR, in_refs):
-        out_ref[lax.rem(ring_place() + Z - k, Z)] = in_ref[...]
+        src = lax.rem(ring_place() + Z - k, Z)
+        out_ref[src, : 2 * HL] = in_ref[: 8 * HL].reshape(2 * HL, F, R, CH, 128)
+        packed = in_ref[8 * HL].astype(F32)
+        for j in range(F * R):
+            tile = packed if j == 0 else pltpu.roll(packed, 128 - 32 * j, 1)
+            out_ref[src, 2 * HL, j // R, j % R] = tile.astype(BF)
     mine = lax.axis_index("zl")
     lane = lanes(N, 128)
     for zh in range(ZH):
         lse = out_ref[ZL * zh + mine, 2 * HL].astype(F32).reshape(N, 128)
-        for zl in range(ZL):
-            dot = out_ref[ZL * zh + zl, 2 * HL].astype(F32).reshape(N, 128)
-            here = lse if zl == 0 else pltpu.roll(lse, 64, 1)
-            side = jnp.where(lane < 16, dot, jnp.where(lane < 32, here, 0.0))
+        dots = [out_ref[ZL * zh + zl, 2 * HL].astype(F32).reshape(N, 128) for zl in range(ZL)]
+        for zl, dot in enumerate(dots):
+            here = pltpu.roll(lse, 7 if zl == 0 else 126, 1)
+            side = jnp.where(lane < 9, dot, jnp.where((lane >= 16) & (lane < 25), here, 0.0))
             out_ref[ZL * zh + zl, 2 * HL] = side.astype(BF).reshape(F, R, CH, 128)
     lo_ref[...] = out_ref[:ZL]
     hi_ref[...] = out_ref[Z - ZL :]
@@ -309,7 +318,7 @@
     wide = lambda block, n: shape(n, *block.shape)
     whole = shape(F, R, CH, HEADS * HD)
     room = lambda *shapes: [pltpu.VMEM(x.shape, x.dtype) for x in shapes] + [pltpu.SemaphoreType.DMA((len(shapes),))]
-    sent_q = call(pack_q, (q_block,) * Z, 4, "pack_q", scratch=room(whole, whole, whole, log_sums), where=pl.ANY, limit=60 * 1024 * 1024)(
+    sent_q = call(pack_q, (shape(8 * HL + 1, CH, HD),) * Z, 4, "pack_q", scratch=room(whole, whole, whole, log_sums), where=pl.ANY, limit=60 * 1024 * 1024)(
         queries, grad_out, outputs, log_sums
     )
     q_got = exchange_by_steps(sent_q, FAR)

time: 113 us -> 111 us (0.982)
  waiting for transfers between devices: 21.6 us -> 19.7 us
    ppermute x14, waiting for transfers between devices: 9.26 us -> 7.42 us  [exchange_by_steps(): lax.ppermute(sends[k], RING, [(i, (i + k) % Z) for i in range(Z)])]
  transfers between devices with their start and end apart: 28 -> 28, of which waited for: 10 -> 10; matrix products, arithmetic and copies ran while one was open for 0% -> 0% of each run, Pallas kernels for 13% -> 14%
where the time goes in v4:
time: 111 us
  starting transfers between devices  68.4 us (62%)
  Pallas kernels  20.4 us (18%)
  waiting for transfers between devices  19.7 us (18%)
  local copies, waits for them, and re-layouts  1.79 us (2%)
    ppermute x14, starting transfers between devices, exchange_by_steps(): lax.ppermute(sends[k], RING, [(i, (i + k) % Z) for i in range(Z)])  38.2 us
    pallas_call x10, Pallas kernels, call(): return lambda *args: made(*args, *after)  20.4 us
    ppermute x12, starting transfers between devices, shift(): lax.ppermute(block, ('x', 'row'), [(flat(x + dx, r + dr), flat(x, r)) for...  17 us
    all_to_all x2, starting transfers between devices, exchange(): return lax.all_to_all(sends, RING, split_axis=0, concat_axis=0, tiled=True)  13.1 us
    ppermute x12, waiting for transfers between devices, shift(): lax.ppermute(block, ('x', 'row'), [(flat(x + dx, r + dr), flat(x, r)) for...  12 us
    ppermute x14, waiting for transfers between devices, exchange_by_steps(): lax.ppermute(sends[k], RING, [(i, (i + k) % Z) for i in range(Z)])  7.42 us
  transfers between devices with their start and end apart: 28, of which 10 were waited for; matrix products, arithmetic and copies ran while one was open for 0% of the time, Pallas kernels for 14%

profile of v4, /device:TPU:32, one launch (start us, length us, event | category | flops | bytes accessed | tf_op | source)
XLA Modules:
  0.0 111.0 jit_solution(1312438673904813286)
XLA Ops:
  0.7 3.0 %pack_q.1 = (bf16[25,16,128]{2,1,0:T(8,128)(2,1)}, bf16[25,16,128]{2,1,0:T(8,128)(2,1)}, bf16[25,16,128]{2,1,0:T(8,128)(2,1)}, bf16[25,16,128]{2,1,0:T(8,128)(2,...) custom-call(bf16[2,2,16,3072]{3,2,1,0:T(8,128)(2,1)} %refs_0_.2, ...), custom_call_target="tpu_custom_call" | custom-call | bytes 1048576 | tf_op jit(solution)/shard_map/pack_q/pallas_call | solution.py:47
  3.6 6.4 %collective-permute-start = (bf16[25,16,128]{2,1,0:T(8,128)(2,1)}, bf16[25,16,128]{2,1,0:T(8,128)(2,1)S(1)}, u32[]{:S(2)}, u32[]{:S(2)}) collective-permute-start(bf16[25,16,128]{2,1,0:T(8,128)(2,1)} %get-tuple-element.26), channel_id=1, source_target_pairs={{0,32},{1,33},{16,48},{17,49},{32,0},{33,1},{48,16},{49,17},{2,34}... | collective-permute-start | bytes 307208 | tf_op jit(solution)/shard_map/ppermute | solution.py:294
  10.0 0.0 collective-permute-start.1
  10.0 5.0 %collective-permute-start.2 = (bf16[25,16,128]{2,1,0:T(8,128)(2,1)}, bf16[25,16,128]{2,1,0:T(8,128)(2,1)S(1)}, u32[]{:S(2)}, u32[]{:S(2)}) collective-permute-start(bf16[25,16,128]{2,1,0:T(8,128)(2,1)} %get-tuple-element.28), channel_id=1, source_target_pairs={{0,33},{1,48},{16,49},{17,0},{32,1},{33,16},{48,17},{49,32},{2,35}... | collective-permute-start | bytes 307208 | tf_op jit(solution)/shard_map/ppermute | solution.py:294
  15.0 0.3 collective-permute-start.3
  15.3 3.9 %collective-permute-start.4 = (bf16[25,16,128]{2,1,0:T(8,128)(2,1)}, bf16[25,16,128]{2,1,0:T(8,128)(2,1)S(1)}, u32[]{:S(2)}, u32[]{:S(2)}) collective-permute-start(bf16[25,16,128]{2,1,0:T(8,128)(2,1)} %get-tuple-element.30), channel_id=1, source_target_pairs={{0,48},{1,49},{16,0},{17,1},{32,16},{33,17},{48,32},{49,33},{2,50}... | collective-permute-start | bytes 307208 | tf_op jit(solution)/shard_map/ppermute | solution.py:294
  19.2 0.0 collective-permute-done.refs_2_.refs_1_
  19.2 0.4 collective-permute-start.5
  19.6 0.1 collective-permute-done.1.refs_3_.refs_2_
  19.7 5.2 %collective-permute-start.6 = (bf16[25,16,128]{2,1,0:T(8,128)(2,1)}, bf16[25,16,128]{2,1,0:T(8,128)(2,1)S(1)}, u32[]{:S(2)}, u32[]{:S(2)}) collective-permute-start(bf16[25,16,128]{2,1,0:T(8,128)(2,1)} %get-tuple-element.32), channel_id=1, source_target_pairs={{0,49},{1,0},{16,1},{17,16},{32,17},{33,32},{48,33},{49,48},{2,51}... | collective-permute-start | bytes 307208 | tf_op jit(solution)/shard_map/ppermute | solution.py:294
  24.9 0.0 collective-permute-done.2.refs_4_.refs_3_
  24.9 2.2 %collective-permute-done.3.refs_5_.refs_4_ = bf16[25,16,128]{2,1,0:T(8,128)(2,1)S(1)} collective-permute-done((bf16[25,16,128]{2,1,0:T(8,128)(2,1)}, bf16[25,16,128]{2,1,0:T(8,128)(2,1)S(1)}, u32[]{:S(2)}, u32[]{:S(2)}) %collective-permute-start.3) | collective-permute-done | bytes 102432 | tf_op jit(solution)/shard_map/ppermute | solution.py:294
  27.1 0.0 collective-permute-done.4.refs_6_.refs_5_
  27.1 1.4 %collective-permute-done.5.refs_7_.refs_6_ = bf16[25,16,128]{2,1,0:T(8,128)(2,1)S(1)} collective-permute-done((bf16[25,16,128]{2,1,0:T(8,128)(2,1)}, bf16[25,16,128]{2,1,0:T(8,128)(2,1)S(1)}, u32[]{:S(2)}, u32[]{:S(2)}) %collective-permute-start.5) | collective-permute-done | bytes 102432 | tf_op jit(solution)/shard_map/ppermute | solution.py:294
  28.5 0.5 collective-permute-done.6.refs_8_.refs_7_
  29.1 1.4 %pack_kv.1 = bf16[8,6,2,2,16,128]{5,4,3,2,1,0:T(8,128)(2,1)} custom-call(bf16[2,2,16,3072]{3,2,1,0:T(8,128)(2,1)S(1)} %copy-done.2, bf16[2,2,16,3072]{3,2,1,0:T(8,128)(2,1)S(1)} %copy-done.3, bf16[25,16,128]{2,1,0:T(8,128)(2,1)S(1)} %collective-permute-done.refs_2_.refs_1_, bf16[25,16,128]{2,1,0:T(8,128)(2,1)S(1)} %collective-permute-done.1.refs_3_.refs_2_, ...), custom_call_target="tpu_custom_call" | custom-call | bytes 1048576 | tf_op jit(solution)/shard_map/pack_kv/pallas_call | solution.py:47
  30.5 0.0 copy-start.5
  30.5 6.1 %all-to-all-start = ((bf16[8,6,2,2,16,128]{5,4,3,2,1,0:T(8,128)(2,1)}), bf16[8,6,2,2,16,128]{5,4,3,2,1,0:T(8,128)(2,1)S(1)}, u32[]{:S(2)}, u32[]{:S(2)}) async-start(bf16[8,6,2,2,16,128]{5,4,3,2,1,0:T(8,128)(2,1)} %pack_kv.1), calls=%async_computation | async-start | bytes 1572864 | tf_op jit(solution)/shard_map/all_to_all | solution.py:290
  36.7 0.5 gather_q.1
  37.2 1.6 %collective-permute-start.10 = (bf16[8,7,2,2,16,128]{5,4,3,2,1,0:T(8,128)(2,1)S(1)}, bf16[8,7,2,2,16,128]{5,4,3,2,1,0:T(8,128)(2,1)S(1)}, u32[]{:S(2)}, u32[]{:S(2)}) collective-permute-start(bf16[8,7,2,2,16,128]{5,4,3,2,1,0:T(8,128)(2,1)S(1)} %get-tuple-element.34.refs_1_.refs_6_), channel_id=1, source_target_pairs={{2,0},{4,2},{6,4},{8,6},{10,8},{12,10},{14,12},{0,14},{66,64},{68,... | collective-permute-start | bytes 2752520 | tf_op jit(solution)/shard_map/ppermute | solution.py:300
  38.8 0.0 collective-permute-start.9
  38.8 1.5 %collective-permute-start.11 = (bf16[2,7,2,2,16,128]{5,4,3,2,1,0:T(8,128)(2,1)S(1)}, bf16[2,7,2,2,16,128]{5,4,3,2,1,0:T(8,128)(2,1)S(1)}, u32[]{:S(2)}, u32[]{:S(2)}) collective-permute-start(bf16[2,7,2,2,16,128]{5,4,3,2,1,0:T(8,128)(2,1)S(1)} %get-tuple-element.35), channel_id=1, source_target_pairs={{192,0},{194,2},{196,4},{198,6},{200,8},{202,10},{204,12},{206,14}... | collective-permute-start | bytes 688136 | tf_op jit(solution)/shard_map/ppermute | solution.py:300
  40.3 1.7 %collective-permute-start.12 = (bf16[2,7,2,2,16,128]{5,4,3,2,1,0:T(8,128)(2,1)S(1)}, bf16[2,7,2,2,16,128]{5,4,3,2,1,0:T(8,128)(2,1)S(1)}, u32[]{:S(2)}, u32[]{:S(2)}) collective-permute-start(bf16[2,7,2,2,16,128]{5,4,3,2,1,0:T(8,128)(2,1)S(1)} %get-tuple-element.36), channel_id=1, source_target_pairs={{64,0},{66,2},{68,4},{70,6},{72,8},{74,10},{76,12},{78,14},{128,64... | collective-permute-start | bytes 688136 | tf_op jit(solution)/shard_map/ppermute | solution.py:300
  42.0 5.6 %collective-permute-done.11.refs_0_ = bf16[2,7,2,2,16,128]{5,4,3,2,1,0:T(8,128)(2,1)S(1)} collective-permute-done((bf16[2,7,2,2,16,128]{5,4,3,2,1,0:T(8,128)(2,1)S(1)}, bf16[2,7,2,2,16,128]{5,4,3,2,1,0:T(8,128)(2,1)S(1)}, u32[]{:S(2)}, u32[]{:S(2)}) %collective-permute-start.11) | collective-permute-done | bytes 229408 | tf_op jit(solution)/shard_map/ppermute | solution.py:300
  47.6 0.0 collective-permute-done.12.refs_1_
  47.6 0.0 collective-permute-start.13
  47.7 2.9 %collective-permute-start.14 = (bf16[4,7,2,2,16,128]{5,4,3,2,1,0:T(8,128)(2,1)S(1)}, bf16[4,7,2,2,16,128]{5,4,3,2,1,0:T(8,128)(2,1)S(1)}, u32[]{:S(2)}, u32[]{:S(2)}) collective-permute-start(bf16[4,7,2,2,16,128]{5,4,3,2,1,0:T(8,128)(2,1)S(1)} %join_q.1.refs_4_), channel_id=1, source_target_pairs={{2,0},{4,2},{6,4},{8,6},{10,8},{12,10},{14,12},{0,14},{66,64},{68,... | collective-permute-start | bytes 1376264 | tf_op jit(solution)/shard_map/ppermute | solution.py:300
  50.6 0.8 copy-done
  51.4 6.3 %collective-permute-done.13.refs_3_ = bf16[4,7,2,2,16,128]{5,4,3,2,1,0:T(8,128)(2,1)S(1)} collective-permute-done((bf16[4,7,2,2,16,128]{5,4,3,2,1,0:T(8,128)(2,1)S(1)}, bf16[4,7,2,2,16,128]{5,4,3,2,1,0:T(8,128)(2,1)S(1)}, u32[]{:S(2)}, u32[]{:S(2)}) %collective-permute-start.13) | collective-permute-done | bytes 458784 | tf_op jit(solution)/shard_map/ppermute | solution.py:300
  57.7 0.0 collective-permute-done.14.refs_4_.refs_5_
  57.7 0.0 collective-permute-done.10.refs_2_
  57.7 0.0 collective-permute-done.9.refs_1_.refs_0_
  57.7 0.3 all-to-all-done.refs_0_.refs_6_.refs_1_
  58.1 1.6 %collective-permute-start.15 = (bf16[2,6,2,2,16,128]{5,4,3,2,1,0:T(8,128)(2,1)S(1)}, bf16[2,6,2,2,16,128]{5,4,3,2,1,0:T(8,128)(2,1)S(1)}, u32[]{:S(2)}, u32[]{:S(2)}) collective-permute-start(bf16[2,6,2,2,16,128]{5,4,3,2,1,0:T(8,128)(2,1)S(1)} %get-tuple-element.37), channel_id=1, source_target_pairs={{192,0},{194,2},{196,4},{198,6},{200,8},{202,10},{204,12},{206,14}... | collective-permute-start | bytes 589832 | tf_op jit(solution)/shard_map/ppermute | solution.py:300
  59.6 1.7 %collective-permute-start.16 = (bf16[2,6,2,2,16,128]{5,4,3,2,1,0:T(8,128)(2,1)S(1)}, bf16[2,6,2,2,16,128]{5,4,3,2,1,0:T(8,128)(2,1)S(1)}, u32[]{:S(2)}, u32[]{:S(2)}) collective-permute-start(bf16[2,6,2,2,16,128]{5,4,3,2,1,0:T(8,128)(2,1)S(1)} %get-tuple-element.38), channel_id=1, source_target_pairs={{64,0},{66,2},{68,4},{70,6},{72,8},{74,10},{76,12},{78,14},{128,64... | collective-permute-start | bytes 589832 | tf_op jit(solution)/shard_map/ppermute | solution.py:300
  61.4 0.0 collective-permute-start.7
  61.4 3.0 %collective-permute-start.8 = (bf16[8,6,2,2,16,128]{5,4,3,2,1,0:T(8,128)(2,1)S(1)}, bf16[8,6,2,2,16,128]{5,4,3,2,1,0:T(8,128)(2,1)}, u32[]{:S(2)}, u32[]{:S(2)}) collective-permute-start(bf16[8,6,2,2,16,128]{5,4,3,2,1,0:T(8,128)(2,1)S(1)} %all-to-all-done.refs_0_.refs_6_.refs_1_), channel_id=1, source_target_pairs={{2,0},{4,2},{6,4},{8,6},{10,8},{12,10},{14,12},{0,14},{66,64},{68,... | collective-permute-start | bytes 2359304 | tf_op jit(solution)/shard_map/ppermute | solution.py:300
  64.4 6.6 %key_grads.1.refs_2_ = bf16[8,6,2,2,16,128]{5,4,3,2,1,0:T(8,128)(2,1)} custom-call(bf16[8,7,2,2,16,128]{5,4,3,2,1,0:T(8,128)(2,1)S(1)} %collective-permute-done.9.refs_1_.refs_0_, bf16[8,7,2,2,16,128]{5,4,3,2,1,0:T(8,128)(2,1)S(1)} %copy-done.7, bf16[8,7,2,2,16,128]{5,4,3,2,1,0:T(8,128)(2,1)S(1)} %collective-permute-done.10.refs_2_, ...), custom_call_target="tpu_custom_call" | custom-call | flops 10000000000 | bytes 1048576 | tf_op jit(solution)/shard_map/key_grads/pallas_call | solution.py:47
  70.9 0.0 collective-permute-done.15.refs_0_
  70.9 0.0 collective-permute-done.16.refs_1_
  71.0 0.0 collective-permute-start.17
  71.0 2.9 %collective-permute-start.18 = (bf16[4,6,2,2,16,128]{5,4,3,2,1,0:T(8,128)(2,1)S(1)}, bf16[4,6,2,2,16,128]{5,4,3,2,1,0:T(8,128)(2,1)}, u32[]{:S(2)}, u32[]{:S(2)}) collective-permute-start(bf16[4,6,2,2,16,128]{5,4,3,2,1,0:T(8,128)(2,1)S(1)} %join_kv.1.refs_4_), channel_id=1, source_target_pairs={{2,0},{4,2},{6,4},{8,6},{10,8},{12,10},{14,12},{0,14},{66,64},{68,... | collective-permute-start | bytes 1179656 | tf_op jit(solution)/shard_map/ppermute | solution.py:300
  73.9 6.9 %all-to-all-start.1 = ((bf16[8,6,2,2,16,128]{5,4,3,2,1,0:T(8,128)(2,1)}), bf16[8,6,2,2,16,128]{5,4,3,2,1,0:T(8,128)(2,1)S(1)}, u32[]{:S(2)}, u32[]{:S(2)}) async-start(bf16[8,6,2,2,16,128]{5,4,3,2,1,0:T(8,128)(2,1)} %key_grads.1.refs_2_), calls=%async_computation.1 | async-start | bytes 1572864 | tf_op jit(solution)/shard_map/all_to_all | solution.py:290
  80.9 0.0 collective-permute-done.17.refs_3_
  80.9 0.0 collective-permute-done.7.refs_0_
  80.9 0.0 collective-permute-done.8.refs_2_
  80.9 7.0 %query_grads.1 = (bf16[3,2,2,16,128]{4,3,2,1,0:T(8,128)(2,1)S(1)}, bf16[3,2,2,16,128]{4,3,2,1,0:T(8,128)(2,1)S(1)}, bf16[3,2,2,16,128]{4,3,2,1,0:T(8,128)(2,1)S(...) custom-call(bf16[8,6,2,2,16,128]{5,4,3,2,1,0:T(8,128)(2,1)} %collect, ...), custom_call_target="tpu_custom_call" | custom-call | flops 99999997952 | bytes 1048576 | tf_op jit(solution)/shard_map/query_grads/pallas_call | solution.py:47
  87.9 1.4 %collective-permute-start.19 = (bf16[3,2,2,16,128]{4,3,2,1,0:T(8,128)(2,1)S(1)}, bf16[3,2,2,16,128]{4,3,2,1,0:T(8,128)(2,1)S(1)}, u32[]{:S(2)}, u32[]{:S(2)}) collective-permute-start(bf16[3,2,2,16,128]{4,3,2,1,0:T(8,128)(2,1)S(1)} %get-tuple-element.40), channel_id=1, source_target_pairs={{0,1},{1,16},{16,17},{17,32},{32,33},{33,48},{48,49},{49,0},{2,3},... | collective-permute-start | bytes 147464 | tf_op jit(solution)/shard_map/ppermute | solution.py:294
  89.3 3.6 %collective-permute-start.20 = (bf16[3,2,2,16,128]{4,3,2,1,0:T(8,128)(2,1)S(1)}, bf16[3,2,2,16,128]{4,3,2,1,0:T(8,128)(2,1)S(1)}, u32[]{:S(2)}, u32[]{:S(2)}) collective-permute-start(bf16[3,2,2,16,128]{4,3,2,1,0:T(8,128)(2,1)S(1)} %get-tuple-element.41), channel_id=1, source_target_pairs={{0,16},{1,17},{16,32},{17,33},{32,48},{33,49},{48,0},{49,1},{2,18}... | collective-permute-start | bytes 147464 | tf_op jit(solution)/shard_map/ppermute | solution.py:294
  92.9 0.6 collective-permute-start.21
  93.5 3.2 %collective-permute-start.22 = (bf16[3,2,2,16,128]{4,3,2,1,0:T(8,128)(2,1)S(1)}, bf16[3,2,2,16,128]{4,3,2,1,0:T(8,128)(2,1)S(1)}, u32[]{:S(2)}, u32[]{:S(2)}) collective-permute-start(bf16[3,2,2,16,128]{4,3,2,1,0:T(8,128)(2,1)S(1)} %get-tuple-element.43), channel_id=1, source_target_pairs={{0,32},{1,33},{16,48},{17,49},{32,0},{33,1},{48,16},{49,17},{2,34}... | collective-permute-start | bytes 147464 | tf_op jit(solution)/shard_map/ppermute | solution.py:294
  96.7 1.2 %collective-permute-start.23 = (bf16[3,2,2,16,128]{4,3,2,1,0:T(8,128)(2,1)S(1)}, bf16[3,2,2,16,128]{4,3,2,1,0:T(8,128)(2,1)S(1)}, u32[]{:S(2)}, u32[]{:S(2)}) collective-permute-start(bf16[3,2,2,16,128]{4,3,2,1,0:T(8,128)(2,1)S(1)} %get-tuple-element.44), channel_id=1, source_target_pairs={{0,33},{1,48},{16,49},{17,0},{32,1},{33,16},{48,17},{49,32},{2,35}... | collective-permute-start | bytes 147464 | tf_op jit(solution)/shard_map/ppermute | solution.py:294
  97.9 0.8 collective-permute-done.19.refs_1_
  98.7 6.3 %collective-permute-start.24 = (bf16[3,2,2,16,128]{4,3,2,1,0:T(8,128)(2,1)S(1)}, bf16[3,2,2,16,128]{4,3,2,1,0:T(8,128)(2,1)S(1)}, u32[]{:S(2)}, u32[]{:S(2)}) collective-permute-start(bf16[3,2,2,16,128]{4,3,2,1,0:T(8,128)(2,1)S(1)} %get-tuple-element.45), channel_id=1, source_target_pairs={{0,48},{1,49},{16,0},{17,1},{32,16},{33,17},{48,32},{49,33},{2,50}... | collective-permute-start | bytes 147464 | tf_op jit(solution)/shard_map/ppermute | solution.py:294
  105.1 0.7 collective-permute-start.25
  105.8 0.0 all-to-all-done.1.refs_0_
  105.8 1.0 unpack_kv.1
  106.8 0.0 collective-permute-done.21.refs_3_
  106.8 0.0 collective-permute-done.22.refs_4_
  106.8 0.0 collective-permute-done.23.refs_5_
  106.8 1.0 collective-permute-done.24.refs_6_
  107.8 1.4 %collective-permute-done.25.refs_7_ = bf16[3,2,2,16,128]{4,3,2,1,0:T(8,128)(2,1)S(1)} collective-permute-done((bf16[3,2,2,16,128]{4,3,2,1,0:T(8,128)(2,1)S(1)}, bf16[3,2,2,16,128]{4,3,2,1,0:T(8,128)(2,1)S(1)}, u32[]{:S(2)}, u32[]{:S(2)}) %collective-permute-start.25) | collective-permute-done | bytes 49184 | tf_op jit(solution)/shard_map/ppermute | solution.py:294
  109.2 1.0 copy-done.4
  110.2 0.8 unpack_q.1
  (20 shorter events, 0.1 us)
Async XLA Ops:
  0.6 28.4 %copy-start.2 = (bf16[2,2,16,3072]{3,2,1,0:T(8,128)(2,1)S(1)}, bf16[2,2,16,3072]{3,2,1,0:T(8,128)(2,1)}, u32[]{:S(2)}) copy-start(bf16[2,2,16,3072]{3,2,1,0:T(8,128)(2,1)} %refs_0_.3) | copy-start | bytes 1179652
  0.6 28.4 %copy-start.3 = (bf16[2,2,16,3072]{3,2,1,0:T(8,128)(2,1)S(1)}, bf16[2,2,16,3072]{3,2,1,0:T(8,128)(2,1)}, u32[]{:S(2)}) copy-start(bf16[2,2,16,3072]{3,2,1,0:T(8,128)(2,1)} %refs_1_.3) | copy-start | bytes 1179652
  3.6 15.5 %collective-permute-start = (bf16[25,16,128]{2,1,0:T(8,128)(2,1)}, bf16[25,16,128]{2,1,0:T(8,128)(2,1)S(1)}, u32[]{:S(2)}, u32[]{:S(2)}) collective-permute-start(bf16[25,16,128]{2,1,0:T(8,128)(2,1)} %get-tuple-element.26), channel_id=1, source_target_pairs={{0,32},{1,33},{16,48},{17,49},{32,0},{33,1},{48,16},{49,17},{2,34}... | collective-permute-start | bytes 307208 | tf_op jit(solution)/shard_map/ppermute | solution.py:294
  10.0 9.7 %collective-permute-start.1 = (bf16[25,16,128]{2,1,0:T(8,128)(2,1)}, bf16[25,16,128]{2,1,0:T(8,128)(2,1)S(1)}, u32[]{:S(2)}, u32[]{:S(2)}) collective-permute-start(bf16[25,16,128]{2,1,0:T(8,128)(2,1)} %get-tuple-element.27), channel_id=1, source_target_pairs={{0,17},{1,32},{16,33},{17,48},{32,49},{33,0},{48,1},{49,16},{2,19}... | collective-permute-start | bytes 307208 | tf_op jit(solution)/shard_map/ppermute | solution.py:294
  10.0 14.9 %collective-permute-start.2 = (bf16[25,16,128]{2,1,0:T(8,128)(2,1)}, bf16[25,16,128]{2,1,0:T(8,128)(2,1)S(1)}, u32[]{:S(2)}, u32[]{:S(2)}) collective-permute-start(bf16[25,16,128]{2,1,0:T(8,128)(2,1)} %get-tuple-element.28), channel_id=1, source_target_pairs={{0,33},{1,48},{16,49},{17,0},{32,1},{33,16},{48,17},{49,32},{2,35}... | collective-permute-start | bytes 307208 | tf_op jit(solution)/shard_map/ppermute | solution.py:294
  15.0 12.1 %collective-permute-start.3 = (bf16[25,16,128]{2,1,0:T(8,128)(2,1)}, bf16[25,16,128]{2,1,0:T(8,128)(2,1)S(1)}, u32[]{:S(2)}, u32[]{:S(2)}) collective-permute-start(bf16[25,16,128]{2,1,0:T(8,128)(2,1)} %get-tuple-element.29), channel_id=1, source_target_pairs={{0,16},{1,17},{16,32},{17,33},{32,48},{33,49},{48,0},{49,1},{2,18}... | collective-permute-start | bytes 307208 | tf_op jit(solution)/shard_map/ppermute | solution.py:294
  15.3 11.8 %collective-permute-start.4 = (bf16[25,16,128]{2,1,0:T(8,128)(2,1)}, bf16[25,16,128]{2,1,0:T(8,128)(2,1)S(1)}, u32[]{:S(2)}, u32[]{:S(2)}) collective-permute-start(bf16[25,16,128]{2,1,0:T(8,128)(2,1)} %get-tuple-element.30), channel_id=1, source_target_pairs={{0,48},{1,49},{16,0},{17,1},{32,16},{33,17},{48,32},{49,33},{2,50}... | collective-permute-start | bytes 307208 | tf_op jit(solution)/shard_map/ppermute | solution.py:294
  19.2 9.3 %collective-permute-start.5 = (bf16[25,16,128]{2,1,0:T(8,128)(2,1)}, bf16[25,16,128]{2,1,0:T(8,128)(2,1)S(1)}, u32[]{:S(2)}, u32[]{:S(2)}) collective-permute-start(bf16[25,16,128]{2,1,0:T(8,128)(2,1)} %get-tuple-element.31), channel_id=1, source_target_pairs={{0,1},{1,16},{16,17},{17,32},{32,33},{33,48},{48,49},{49,0},{2,3},... | collective-permute-start | bytes 307208 | tf_op jit(solution)/shard_map/ppermute | solution.py:294
  19.7 9.3 %collective-permute-start.6 = (bf16[25,16,128]{2,1,0:T(8,128)(2,1)}, bf16[25,16,128]{2,1,0:T(8,128)(2,1)S(1)}, u32[]{:S(2)}, u32[]{:S(2)}) collective-permute-start(bf16[25,16,128]{2,1,0:T(8,128)(2,1)} %get-tuple-element.32), channel_id=1, source_target_pairs={{0,49},{1,0},{16,1},{17,16},{32,17},{33,32},{48,33},{49,48},{2,51}... | collective-permute-start | bytes 307208 | tf_op jit(solution)/shard_map/ppermute | solution.py:294
  30.5 6.2 %copy-start.5 = (bf16[25,16,128]{2,1,0:T(8,128)(2,1)S(1)}, bf16[25,16,128]{2,1,0:T(8,128)(2,1)}, u32[]{:S(2)}) copy-start(bf16[25,16,128]{2,1,0:T(8,128)(2,1)} %get-tuple-element.33.refs_0_) | copy-start | bytes 307204
  30.5 27.5 %all-to-all-start = ((bf16[8,6,2,2,16,128]{5,4,3,2,1,0:T(8,128)(2,1)}), bf16[8,6,2,2,16,128]{5,4,3,2,1,0:T(8,128)(2,1)S(1)}, u32[]{:S(2)}, u32[]{:S(2)}) async-start(bf16[8,6,2,2,16,128]{5,4,3,2,1,0:T(8,128)(2,1)} %pack_kv.1), calls=%async_computation | async-start | bytes 1572864 | tf_op jit(solution)/shard_map/all_to_all | solution.py:290
  37.1 20.6 %copy-start.6 = (bf16[8,7,2,2,16,128]{5,4,3,2,1,0:T(8,128)(2,1)}, bf16[8,7,2,2,16,128]{5,4,3,2,1,0:T(8,128)(2,1)S(1)}, u32[]{:S(2)}) copy-start(bf16[8,7,2,2,16,128]{5,4,3,2,1,0:T(8,128)(2,1)S(1)} %get-tuple-element.34.refs_1_.refs_6_) | copy-start | bytes 2752516
  37.2 20.6 %collective-permute-start.10 = (bf16[8,7,2,2,16,128]{5,4,3,2,1,0:T(8,128)(2,1)S(1)}, bf16[8,7,2,2,16,128]{5,4,3,2,1,0:T(8,128)(2,1)S(1)}, u32[]{:S(2)}, u32[]{:S(2)}) collective-permute-start(bf16[8,7,2,2,16,128]{5,4,3,2,1,0:T(8,128)(2,1)S(1)} %get-tuple-element.34.refs_1_.refs_6_), channel_id=1, source_target_pairs={{2,0},{4,2},{6,4},{8,6},{10,8},{12,10},{14,12},{0,14},{66,64},{68,... | collective-permute-start | bytes 2752520 | tf_op jit(solution)/shard_map/ppermute | solution.py:300
  38.8 19.0 %collective-permute-start.9 = (bf16[8,7,2,2,16,128]{5,4,3,2,1,0:T(8,128)(2,1)S(1)}, bf16[8,7,2,2,16,128]{5,4,3,2,1,0:T(8,128)(2,1)S(1)}, u32[]{:S(2)}, u32[]{:S(2)}) collective-permute-start(bf16[8,7,2,2,16,128]{5,4,3,2,1,0:T(8,128)(2,1)S(1)} %get-tuple-element.34.refs_1_.refs_6_), channel_id=1, source_target_pairs={{14,0},{0,2},{2,4},{4,6},{6,8},{8,10},{10,12},{12,14},{78,64},{64,... | collective-permute-start | bytes 2752520 | tf_op jit(solution)/shard_map/ppermute | solution.py:300
  38.8 8.8 %collective-permute-start.11 = (bf16[2,7,2,2,16,128]{5,4,3,2,1,0:T(8,128)(2,1)S(1)}, bf16[2,7,2,2,16,128]{5,4,3,2,1,0:T(8,128)(2,1)S(1)}, u32[]{:S(2)}, u32[]{:S(2)}) collective-permute-start(bf16[2,7,2,2,16,128]{5,4,3,2,1,0:T(8,128)(2,1)S(1)} %get-tuple-element.35), channel_id=1, source_target_pairs={{192,0},{194,2},{196,4},{198,6},{200,8},{202,10},{204,12},{206,14}... | collective-permute-start | bytes 688136 | tf_op jit(solution)/shard_map/ppermute | solution.py:300
  40.3 7.3 %collective-permute-start.12 = (bf16[2,7,2,2,16,128]{5,4,3,2,1,0:T(8,128)(2,1)S(1)}, bf16[2,7,2,2,16,128]{5,4,3,2,1,0:T(8,128)(2,1)S(1)}, u32[]{:S(2)}, u32[]{:S(2)}) collective-permute-start(bf16[2,7,2,2,16,128]{5,4,3,2,1,0:T(8,128)(2,1)S(1)} %get-tuple-element.36), channel_id=1, source_target_pairs={{64,0},{66,2},{68,4},{70,6},{72,8},{74,10},{76,12},{78,14},{128,64... | collective-permute-start | bytes 688136 | tf_op jit(solution)/shard_map/ppermute | solution.py:300
  47.6 10.1 %collective-permute-start.13 = (bf16[4,7,2,2,16,128]{5,4,3,2,1,0:T(8,128)(2,1)S(1)}, bf16[4,7,2,2,16,128]{5,4,3,2,1,0:T(8,128)(2,1)S(1)}, u32[]{:S(2)}, u32[]{:S(2)}) collective-permute-start(bf16[4,7,2,2,16,128]{5,4,3,2,1,0:T(8,128)(2,1)S(1)} %join_q.1.refs_4_), channel_id=1, source_target_pairs={{14,0},{0,2},{2,4},{4,6},{6,8},{8,10},{10,12},{12,14},{78,64},{64,... | collective-permute-start | bytes 1376264 | tf_op jit(solution)/shard_map/ppermute | solution.py:300
  47.7 10.1 %collective-permute-start.14 = (bf16[4,7,2,2,16,128]{5,4,3,2,1,0:T(8,128)(2,1)S(1)}, bf16[4,7,2,2,16,128]{5,4,3,2,1,0:T(8,128)(2,1)S(1)}, u32[]{:S(2)}, u32[]{:S(2)}) collective-permute-start(bf16[4,7,2,2,16,128]{5,4,3,2,1,0:T(8,128)(2,1)S(1)} %join_q.1.refs_4_), channel_id=1, source_target_pairs={{2,0},{4,2},{6,4},{8,6},{10,8},{12,10},{14,12},{0,14},{66,64},{68,... | collective-permute-start | bytes 1376264 | tf_op jit(solution)/shard_map/ppermute | solution.py:300
  50.6 0.8 copy-start
  58.0 6.3 %copy-start.1 = (bf16[4,7,2,2,16,128]{5,4,3,2,1,0:T(8,128)(2,1)S(1)}, bf16[4,7,2,2,16,128]{5,4,3,2,1,0:T(8,128)(2,1)}, u32[]{:S(2)}) copy-start(bf16[4,7,2,2,16,128]{5,4,3,2,1,0:T(8,128)(2,1)} %copy-done) | copy-start | bytes 1376260
  58.0 6.3 %copy-start.7 = (bf16[8,7,2,2,16,128]{5,4,3,2,1,0:T(8,128)(2,1)S(1)}, bf16[8,7,2,2,16,128]{5,4,3,2,1,0:T(8,128)(2,1)}, u32[]{:S(2)}) copy-start(bf16[8,7,2,2,16,128]{5,4,3,2,1,0:T(8,128)(2,1)} %copy-done.6) | copy-start | bytes 2752516
  58.1 12.8 %collective-permute-start.15 = (bf16[2,6,2,2,16,128]{5,4,3,2,1,0:T(8,128)(2,1)S(1)}, bf16[2,6,2,2,16,128]{5,4,3,2,1,0:T(8,128)(2,1)S(1)}, u32[]{:S(2)}, u32[]{:S(2)}) collective-permute-start(bf16[2,6,2,2,16,128]{5,4,3,2,1,0:T(8,128)(2,1)S(1)} %get-tuple-element.37), channel_id=1, source_target_pairs={{192,0},{194,2},{196,4},{198,6},{200,8},{202,10},{204,12},{206,14}... | collective-permute-start | bytes 589832 | tf_op jit(solution)/shard_map/ppermute | solution.py:300
  59.6 11.3 %collective-permute-start.16 = (bf16[2,6,2,2,16,128]{5,4,3,2,1,0:T(8,128)(2,1)S(1)}, bf16[2,6,2,2,16,128]{5,4,3,2,1,0:T(8,128)(2,1)S(1)}, u32[]{:S(2)}, u32[]{:S(2)}) collective-permute-start(bf16[2,6,2,2,16,128]{5,4,3,2,1,0:T(8,128)(2,1)S(1)} %get-tuple-element.38), channel_id=1, source_target_pairs={{64,0},{66,2},{68,4},{70,6},{72,8},{74,10},{76,12},{78,14},{128,64... | collective-permute-start | bytes 589832 | tf_op jit(solution)/shard_map/ppermute | solution.py:300
  61.4 19.5 %collective-permute-start.7 = (bf16[8,6,2,2,16,128]{5,4,3,2,1,0:T(8,128)(2,1)S(1)}, bf16[8,6,2,2,16,128]{5,4,3,2,1,0:T(8,128)(2,1)}, u32[]{:S(2)}, u32[]{:S(2)}) collective-permute-start(bf16[8,6,2,2,16,128]{5,4,3,2,1,0:T(8,128)(2,1)S(1)} %all-to-all-done.refs_0_.refs_6_.refs_1_), channel_id=1, source_target_pairs={{14,0},{0,2},{2,4},{4,6},{6,8},{8,10},{10,12},{12,14},{78,64},{64,... | collective-permute-start | bytes 2359304 | tf_op jit(solution)/shard_map/ppermute | solution.py:300
  61.4 19.5 %collective-permute-start.8 = (bf16[8,6,2,2,16,128]{5,4,3,2,1,0:T(8,128)(2,1)S(1)}, bf16[8,6,2,2,16,128]{5,4,3,2,1,0:T(8,128)(2,1)}, u32[]{:S(2)}, u32[]{:S(2)}) collective-permute-start(bf16[8,6,2,2,16,128]{5,4,3,2,1,0:T(8,128)(2,1)S(1)} %all-to-all-done.refs_0_.refs_6_.refs_1_), channel_id=1, source_target_pairs={{2,0},{4,2},{6,4},{8,6},{10,8},{12,10},{14,12},{0,14},{66,64},{68,... | collective-permute-start | bytes 2359304 | tf_op jit(solution)/shard_map/ppermute | solution.py:300
  71.0 9.9 %copy-start.8 = (bf16[8,7,2,2,16,128]{5,4,3,2,1,0:T(8,128)(2,1)S(1)}, bf16[8,7,2,2,16,128]{5,4,3,2,1,0:T(8,128)(2,1)}, u32[]{:S(2)}) copy-start(bf16[8,7,2,2,16,128]{5,4,3,2,1,0:T(8,128)(2,1)} %copy-done.6) | copy-start | bytes 2752516
  71.0 9.9 %collective-permute-start.17 = (bf16[4,6,2,2,16,128]{5,4,3,2,1,0:T(8,128)(2,1)S(1)}, bf16[4,6,2,2,16,128]{5,4,3,2,1,0:T(8,128)(2,1)S(1)}, u32[]{:S(2)}, u32[]{:S(2)}) collective-permute-start(bf16[4,6,2,2,16,128]{5,4,3,2,1,0:T(8,128)(2,1)S(1)} %join_kv.1.refs_4_), channel_id=1, source_target_pairs={{14,0},{0,2},{2,4},{4,6},{6,8},{8,10},{10,12},{12,14},{78,64},{64,... | collective-permute-start | bytes 1179656 | tf_op jit(solution)/shard_map/ppermute | solution.py:300
  71.0 9.9 %collective-permute-start.18 = (bf16[4,6,2,2,16,128]{5,4,3,2,1,0:T(8,128)(2,1)S(1)}, bf16[4,6,2,2,16,128]{5,4,3,2,1,0:T(8,128)(2,1)}, u32[]{:S(2)}, u32[]{:S(2)}) collective-permute-start(bf16[4,6,2,2,16,128]{5,4,3,2,1,0:T(8,128)(2,1)S(1)} %join_kv.1.refs_4_), channel_id=1, source_target_pairs={{2,0},{4,2},{6,4},{8,6},{10,8},{12,10},{14,12},{0,14},{66,64},{68,... | collective-permute-start | bytes 1179656 | tf_op jit(solution)/shard_map/ppermute | solution.py:300
  73.9 31.8 %all-to-all-start.1 = ((bf16[8,6,2,2,16,128]{5,4,3,2,1,0:T(8,128)(2,1)}), bf16[8,6,2,2,16,128]{5,4,3,2,1,0:T(8,128)(2,1)S(1)}, u32[]{:S(2)}, u32[]{:S(2)}) async-start(bf16[8,6,2,2,16,128]{5,4,3,2,1,0:T(8,128)(2,1)} %key_grads.1.refs_2_), calls=%async_computation.1 | async-start | bytes 1572864 | tf_op jit(solution)/shard_map/all_to_all | solution.py:290
  87.9 10.8 %collective-permute-start.19 = (bf16[3,2,2,16,128]{4,3,2,1,0:T(8,128)(2,1)S(1)}, bf16[3,2,2,16,128]{4,3,2,1,0:T(8,128)(2,1)S(1)}, u32[]{:S(2)}, u32[]{:S(2)}) collective-permute-start(bf16[3,2,2,16,128]{4,3,2,1,0:T(8,128)(2,1)S(1)} %get-tuple-element.40), channel_id=1, source_target_pairs={{0,1},{1,16},{16,17},{17,32},{32,33},{33,48},{48,49},{49,0},{2,3},... | collective-permute-start | bytes 147464 | tf_op jit(solution)/shard_map/ppermute | solution.py:294
  89.3 15.7 %collective-permute-start.20 = (bf16[3,2,2,16,128]{4,3,2,1,0:T(8,128)(2,1)S(1)}, bf16[3,2,2,16,128]{4,3,2,1,0:T(8,128)(2,1)S(1)}, u32[]{:S(2)}, u32[]{:S(2)}) collective-permute-start(bf16[3,2,2,16,128]{4,3,2,1,0:T(8,128)(2,1)S(1)} %get-tuple-element.41), channel_id=1, source_target_pairs={{0,16},{1,17},{16,32},{17,33},{32,48},{33,49},{48,0},{49,1},{2,18}... | collective-permute-start | bytes 147464 | tf_op jit(solution)/shard_map/ppermute | solution.py:294
  92.9 13.9 %collective-permute-start.21 = (bf16[3,2,2,16,128]{4,3,2,1,0:T(8,128)(2,1)}, bf16[3,2,2,16,128]{4,3,2,1,0:T(8,128)(2,1)S(1)}, u32[]{:S(2)}, u32[]{:S(2)}) collective-permute-start(bf16[3,2,2,16,128]{4,3,2,1,0:T(8,128)(2,1)} %get-tuple-element.42), channel_id=1, source_target_pairs={{0,17},{1,32},{16,33},{17,48},{32,49},{33,0},{48,1},{49,16},{2,19}... | collective-permute-start | bytes 147464 | tf_op jit(solution)/shard_map/ppermute | solution.py:294
  93.5 13.3 %collective-permute-start.22 = (bf16[3,2,2,16,128]{4,3,2,1,0:T(8,128)(2,1)S(1)}, bf16[3,2,2,16,128]{4,3,2,1,0:T(8,128)(2,1)S(1)}, u32[]{:S(2)}, u32[]{:S(2)}) collective-permute-start(bf16[3,2,2,16,128]{4,3,2,1,0:T(8,128)(2,1)S(1)} %get-tuple-element.43), channel_id=1, source_target_pairs={{0,32},{1,33},{16,48},{17,49},{32,0},{33,1},{48,16},{49,17},{2,34}... | collective-permute-start | bytes 147464 | tf_op jit(solution)/shard_map/ppermute | solution.py:294
  96.7 10.1 %collective-permute-start.23 = (bf16[3,2,2,16,128]{4,3,2,1,0:T(8,128)(2,1)S(1)}, bf16[3,2,2,16,128]{4,3,2,1,0:T(8,128)(2,1)S(1)}, u32[]{:S(2)}, u32[]{:S(2)}) collective-permute-start(bf16[3,2,2,16,128]{4,3,2,1,0:T(8,128)(2,1)S(1)} %get-tuple-element.44), channel_id=1, source_target_pairs={{0,33},{1,48},{16,49},{17,0},{32,1},{33,16},{48,17},{49,32},{2,35}... | collective-permute-start | bytes 147464 | tf_op jit(solution)/shard_map/ppermute | solution.py:294
  98.7 9.1 %collective-permute-start.24 = (bf16[3,2,2,16,128]{4,3,2,1,0:T(8,128)(2,1)S(1)}, bf16[3,2,2,16,128]{4,3,2,1,0:T(8,128)(2,1)S(1)}, u32[]{:S(2)}, u32[]{:S(2)}) collective-permute-start(bf16[3,2,2,16,128]{4,3,2,1,0:T(8,128)(2,1)S(1)} %get-tuple-element.45), channel_id=1, source_target_pairs={{0,48},{1,49},{16,0},{17,1},{32,16},{33,17},{48,32},{49,33},{2,50}... | collective-permute-start | bytes 147464 | tf_op jit(solution)/shard_map/ppermute | solution.py:294
  105.1 4.1 %collective-permute-start.25 = (bf16[3,2,2,16,128]{4,3,2,1,0:T(8,128)(2,1)S(1)}, bf16[3,2,2,16,128]{4,3,2,1,0:T(8,128)(2,1)S(1)}, u32[]{:S(2)}, u32[]{:S(2)}) collective-permute-start(bf16[3,2,2,16,128]{4,3,2,1,0:T(8,128)(2,1)S(1)} %get-tuple-element.46), channel_id=1, source_target_pairs={{0,49},{1,0},{16,1},{17,16},{32,17},{33,32},{48,33},{49,48},{2,51}... | collective-permute-start | bytes 147464 | tf_op jit(solution)/shard_map/ppermute | solution.py:294
  109.2 1.0 copy-start.4
